TPU v7x, 512 devices: a whole 4x4x16 slice. The times are simulated.
512 devices in a mesh: lat: 8 (over y_hi, x), lon: 64 (over z, y_lo, core).
Axes of the slice: x: 4, y: 4 (y_hi: 2, y_lo: 2; y = y_hi * 2 + y_lo), z: 16, core: 2. Of those that a mesh axis runs over, the one named last changes fastest.
Arguments:
- patches: bfloat16 [96, 2304, 512], P('lat', 'lon'), may hold values from -6 to 6
- query_key_value_weight: bfloat16 [512, 1536], P('lon'), may hold values from -0.25 to 0.25
- attention_output_weight: bfloat16 [512, 512], P('lon'), may hold values from -0.25 to 0.25
- feedforward_in_weight: bfloat16 [512, 2048], P('lon'), may hold values from -0.25 to 0.25
- feedforward_out_weight: bfloat16 [2048, 512], P('lon'), may hold values from -0.125 to 0.125
- merging_reduction_weight: bfloat16 [2048, 1024], P('lon'), may hold values from -0.125 to 0.125
- head_scale_logarithm: float32 [8], replicated, may hold values from 2.3 to 5.3
- bias_network_first_weight: float32 [2, 512], replicated, may hold values from -4 to 4
- bias_network_first_bias: float32 [512], replicated, may hold values from -4 to 4
- bias_network_second_weight: float32 [512, 8], replicated, may hold values from -0.25 to 0.25
- attention_norm_gain: float32 [512], replicated, may hold values from 0.1 to 1.9
- attention_norm_offset: float32 [512], replicated, may hold values from -3 to 3
- feedforward_norm_gain: float32 [512], replicated, may hold values from 0.1 to 1.9
- feedforward_norm_offset: float32 [512], replicated, may hold values from -3 to 3
- merging_norm_gain: float32 [1024], replicated, may hold values from 0.1 to 1.9
- merging_norm_offset: float32 [1024], replicated, may hold values from -3 to 3
Outputs:
- merged: bfloat16 [48, 1152, 1024], P('lat', 'lon')
All inputs are finite; a program needn't handle non-finite values.
Results may differ from a plain program's by a relative error of at most 0.012.
Values may be sent and summed in bfloat16 or wider, within the bound.
No kernel may reach another device: no remote copies, remote signals or barrier semaphores. Data moves between devices by JAX's collectives and lax.ppermute only.
A program may use at most 64 MiB of HBM per device.

v0:
```python
import jax
import jax.numpy as jnp
from jax import lax
from jax.sharding import PartitionSpec as P

HEAD_COUNT = 8
WIN_ROWS = 6
WIN_COLS = 12
SHIFT_ROWS = 3
SHIFT_COLS = 6


def passed_along(block, axis, distance):
    devices = range(lax.axis_size(axis))
    route = [((i - distance) % len(devices), i) for i in devices]
    return lax.ppermute(block, axis, route)


def passed_along_2(shard, axis, by):
    size = lax.axis_size(axis)
    pairs = [(i, i + by) for i in range(size) if 0 <= i + by < size]
    return lax.ppermute(shard, axis, pairs)


def layer_norm(values, norm_gain, norm_shift):
    average = jnp.mean(values, axis=-1, keepdims=True)
    centred = values - average
    variance = jnp.mean(centred * centred, axis=-1, keepdims=True)
    return centred * lax.rsqrt(variance + 1e-05) * norm_gain + norm_shift


def bias_by_position(
    bias_network_first_weight, bias_network_first_bias, bias_network_second_weight
):
    span_rows = 2 * WIN_ROWS - 1
    span_cols = 2 * WIN_COLS - 1
    entry_index = jnp.arange(span_rows * span_cols, dtype=jnp.int32)
    offset_rows = entry_index // span_cols - (WIN_ROWS - 1)
    offset_cols = entry_index % span_cols - (WIN_COLS - 1)
    relative_coordinates = jnp.stack(
        [
            offset_rows.astype(jnp.float32) * (8.0 / (WIN_ROWS - 1)),
            offset_cols.astype(jnp.float32) * (8.0 / (WIN_COLS - 1)),
        ],
        axis=1,
    )
    relative_coordinates = (
        jnp.sign(relative_coordinates) * jnp.log2(jnp.abs(relative_coordinates) + 1.0) / 3.0
    )
    bias_hidden_layer = jax.nn.relu(
        jnp.dot(relative_coordinates, bias_network_first_weight, precision=lax.Precision.HIGHEST)
        + bias_network_first_bias
    )
    table_entries = 16.0 * jax.nn.sigmoid(
        jnp.dot(bias_hidden_layer, bias_network_second_weight, precision=lax.Precision.HIGHEST)
    )
    window_tokens = WIN_ROWS * WIN_COLS
    token_row = jnp.arange(window_tokens, dtype=jnp.int32) // WIN_COLS
    token_col = jnp.arange(window_tokens, dtype=jnp.int32) % WIN_COLS
    lookup = (
        (token_row[:, None] - token_row[None, :] + WIN_ROWS - 1) * span_cols
        + token_col[:, None]
        - token_col[None, :]
        + WIN_COLS
        - 1
    )
    one_hot = (lookup[:, :, None] == entry_index[None, None, :]).astype(jnp.float32)
    return jnp.einsum("qkr,rh->hqk", one_hot, table_entries, precision=lax.Precision.HIGHEST)


def unit_rows(vectors):
    square_sum = jnp.sum(vectors * vectors, axis=-1, keepdims=True) + 1e-06
    return (vectors * lax.rsqrt(square_sum)).astype(jnp.bfloat16)


def window_attention(triple, region, relative_position_bias, head_scale, band_rows):
    tile_rows, tile_cols, triple_width = triple.shape
    model_width = triple_width // 3
    head_dim = model_width // HEAD_COUNT
    band_count = tile_rows // band_rows
    col_count = tile_cols // WIN_COLS
    window_tokens = band_rows * WIN_COLS
    windows = triple.reshape(band_count, band_rows, col_count, WIN_COLS, triple_width).transpose(
        0, 2, 1, 3, 4
    )
    windows = windows.reshape(band_count * col_count, window_tokens, 3, HEAD_COUNT, head_dim)
    unit_q = unit_rows(windows[:, :, 0].astype(jnp.float32))
    unit_k = unit_rows(windows[:, :, 1].astype(jnp.float32))
    values_all = windows[:, :, 2]
    scores = jnp.einsum("wqhd,wkhd->whqk", unit_q, unit_k, preferred_element_type=jnp.float32)
    scores = (
        scores * head_scale[None, :, None, None]
        + relative_position_bias[None, :, :window_tokens, :window_tokens]
    )
    labels = jnp.broadcast_to(
        region.reshape(band_count, 1, band_rows, 1), (band_count, col_count, band_rows, WIN_COLS)
    ).reshape(band_count * col_count, window_tokens)
    allowed = labels[:, :, None] == labels[:, None, :]
    scores = jnp.where(allowed[:, None], scores, -jnp.inf)
    peak = jnp.max(scores, axis=-1, keepdims=True)
    expo = jnp.exp(scores - peak)
    weights = (expo / jnp.sum(expo, axis=-1, keepdims=True)).astype(jnp.bfloat16)
    mixed = jnp.einsum(
        "whqk,wkhd->wqhd", weights, values_all, preferred_element_type=jnp.float32
    ).astype(jnp.bfloat16)
    mixed = mixed.reshape(band_count, col_count, band_rows, WIN_COLS, model_width).transpose(
        0, 2, 1, 3, 4
    )
    return mixed.reshape(tile_rows, tile_cols, model_width)


def local(
    patches,
    query_key_value_weight,
    attention_output_weight,
    feedforward_in_weight,
    feedforward_out_weight,
    merging_reduction_weight,
    head_scale_logarithm,
    bias_network_first_weight,
    bias_network_first_bias,
    bias_network_second_weight,
    attention_norm_gain,
    attention_norm_offset,
    feedforward_norm_gain,
    feedforward_norm_offset,
    merging_norm_gain,
    merging_norm_offset,
):
    tile_rows, tile_cols, model_width = patches.shape
    qkv_full, proj_full, fc1_full, fc2_full, merge_full = (
        lax.all_gather(query_key_value_weight, "lon", axis=0, tiled=True),
        lax.all_gather(attention_output_weight, "lon", axis=0, tiled=True),
        lax.all_gather(feedforward_in_weight, "lon", axis=0, tiled=True),
        lax.all_gather(feedforward_out_weight, "lon", axis=0, tiled=True),
        lax.all_gather(merging_reduction_weight, "lon", axis=0, tiled=True),
    )
    relative_position_bias = bias_by_position(
        bias_network_first_weight, bias_network_first_bias, bias_network_second_weight
    )
    head_scale = jnp.exp(jnp.minimum(head_scale_logarithm, jnp.log(100.0)))
    east_cols = passed_along(patches[:, :SHIFT_COLS], "lon", -1)
    col_frame = jnp.concatenate([patches[:, SHIFT_COLS:], east_cols], axis=1)
    south_rows = passed_along_2(col_frame[:SHIFT_ROWS], "lat", -1)
    extended = jnp.concatenate([col_frame[SHIFT_ROWS:], south_rows], axis=0)
    tokens_flat = jnp.concatenate(
        [extended.reshape(-1, model_width), col_frame[:SHIFT_ROWS].reshape(-1, model_width)], axis=0
    )
    triple_sum = jnp.dot(tokens_flat, qkv_full, preferred_element_type=jnp.float32)
    triple = triple_sum.astype(jnp.bfloat16)
    main_count = tile_rows * tile_cols
    is_last = lax.axis_index("lat") == lax.axis_size("lat") - 1
    region = jnp.where(
        is_last & (jnp.arange(tile_rows, dtype=jnp.int32) >= tile_rows - SHIFT_ROWS), 1, 0
    ).astype(jnp.int32)
    attended_main = window_attention(
        triple[:main_count].reshape(tile_rows, tile_cols, 3 * model_width),
        region,
        relative_position_bias,
        head_scale,
        WIN_ROWS,
    )
    attended_top = window_attention(
        triple[main_count:].reshape(SHIFT_ROWS, tile_cols, 3 * model_width),
        jnp.zeros((SHIFT_ROWS,), jnp.int32),
        relative_position_bias,
        head_scale,
        SHIFT_ROWS,
    )
    attended = jnp.concatenate(
        [attended_main.reshape(-1, model_width), attended_top.reshape(-1, model_width)], axis=0
    )
    projected = jnp.dot(attended, proj_full, preferred_element_type=jnp.float32)
    branch_all = layer_norm(projected, attention_norm_gain, attention_norm_offset).astype(
        jnp.bfloat16
    )
    branch_main = branch_all[:main_count].reshape(tile_rows, tile_cols, model_width)
    branch_top = branch_all[main_count:].reshape(SHIFT_ROWS, tile_cols, model_width)
    from_north = passed_along_2(branch_main[tile_rows - SHIFT_ROWS :], "lat", 1)
    top_rows = jnp.where(lax.axis_index("lat") == 0, branch_top, from_north)
    row_frame = jnp.concatenate([top_rows, branch_main[: tile_rows - SHIFT_ROWS]], axis=0)
    from_west = passed_along(row_frame[:, tile_cols - SHIFT_COLS :], "lon", 1)
    attn_branch = jnp.concatenate([from_west, row_frame[:, : tile_cols - SHIFT_COLS]], axis=1)
    first = (patches.astype(jnp.float32) + attn_branch.astype(jnp.float32)).astype(jnp.bfloat16)
    first_flat = first.reshape(-1, model_width)
    up_sum = jnp.dot(first_flat, fc1_full, preferred_element_type=jnp.float32)
    hidden = jax.nn.gelu(up_sum, approximate=False).astype(jnp.bfloat16)
    down_sum = jnp.dot(hidden, fc2_full, preferred_element_type=jnp.float32)
    branch_two = layer_norm(down_sum, feedforward_norm_gain, feedforward_norm_offset)
    second = (
        (first_flat.astype(jnp.float32) + branch_two)
        .astype(jnp.bfloat16)
        .reshape(tile_rows, tile_cols, model_width)
    )
    quads = second.reshape(tile_rows // 2, 2, tile_cols // 2, 2, model_width).transpose(
        0, 2, 3, 1, 4
    )
    quads = quads.reshape(tile_rows // 2 * (tile_cols // 2), 4 * model_width)
    reduced_sum = jnp.dot(quads, merge_full, preferred_element_type=jnp.float32)
    reduced = layer_norm(reduced_sum, merging_norm_gain, merging_norm_offset)
    return reduced.astype(jnp.bfloat16).reshape(tile_rows // 2, tile_cols // 2, 2 * model_width)


def solution(mesh):
    in_specs = (
        P("lat", "lon", None),
        P("lon", None),
        P("lon", None),
        P("lon", None),
        P("lon", None),
        P("lon", None),
        P(),
        P(),
        P(),
        P(),
        P(),
        P(),
        P(),
        P(),
        P(),
        P(),
    )
    out_specs = P("lat", "lon", None)
    return jax.shard_map(local, mesh=mesh, in_specs=in_specs, out_specs=out_specs, check_vma=False)
```

profile of v0, /device:TPU:1, one launch (start us, length us, event | category | flops | bytes accessed | tf_op | source)
XLA Modules:
  0.0 511.8 jit_solution(6285002656658142179)
XLA Ops:
  6.5 0.7 all-gather.5.cloned.1.call-update
  7.3 0.7 all-gather.9.cloned.1.call-update
  8.1 0.7 all-gather.7.cloned.1.call-update
  8.8 0.9 slice.65
  9.7 8.8 %collective-permute-start = (bf16[12,6,512]{2,1,0:T(8,128)(2,1)S(1)}, bf16[12,6,512]{2,1,0:T(8,128)(2,1)S(1)}, u32[]{:S(2)}, u32[]{:S(2)}) collective-permute-start(bf16[12,6,512]{2,1,0:T(8,128)(2,1)S(1)} %slice.65), channel_id=1, source_target_pairs={{1,0},{2,1},{3,2},{4,3},{5,4},{6,5},{7,6},{8,7},{9,8},{10,9},{11,1... | collective-permute-start | bytes 221192 | tf_op jit(solution)/shard_map/ppermute | solution.py:16
  18.5 71.1 %all_gather.16 = bf16[512,512]{1,0:T(8,128)(2,1)} all-gather(bf16[8,512]{1,0:T(8,128)(2,1)} %param.18), channel_id=1, replica_groups=mesh['lat'=8,'lon'=64] {'lon'}, dimensions={0}, use_global_device_ids=true | all-gather | bytes 532480 | tf_op jit(solution)/shard_map/all_gather | solution.py:133
  89.8 0.8 broadcast_compare_fusion
  90.6 1.4 fusion.22
  92.0 0.5 fusion.30
  92.6 3.7 fusion.2
  96.5 0.9 copy.42
  97.6 1.5 collective-permute-start.1
  99.1 5.2 %collective-permute-done.1 = bf16[3,36,512]{2,1,0:T(8,128)(2,1)S(1)} collective-permute-done((bf16[3,36,512]{2,1,0:T(8,128)(2,1)S(1)}, bf16[3,36,512]{2,1,0:T(8,128)(2,1)S(1)}, u32[]{:S(2)}, u32[]{:S(2)}) %collective-permute-start.1) | collective-permute-done | bytes 110624 | tf_op jit(solution)/shard_map/ppermute | solution.py:22
  104.5 32.4 %all-gather.5.cloned.1.call-done = bf16[512,1536]{1,0:T(8,128)(2,1)} async-done(((bf16[8,1536]{1,0:T(8,128)(2,1)}), bf16[512,1536]{1,0:T(8,128)(2,1)}) %all-gather.5.cloned.1.call-update) | async-done | bytes 1572880 | tf_op jit(solution)/shard_map/all_gather | solution.py:132
  137.0 2.4 convolution_convert_fusion
  139.6 0.4 reshape.294
  140.0 0.8 slice.91
  140.8 0.3 fusion.42
  141.1 0.3 fusion.43
  141.4 0.3 fusion.24
  141.9 1.3 fusion.25
  143.4 0.7 reshape_reshape.18
  144.1 0.3 reshape_reshape.15
  144.4 1.4 copy.38
  145.8 3.4 reshape.292
  149.4 1.4 copy.57
  150.7 1.0 fusion.14
  151.8 1.2 fusion.15
  153.0 0.6 add_select_fusion
  153.7 0.4 fusion.106
  154.1 0.6 fusion.20
  154.8 0.7 copy.44
  155.5 0.6 reshape.293
  156.2 0.6 fusion.107
  156.8 0.3 multiply_reduce_fusion
  157.4 3.1 collective-permute-start.2
  160.7 2.3 collective-permute-done.2
  163.0 4.0 collective-permute-start.3
  167.0 1.6 collective-permute-done.3
  169.0 88.7 %all-gather.9.cloned.1.call-done = bf16[2048,512]{1,0:T(8,128)(2,1)} async-done(((bf16[32,512]{1,0:T(8,128)(2,1)}), bf16[2048,512]{1,0:T(8,128)(2,1)}) %all-gather.9.cloned.1.call-update) | async-done | bytes 2097168 | tf_op jit(solution)/shard_map/all_gather | solution.py:135
  257.7 120.6 %all-gather.7.cloned.1.call-done = bf16[512,2048]{1,0:T(8,128)(2,1)} async-done(((bf16[8,2048]{1,0:T(8,128)(2,1)}), bf16[512,2048]{1,0:T(8,128)(2,1)}) %all-gather.7.cloned.1.call-update) | async-done | bytes 2097168 | tf_op jit(solution)/shard_map/all_gather | solution.py:134
  378.3 11.1 %fusion.108 = (f32[432]{0:T(512)S(1)}, f32[432,512]{1,0:T(8,128)S(1)}) fusion(bf16[2048,512]{1,0:T(8,128)(2,1)} %all-gather.9.cloned.1.call-done, bf16[432,512]{1,0:T(8,128)(2,1)S(1)} %reshape.297, bf16[512,2048]{1,0:T(8,128)(2,1)} %all-gather.7.cloned.1.call-done), kind=kOutput, calls=%fused_computation.181 | convolution fusion | flops 1869667968 | bytes 5523136 | tf_op jit(solution)/shard_map/dot_general | solution.py:188
  389.7 0.3 add_convert_fusion.2
  390.1 0.3 copy.71
  390.5 0.3 reshape.298
  390.8 110.3 %all-gather.11.cloned.1.call-done = bf16[2048,1024]{1,0:T(8,128)(2,1)} async-done(((bf16[32,1024]{1,0:T(8,128)(2,1)}), bf16[2048,1024]{1,0:T(8,128)(2,1)}) %all-gather.11.cloned.1.call-update) | async-done | bytes 4194320 | tf_op jit(solution)/shard_map/all_gather | solution.py:136
  501.1 3.0 fusion.109
  504.5 0.8 reshape.299
  (91 shorter events, 3.5 us)
Async XLA Ops:
  6.5 85.4 %copy-start = (f32[512,8]{0,1:T(8,128)S(1)}, f32[512,8]{0,1:T(8,128)}, u32[]{:S(2)}) copy-start(f32[512,8]{0,1:T(8,128)} %param.25) | copy-start | bytes 49156
  6.5 89.8 %copy-start.2 = (bf16[12,36,512]{2,1,0:T(8,128)(2,1)S(1)}, bf16[12,36,512]{2,1,0:T(8,128)(2,1)}, u32[]{:S(2)}) copy-start(bf16[12,36,512]{2,1,0:T(8,128)(2,1)} %param.16) | copy-start | bytes 1327108
  6.5 89.8 %copy-start.17 = (f32[8]{0:T(128)S(1)}, f32[8]{0:T(128)}, u32[]{:S(2)}) copy-start(f32[8]{0:T(128)} %param.22) | copy-start | bytes 100
  6.5 130.4 %all-gather.5.cloned.1.call-start = ((), (), s32[]{:S(2)}) async-start(), calls=%async_computation | async-start | bytes 1597440 | tf_op jit(solution)/shard_map/all_gather | solution.py:132
  7.3 250.4 %all-gather.9.cloned.1.call-start = ((), (), s32[]{:S(2)}) async-start(), calls=%async_computation.2 | async-start | bytes 2129920 | tf_op jit(solution)/shard_map/all_gather | solution.py:135
  8.0 370.3 %all-gather.7.cloned.1.call-start = ((), (), s32[]{:S(2)}) async-start(), calls=%async_computation.1 | async-start | bytes 2129920 | tf_op jit(solution)/shard_map/all_gather | solution.py:134
  8.7 492.3 %all-gather.11.cloned.1.call-start = ((), (), s32[]{:S(2)}) async-start(), calls=%async_computation.3 | async-start | bytes 4259840 | tf_op jit(solution)/shard_map/all_gather | solution.py:136
  9.7 87.8 %collective-permute-start = (bf16[12,6,512]{2,1,0:T(8,128)(2,1)S(1)}, bf16[12,6,512]{2,1,0:T(8,128)(2,1)S(1)}, u32[]{:S(2)}, u32[]{:S(2)}) collective-permute-start(bf16[12,6,512]{2,1,0:T(8,128)(2,1)S(1)} %slice.65), channel_id=1, source_target_pairs={{1,0},{2,1},{3,2},{4,3},{5,4},{6,5},{7,6},{8,7},{9,8},{10,9},{11,1... | collective-permute-start | bytes 221192 | tf_op jit(solution)/shard_map/ppermute | solution.py:16
  96.4 45.1 %copy-start.15 = (f32[8]{0:T(128)}, f32[8]{0:T(128)S(1)}, u32[]{:S(2)}) copy-start(f32[8]{0:T(128)S(1)} %minimum_exponential_fusion) | copy-start | bytes 100
  97.6 6.8 %collective-permute-start.1 = (bf16[3,36,512]{2,1,0:T(8,128)(2,1)S(1)}, bf16[3,36,512]{2,1,0:T(8,128)(2,1)S(1)}, u32[]{:S(2)}, u32[]{:S(2)}) collective-permute-start(bf16[3,36,512]{2,1,0:T(8,128)(2,1)S(1)} %pad_maximum_fusion.2), channel_id=1, source_target_pairs={{64,0},{128,64},{192,128},{256,192},{320,256},{384,320},{448,384},... | collective-permute-start | bytes 331784 | tf_op jit(solution)/shard_map/ppermute | solution.py:22
  139.4 1.7 copy-start.1
  141.1 3.0 slice-start
  150.7 2.3 copy-start.6
  150.7 2.3 copy-start.8
  150.7 2.3 copy-start.16
  153.0 1.1 copy-start.4
  154.7 1.5 copy-start.5
  154.8 1.5 copy-start.7
  155.4 1.7 copy-start.11
  155.5 1.7 copy-start.12
  156.8 11.8 %copy-start.3 = (bf16[12,36,512]{2,1,0:T(8,128)(2,1)S(1)}, bf16[12,36,512]{2,1,0:T(8,128)(2,1)}, u32[]{:S(2)}) copy-start(bf16[12,36,512]{2,1,0:T(8,128)(2,1)} %param.16) | copy-start | bytes 1327108
  157.4 5.5 %collective-permute-start.2 = (bf16[3,36,512]{2,1,0:T(8,128)(2,1)S(1)}, bf16[3,36,512]{2,1,0:T(8,128)(2,1)S(1)}, u32[]{:S(2)}, u32[]{:S(2)}) collective-permute-start(bf16[3,36,512]{2,1,0:T(8,128)(2,1)S(1)} %slice.79), channel_id=1, source_target_pairs={{0,64},{64,128},{128,192},{192,256},{256,320},{320,384},{384,448},... | collective-permute-start | bytes 331784 | tf_op jit(solution)/shard_map/ppermute | solution.py:22
  163.0 5.6 %collective-permute-start.3 = (bf16[12,6,512]{2,1,0:T(8,128)(2,1)S(1)}, bf16[12,6,512]{2,1,0:T(8,128)(2,1)S(1)}, u32[]{:S(2)}, u32[]{:S(2)}) collective-permute-start(bf16[12,6,512]{2,1,0:T(8,128)(2,1)S(1)} %pad_maximum_fusion.3), channel_id=1, source_target_pairs={{63,0},{0,1},{1,2},{2,3},{3,4},{4,5},{5,6},{6,7},{7,8},{8,9},{9,10... | collective-permute-start | bytes 221192 | tf_op jit(solution)/shard_map/ppermute | solution.py:16
  168.9 220.7 %copy-start.13 = (f32[512]{0:T(512)S(1)}, f32[512]{0:T(512)}, u32[]{:S(2)}) copy-start(f32[512]{0:T(512)} %param.29) | copy-start | bytes 6148
  169.0 220.7 %copy-start.14 = (f32[512]{0:T(512)S(1)}, f32[512]{0:T(512)}, u32[]{:S(2)}) copy-start(f32[512]{0:T(512)} %param.28) | copy-start | bytes 6148
  390.1 114.2 %copy-start.9 = (f32[1024]{0:T(1024)S(1)}, f32[1024]{0:T(1024)}, u32[]{:S(2)}) copy-start(f32[1024]{0:T(1024)} %param.31) | copy-start | bytes 12292
  390.1 114.2 %copy-start.10 = (f32[1024]{0:T(1024)S(1)}, f32[1024]{0:T(1024)}, u32[]{:S(2)}) copy-start(f32[1024]{0:T(1024)} %param.30) | copy-start | bytes 12292
Sparse Core Ops, SparseCore 0:
  9.5 127.3 all-gather.4
  139.1 118.5 all-gather.8
  259.8 118.3 all-gather.6
  380.3 120.7 all-gather.10
where the time goes:
time: 512 us
  waiting for transfers between devices  363 us (71%)
  blocking collectives  71.1 us (14%)
  matrix products  25.6 us (5%)
  starting transfers between devices  17.5 us (3%)
  local copies, waits for them, and re-layouts  14.4 us (3%)
  between operations  13.8 us (3%)
  other arithmetic  6.18 us (1%)
    all_gather x1, waiting for transfers between devices, local(): lax.all_gather(feedforward_in_weight, 'lon', axis=0, tiled=True)  121 us
    all_gather x1, waiting for transfers between devices, local(): lax.all_gather(merging_reduction_weight, 'lon', axis=0, tiled=True)  110 us
    all_gather x1, waiting for transfers between devices, local(): lax.all_gather(feedforward_out_weight, 'lon', axis=0, tiled=True)  88.7 us
    all_gather x1, blocking collectives, local(): lax.all_gather(attention_output_weight, 'lon', axis=0, tiled=True)  71.1 us
    all_gather x1, waiting for transfers between devices, local(): lax.all_gather(query_key_value_weight, 'lon', axis=0, tiled=True)  32.4 us
    ppermute x2, starting transfers between devices, passed_along(): return lax.ppermute(block, axis, route)  12.8 us
    dot_general x1, matrix products, local(): down_sum = jnp.dot(hidden, fc2_full, preferred_element_type=jnp.float32)  11.1 us
  transfers between devices with their start and end apart: 8, of which 7 were waited for; matrix products, arithmetic and copies ran while one was open for 8% of the time, Pallas kernels for 0%

commit v1 on v0

v1 whole, which is shorter than its diff:
```python
import jax
import jax.numpy as jnp
import numpy as np
from jax import lax
from jax.experimental import pallas as pl
from jax.experimental.pallas import tpu as pltpu
from jax.sharding import Mesh
from jax.sharding import PartitionSpec as P

D = 512
HEAD_COUNT = 8
WIN_ROWS = 6
WIN_COLS = 12
PAD_COLS = 16
SHIFT_ROWS = 3
SHIFT_COLS = 6
FFN = 2048
WIN_PAD = WIN_ROWS * PAD_COLS
KEY_PAD = 128
BANDS = 3
WINS = 4
QUAD_ROWS = 112
LAT = ("y_hi", "x")
LON = ("z", "y_lo", "core")
PLANE = ("y_hi", "x", "y_lo")
OFF = -1e30
BF16 = jnp.bfloat16
F32 = jnp.float32
QUERY_ROWS = ((48, 48), (0, 96), (0, 48))


def shifted(block, axes, by, wrap):
    size = lax.axis_size(axes)
    pairs = [(i, (i + by) % size) for i in range(size) if wrap or 0 <= i + by < size]
    return lax.ppermute(block, axes, pairs)


def spread(block, axes):
    size = lax.axis_size(axes)
    return lax.all_to_all(jnp.broadcast_to(block[None], (size,) + block.shape), axes, 0, 0)


def bias_entries(first_weight, first_bias, second_weight):
    span_rows = 2 * WIN_ROWS - 1
    span_cols = 2 * WIN_COLS - 1
    entry = np.arange(span_rows * span_cols)
    coordinates = np.stack(
        [
            (entry // span_cols - (WIN_ROWS - 1)) * (8.0 / (WIN_ROWS - 1)),
            (entry % span_cols - (WIN_COLS - 1)) * (8.0 / (WIN_COLS - 1)),
        ],
        axis=1,
    )
    coordinates = np.sign(coordinates) * np.log2(np.abs(coordinates) + 1.0) / 3.0
    coordinates = jnp.asarray(coordinates, F32)
    hidden = jax.nn.relu(
        coordinates[:, :1] * first_weight[:1] + coordinates[:, 1:] * first_weight[1:] + first_bias
    )
    return 16.0 * jax.nn.sigmoid(
        lax.dot_general(
            second_weight, hidden, (((0,), (1,)), ((), ())), precision=lax.Precision.HIGHEST
        )
    )


def bias_lookup():
    q = np.arange(WIN_PAD)
    k = np.arange(KEY_PAD)
    qa, qb = q // PAD_COLS, np.minimum(q % PAD_COLS, WIN_COLS - 1)
    ka, kb = np.minimum(k // PAD_COLS, WIN_ROWS - 1), np.minimum(k % PAD_COLS, WIN_COLS - 1)
    rows = qa[:, None] - ka[None] + WIN_ROWS - 1
    cols = qb[:, None] - kb[None] + WIN_COLS - 1
    return rows * (2 * WIN_COLS - 1) + cols


def unit_norm(triple, ones):
    rounded = triple.astype(BF16)
    exact = rounded.astype(F32)
    square = exact * exact
    high = square.astype(BF16)
    low = (square - high.astype(F32)).astype(BF16)
    parts = []
    for i in range(D // 256):
        cut = slice(i * 256, i * 256 + 256)
        total = jnp.dot(high[:, cut], ones, preferred_element_type=F32)
        total += jnp.dot(low[:, cut], ones, preferred_element_type=F32)
        parts.append((exact[:, cut] * lax.rsqrt(total + 1e-06)).astype(BF16))
    return parts


def norm_rows(values, gain, offset):
    average = jnp.mean(values, axis=-1, keepdims=True)
    centred = values - average
    variance = jnp.mean(centred * centred, axis=-1, keepdims=True)
    return centred * lax.rsqrt(variance + 1e-05) * gain + offset


def attention_kernel(
    core_ref,
    scale_ref,
    windows_ref,
    bias_ref,
    patches_ref,
    select_ref,
    gain_ref,
    offset_ref,
    mine_ref,
    other_ref,
    out_ref,
    weight,
    queries,
    keys,
    values,
    heads,
    sems,
):
    core = core_ref[0]
    copies = []
    for m in range(16):
        lat, y_lo = m // 2, m % 2
        for part, (ref, of) in enumerate(((mine_ref, core), (other_ref, 1 - core))):
            column = pl.multiple_of((lat * 2 + of) * 128, 128)
            copies.append(
                pltpu.make_async_copy(
                    ref.at[m],
                    weight.at[:, pl.ds(y_lo * 16, 16), pl.ds(column, 128)],
                    sems.at[m * 2 + part],
                )
            )
    for copy in copies:
        copy.start()
    for copy in copies:
        copy.wait()

    row = lax.broadcasted_iota(jnp.int32, (256, 256), 0)
    lane = lax.broadcasted_iota(jnp.int32, (256, 256), 1)
    ones = jnp.where(row // 64 == lane // 64, 1.0, 0.0).astype(BF16)
    row2 = lax.broadcasted_iota(jnp.int32, (256, 128), 0)
    lane2 = lax.broadcasted_iota(jnp.int32, (256, 128), 1)
    counts = jnp.where((row2 >= 128) == (lane2 >= 64), 1.0, 0.0).astype(BF16)
    low_half = lax.broadcasted_iota(jnp.int32, (WIN_PAD, 128), 1) < 64
    zero = jnp.zeros((WIN_PAD, 128), BF16)
    gap = jnp.zeros((KEY_PAD - WIN_PAD, 128), BF16)
    half = WINS * WIN_PAD

    def columns(start, width):
        return weight[:, :, start : start + width].reshape(D, width)

    def both(block):
        return jnp.concatenate(
            [jnp.where(low_half, block, zero), gap, jnp.where(low_half, zero, block), gap], axis=0
        )

    done = 0
    for band in range(BANDS):
        tokens = windows_ref[band * half : (band + 1) * half, :]
        for target, start in ((queries, 0), (keys, D)):
            total = jnp.dot(tokens, columns(start, D), preferred_element_type=F32)
            for i, part in enumerate(unit_norm(total, ones)):
                target[:, i * 256 : i * 256 + 256] = part
        values[...] = jnp.dot(tokens, columns(2 * D, D), preferred_element_type=F32).astype(BF16)
        first, count = QUERY_ROWS[band]

        def window(w, _, band=band, first=first, count=count, done=done):
            base = pl.multiple_of(w * WIN_PAD, WIN_PAD)
            for pair in range(HEAD_COUNT // 2):
                cut = slice(pair * 128, pair * 128 + 128)
                query = queries[pl.ds(base + first, count), cut]
                key = both(keys[pl.ds(base, WIN_PAD), cut])
                value = both(values[pl.ds(base, WIN_PAD), cut])
                scores = lax.dot_general(
                    query, key, (((1,), (1,)), ((), ())), preferred_element_type=F32
                )
                expo = []
                for h in range(2):
                    head = pair * 2 + h
                    one = scores[:, h * 128 : h * 128 + 128] * scale_ref[head]
                    one = one + bias_ref[band, head, first : first + count, :]
                    peak = jnp.max(one, axis=-1, keepdims=True)
                    expo.append(jnp.exp(one - peak).astype(BF16))
                mixed = jnp.dot(
                    jnp.concatenate(expo, axis=1),
                    jnp.concatenate([value, counts], axis=1),
                    preferred_element_type=F32,
                )
                place = pl.multiple_of(done + w * count, 16)
                heads[pl.ds(place, count), cut] = (mixed[:, :128] / mixed[:, 128:]).astype(BF16)
            return 0

        lax.fori_loop(0, WINS, window, 0)
        done += WINS * count

    own = jnp.dot(select_ref[...], heads[...], preferred_element_type=F32).astype(BF16)
    projected = jnp.dot(own, columns(3 * D, D), preferred_element_type=F32)
    branch = norm_rows(projected, gain_ref[...], offset_ref[...]).astype(BF16)
    out_ref[...] = (patches_ref[...].astype(F32) + branch.astype(F32)).astype(BF16)


def feedforward_kernel(
    core_ref,
    first_ref,
    gain_ref,
    offset_ref,
    merge_gain_ref,
    merge_offset_ref,
    mine_ref,
    other_ref,
    merge_ref,
    out_ref,
    up,
    down,
    merge,
    up_sems,
    down_sems,
    merge_sems,
):
    core = core_ref[0]
    ups, downs, merges = [], [], []
    for m in range(16):
        y_hi, x, y_lo = m // 8, m // 2 % 4, m % 2
        for part, (ref, of) in enumerate(((mine_ref, core), (other_ref, 1 - core))):
            column = pl.multiple_of((m // 2 * 2 + of) * 128, 128)
            ups.append(
                pltpu.make_async_copy(
                    ref.at[m, 0],
                    up.at[:, pl.ds(y_lo * 16, 16), pl.ds(column, 128)],
                    up_sems.at[m * 2 + part],
                )
            )
            start = pl.multiple_of(y_lo * 64 + of * 32 + y_hi * 16, 16)
            downs.append(
                pltpu.make_async_copy(
                    ref.at[m, 1],
                    down.at[:, pl.ds(start, 16), pl.ds(x * 128, 128)],
                    down_sems.at[m * 2 + part],
                )
            )
        x, y_lo, of = m // 4, m // 2 % 2, m % 2
        merges.append(
            pltpu.make_async_copy(
                merge_ref.at[m],
                merge.at[:, pl.ds(y_lo * 64 + of * 32, 32), pl.ds(x * 256, 256)],
                merge_sems.at[m],
            )
        )
    for copy in ups + downs + merges:
        copy.start()
    for copy in ups:
        copy.wait()
    tokens = first_ref[...]
    total = None
    for n in range(FFN // 512):
        cut = slice(n * 512, n * 512 + 512)
        hidden = jnp.dot(tokens, up[:, :, cut].reshape(D, 512), preferred_element_type=F32)
        hidden = (0.5 * hidden * (1.0 + lax.erf(hidden * (0.5**0.5)))).astype(BF16)
        if n == 0:
            for copy in downs:
                copy.wait()
        piece = jnp.dot(
            hidden, down[n * 4 : n * 4 + 4].reshape(512, D), preferred_element_type=F32
        )
        total = piece if total is None else total + piece
    branch = norm_rows(total, gain_ref[...], offset_ref[...])
    second = (tokens.astype(F32) + branch).astype(BF16)
    for copy in merges:
        copy.wait()
    total = None
    for n in range(4):
        piece = jnp.dot(
            second[n * QUAD_ROWS : (n + 1) * QUAD_ROWS],
            merge[n * 4 : n * 4 + 4].reshape(512, 2 * D),
            preferred_element_type=F32,
        )
        total = piece if total is None else total + piece
    reduced = norm_rows(total, merge_gain_ref[...], merge_offset_ref[...])
    for i in range(6):
        out_ref[i] = reduced[i * 18 : i * 18 + 18].astype(BF16)


def selection():
    place = np.full((12, 36), -1)
    done = 0
    for band in range(BANDS):
        first, count = QUERY_ROWS[band]
        for w in range(WINS):
            for r in range(count):
                a, b = (first + r) // PAD_COLS, (first + r) % PAD_COLS
                i = band * WIN_ROWS + a - SHIFT_ROWS
                j = w * WIN_COLS + b - SHIFT_COLS
                if b < WIN_COLS and 0 <= j < 36:
                    place[i, j] = done + r
            done += count
    order = place.reshape(6, 2, 18, 2).transpose(3, 1, 0, 2).reshape(4, 108)
    order = np.pad(order, ((0, 0), (0, QUAD_ROWS - 108)), constant_values=-1).reshape(-1)
    return (order[:, None] == np.arange(done)[None]).astype(np.float32)


def local(
    patches,
    query_key_value_weight,
    attention_output_weight,
    feedforward_in_weight,
    feedforward_out_weight,
    merging_reduction_weight,
    head_scale_logarithm,
    bias_network_first_weight,
    bias_network_first_bias,
    bias_network_second_weight,
    attention_norm_gain,
    attention_norm_offset,
    feedforward_norm_gain,
    feedforward_norm_offset,
    merging_norm_gain,
    merging_norm_offset,
):
    lat = lax.axis_index(LAT)
    core = lax.axis_index("core")
    x = lax.axis_index("x")

    mine = jnp.concatenate(
        [query_key_value_weight, attention_output_weight, feedforward_in_weight], axis=1
    )
    theirs = shifted(mine, "core", 1, True)
    rows = jnp.concatenate(
        [jnp.where(core == 0, mine, theirs), jnp.where(core == 0, theirs, mine)], axis=0
    )
    at = (lat * 2 + core) * 128
    units = jnp.stack(
        [
            lax.dynamic_slice(rows, (0, at), (16, 128)),
            lax.dynamic_slice(rows, (0, 2048 + at), (16, 128)),
            lax.dynamic_slice(
                feedforward_out_weight, (lax.axis_index("y_hi") * 16, x * 128), (16, 128)
            ),
        ]
    )
    along_z = spread(units, "z")
    merge_part = lax.dynamic_slice(merging_reduction_weight, (0, x * 256), (32, 256))
    merge_z = spread(merge_part, "z")
    merge_all = lax.all_gather(merge_z, ("x", "y_lo", "core"), axis=0)
    attn_mine = spread(along_z[:, 0], PLANE)
    attn_other = shifted(attn_mine, "core", 1, True)
    ffn_mine = spread(along_z[:, 1:].transpose(1, 0, 2, 3), PLANE)
    ffn_other = shifted(ffn_mine, "core", 1, True)

    east = shifted(patches[:, :SHIFT_COLS], LON, -1, True)
    west = shifted(patches[:, 36 - SHIFT_COLS :], LON, 1, True)
    wide = jnp.concatenate([west, patches, east], axis=1)
    south = shifted(wide[:SHIFT_ROWS], LAT, -1, False)
    north = shifted(wide[12 - SHIFT_ROWS :], LAT, 1, False)
    tall = jnp.concatenate([north, wide, south], axis=0)
    windows = tall.reshape(BANDS, WIN_ROWS, WINS, WIN_COLS, D).transpose(0, 2, 1, 3, 4)
    windows = jnp.pad(windows, ((0, 0), (0, 0), (0, 0), (0, PAD_COLS - WIN_COLS), (0, 0)))
    windows = windows.reshape(BANDS * WINS * WIN_PAD, D)
    ordered = patches.reshape(6, 2, 18, 2, D).transpose(3, 1, 0, 2, 4).reshape(4, 108, D)
    ordered = jnp.pad(ordered, ((0, 0), (0, QUAD_ROWS - 108), (0, 0))).reshape(4 * QUAD_ROWS, D)

    table = bias_entries(
        bias_network_first_weight, bias_network_first_bias, bias_network_second_weight
    )
    lookup = bias_lookup()
    entries = table.shape[1]
    one_hot = (
        jnp.asarray(lookup.reshape(-1), jnp.int32)[None, :]
        == jnp.arange(entries, dtype=jnp.int32)[:, None]
    ).astype(F32)
    bias = jnp.dot(table, one_hot, precision=lax.Precision.HIGHEST)
    bias = bias.reshape(HEAD_COUNT, WIN_PAD, KEY_PAD)
    key = np.arange(KEY_PAD)
    held = (key < WIN_PAD) & (key % PAD_COLS < WIN_COLS)
    bias = jnp.where(jnp.asarray(held), bias, OFF)
    apart = (np.arange(WIN_PAD)[:, None] // 48) != (key[None] // 48)
    seam = jnp.stack([lat == 0, jnp.bool_(False), lat == 7])
    bias = jnp.where(seam[:, None, None, None] & jnp.asarray(apart), OFF, bias[None])
    head_scale = jnp.exp(jnp.minimum(head_scale_logarithm, jnp.log(100.0)))

    vmem = pl.BlockSpec(memory_space=pltpu.VMEM)
    smem = pl.BlockSpec(memory_space=pltpu.SMEM)
    anywhere = pl.BlockSpec(memory_space=pl.ANY)
    core_index = core.astype(jnp.int32).reshape(1)
    half = WINS * WIN_PAD
    first = pl.pallas_call(
        attention_kernel,
        out_shape=jax.ShapeDtypeStruct((4 * QUAD_ROWS, D), BF16),
        in_specs=[smem, smem] + [vmem] * 6 + [anywhere] * 2,
        out_specs=vmem,
        scratch_shapes=[
            pltpu.VMEM((16, 32, 2048), BF16),
            pltpu.VMEM((half, D), BF16),
            pltpu.VMEM((half, D), BF16),
            pltpu.VMEM((half, D), BF16),
            pltpu.VMEM((768, D), BF16),
            pltpu.SemaphoreType.DMA((32,)),
        ],
        compiler_params=pltpu.CompilerParams(vmem_limit_bytes=40 * 1024 * 1024),
        cost_estimate=pl.CostEstimate(
            flops=6_000_000_000, bytes_accessed=20_000_000, transcendentals=1_000_000
        ),
        name="attention",
    )(
        core_index,
        head_scale,
        windows,
        bias,
        ordered,
        jnp.asarray(selection(), BF16),
        attention_norm_gain.reshape(1, D),
        attention_norm_offset.reshape(1, D),
        attn_mine,
        attn_other,
    )
    return pl.pallas_call(
        feedforward_kernel,
        out_shape=jax.ShapeDtypeStruct((6, 18, 2 * D), BF16),
        in_specs=[smem] + [vmem] * 5 + [anywhere] * 3,
        out_specs=vmem,
        scratch_shapes=[
            pltpu.VMEM((16, 32, FFN), BF16),
            pltpu.VMEM((16, 128, D), BF16),
            pltpu.VMEM((16, 128, 2 * D), BF16),
            pltpu.SemaphoreType.DMA((32,)),
            pltpu.SemaphoreType.DMA((32,)),
            pltpu.SemaphoreType.DMA((16,)),
        ],
        compiler_params=pltpu.CompilerParams(vmem_limit_bytes=40 * 1024 * 1024),
        cost_estimate=pl.CostEstimate(
            flops=3_000_000_000, bytes_accessed=20_000_000, transcendentals=1_000_000
        ),
        name="feedforward",
    )(
        core_index,
        first,
        feedforward_norm_gain.reshape(1, D),
        feedforward_norm_offset.reshape(1, D),
        merging_norm_gain.reshape(1, 2 * D),
        merging_norm_offset.reshape(1, 2 * D),
        ffn_mine,
        ffn_other,
        merge_all.reshape(16, 16, 32, 256),
    )


def solution(mesh):
    fine = Mesh(mesh.devices.reshape(2, 4, 16, 2, 2), ("y_hi", "x", "z", "y_lo", "core"))
    in_specs = (P(LAT, LON, None),) + (P(LON, None),) * 5 + (P(),) * 10
    return jax.shard_map(
        local, mesh=fine, in_specs=in_specs, out_specs=P(LAT, LON, None), check_vma=False
    )
```

time: 512 us -> 207 us (0.40)
  the two profiles are of different devices: /device:TPU:1 before, /device:TPU:38 now
where the time goes in v1:
time: 207 us; the launch traced here: 206 us
  blocking collectives  55.3 us (27%)
  waiting for transfers between devices  41.5 us (20%)
  starting transfers between devices  34.2 us (17%)
  Pallas kernels  28.2 us (14%)
  local copies, waits for them, and re-layouts  24.8 us (12%)
  between operations  13.8 us (7%)
  matrix products  4.62 us (2%)
  other arithmetic  3 us (1%)
    all_to_all x2, blocking collectives, spread(): lax.all_to_all(jnp.broadcast_to(block[None], (size,) + block.shape), axes...  55.3 us
    all_to_all x2, waiting for transfers between devices, spread(): lax.all_to_all(jnp.broadcast_to(block[None], (size,) + block.shape), axes...  31 us
    pallas_call x1, Pallas kernels, local(): pl.pallas_call(attention_kernel, out_shape=jax.ShapeDtypeStruct((4 * QUAD...  21.8 us
    ppermute x7, starting transfers between devices, shifted(): return lax.ppermute(block, axes, pairs)  19.4 us
    all_to_all x2, starting transfers between devices, spread(): lax.all_to_all(jnp.broadcast_to(block[None], (size,) + block.shape), axes...  14.8 us
    ppermute x7, waiting for transfers between devices, shifted(): return lax.ppermute(block, axes, pairs)  10.6 us
    unnamed x50, local copies, waits for them, and re-layouts  9.91 us
    pallas_call x1, Pallas kernels, local(): pl.pallas_call(feedforward_kernel, out_shape=jax.ShapeDtypeStruct((6, 18,...  6.48 us
  transfers between devices with their start and end apart: 10, of which 5 were waited for; matrix products, arithmetic and copies ran while one was open for 13% of the time, Pallas kernels for 11%

profile of v1, /device:TPU:38, one launch (start us, length us, event | category | flops | bytes accessed | tf_op | source)
XLA Modules:
  0.0 205.5 jit_solution(15026446375708272646)
XLA Ops:
  6.5 0.8 copy-done
  7.4 33.0 %all_to_all.20 = bf16[16,32,256]{2,1,0:T(8,128)(2,1)} all-to-all(bf16[16,32,256]{2,1,0:T(8,128)(2,1)S(1)} %broadcast_in_dim.68), channel_id=1, replica_groups=mesh['y_hi'=2,'x'=4,'z'=16,'y_lo'=2,'core'=2] {'z'}, dimensions={0} | all-to-all | bytes 524288 | tf_op jit(solution)/shard_map/all_to_all | solution.py:40
  40.4 0.0 all-gather.3.cloned.1.call-update
  40.4 0.7 constant_dynamic-update-slice_fusion.2
  41.2 0.7 constant_dynamic-update-slice_fusion.1
  41.9 0.8 constant_dynamic-update-slice_fusion
  42.6 1.9 collective-permute-start.4
  44.6 1.2 collective-permute-done.4
  45.8 0.7 fusion.20
  46.5 22.3 %all_to_all.21 = bf16[16,3,16,128]{3,2,1,0:T(8,128)(2,1)S(1)} all-to-all(bf16[16,3,16,128]{3,2,1,0:T(8,128)(2,1)S(1)} %broadcast_in_dim.64), channel_id=1, replica_groups=mesh['y_hi'=2,'x'=4,'z'=16,'y_lo'=2,'core'=2] {'z'}, dimensions={0} | all-to-all | bytes 393216 | tf_op jit(solution)/shard_map/all_to_all | solution.py:40
  68.9 1.9 broadcast_in_dim.67
  70.7 7.4 %all-to-all-start.2 = ((bf16[16,2,16,16,128]{4,3,2,1,0:T(8,128)(2,1)}), bf16[16,2,16,16,128]{4,3,2,1,0:T(8,128)(2,1)S(1)}, u32[]{:S(2)}, u32[]{:S(2)}) async-start(bf16[16,2,16,16,128]{4,3,2,1,0:T(8,128)(2,1)} %broadcast_in_dim.67), calls=%async_computation.2 | async-start | bytes 4194304 | tf_op jit(solution)/shard_map/all_to_all | solution.py:40
  78.2 27.5 %all-to-all-done.2.mine_ref = bf16[16,2,16,16,128]{4,3,2,1,0:T(8,128)(2,1)S(1)} async-done(((bf16[16,2,16,16,128]{4,3,2,1,0:T(8,128)(2,1)}), bf16[16,2,16,16,128]{4,3,2,1,0:T(8,128)(2,1)S(1)}, u32[]{:S(2)}, u32[]{:S(2)}) %all-to-all-start.2) | async-done | bytes 2097184 | tf_op jit(solution)/shard_map/all_to_all | solution.py:40
  105.7 1.2 broadcast_in_dim.66
  106.9 7.4 %all-to-all-start.1 = ((bf16[16,16,16,128]{3,2,1,0:T(8,128)(2,1)}), bf16[16,16,16,128]{3,2,1,0:T(8,128)(2,1)}, u32[]{:S(2)}, u32[]{:S(2)}) async-start(bf16[16,16,16,128]{3,2,1,0:T(8,128)(2,1)} %broadcast_in_dim.66), calls=%async_computation.1 | async-start | bytes 2097152 | tf_op jit(solution)/shard_map/all_to_all | solution.py:40
  114.3 1.7 fusion.23
  116.0 1.9 collective-permute-start
  117.9 4.5 %collective-permute-start.1 = (bf16[12,6,512]{2,1,0:T(8,128)(2,1)}, bf16[12,6,512]{2,1,0:T(8,128)(2,1)S(1)}, u32[]{:S(2)}, u32[]{:S(2)}) collective-permute-start(bf16[12,6,512]{2,1,0:T(8,128)(2,1)} %get-tuple-element.8), channel_id=1, source_target_pairs={{0,63},{1,0},{2,1},{3,2},{4,3},{5,4},{6,5},{7,6},{8,7},{9,8},{10,9... | collective-permute-start | bytes 221192 | tf_op jit(solution)/shard_map/ppermute | solution.py:35
  122.5 1.9 collective-permute-start.6
  124.4 0.7 fusion.6
  125.1 0.1 pad_add_fusion
  125.2 0.7 broadcast_and_fusion
  125.9 3.4 %all-to-all-done.1.mine_ref = bf16[16,16,16,128]{3,2,1,0:T(8,128)(2,1)} async-done(((bf16[16,16,16,128]{3,2,1,0:T(8,128)(2,1)}), bf16[16,16,16,128]{3,2,1,0:T(8,128)(2,1)}, u32[]{:S(2)}, u32[]{:S(2)}) %all-to-all-start.1) | async-done | bytes 1048608 | tf_op jit(solution)/shard_map/all_to_all | solution.py:40
  129.3 2.0 collective-permute-start.5
  131.4 4.0 %fusion.2 = f32[8,96,128]{2,0,1:T(8,128)S(1)} fusion(f32[253,8]{0,1:T(8,128)S(1)} %fusion.6, s32[12288]{0:T(1024)S(1)} %copy-done.20), kind=kOutput, calls=%fused_computation.3 | convolution fusion | flops 301559808 | bytes 450464 | tf_op jit(solution)/shard_map/dot_general | solution.py:367
  135.4 0.1 copy_select_fusion
  135.5 0.1 broadcast_select_fusion.bias_ref
  135.6 2.1 %reshape.62 = bf16[6,2,18,2,512]{4,3,2,1,0:T(2,128)(2,1)} reshape(bf16[12,36,512]{2,1,0:T(8,128)(2,1)} %param.21) | data formatting | bytes 884736 | tf_op jit(solution)/shard_map/reshape | solution.py:355
  137.7 2.1 %copy.38 = bf16[6,2,18,2,512]{4,1,3,2,0:T(2,128)(2,1)} copy(bf16[6,2,18,2,512]{4,3,2,1,0:T(2,128)(2,1)} %reshape.62) | data formatting | bytes 884736 | tf_op jit(solution)/shard_map/reshape | solution.py:355
  139.8 2.0 reshape.63
  141.8 1.1 copy.35
  143.0 0.8 pad.9.clone
  143.8 0.1 pad_maximum_fusion.3
  143.9 5.0 %collective-permute-start.2 = (bf16[3,48,512]{2,1,0:T(8,128)(2,1)S(1)}, bf16[3,48,512]{2,1,0:T(8,128)(2,1)S(1)}, u32[]{:S(2)}, u32[]{:S(2)}) collective-permute-start(bf16[3,48,512]{2,1,0:T(8,128)(2,1)S(1)} %get-tuple-element.5), channel_id=1, source_target_pairs={{0,64},{64,128},{128,192},{192,256},{256,320},{320,384},{384,448},... | collective-permute-start | bytes 442376 | tf_op jit(solution)/shard_map/ppermute | solution.py:35
  148.9 2.1 %collective-permute-start.3 = (bf16[3,48,512]{2,1,0:T(8,128)(2,1)S(1)}, bf16[3,48,512]{2,1,0:T(8,128)(2,1)S(1)}, u32[]{:S(2)}, u32[]{:S(2)}) collective-permute-start(bf16[3,48,512]{2,1,0:T(8,128)(2,1)S(1)} %get-tuple-element.6), channel_id=1, source_target_pairs={{64,0},{128,64},{192,128},{256,192},{320,256},{384,320},{448,384},... | collective-permute-start | bytes 442376 | tf_op jit(solution)/shard_map/ppermute | solution.py:35
  151.1 1.6 collective-permute-done.2
  152.7 7.7 %collective-permute-done.3 = bf16[3,48,512]{2,1,0:T(8,128)(2,1)S(1)} collective-permute-done((bf16[3,48,512]{2,1,0:T(8,128)(2,1)S(1)}, bf16[3,48,512]{2,1,0:T(8,128)(2,1)S(1)}, u32[]{:S(2)}, u32[]{:S(2)}) %collective-permute-start.3) | collective-permute-done | bytes 147488 | tf_op jit(solution)/shard_map/ppermute | solution.py:35
  160.4 1.2 pad_maximum_fusion
  161.6 2.2 %reshape.59 = bf16[3,6,4,12,512]{4,3,2,1,0:T(8,128)(2,1)} reshape(bf16[18,48,512]{2,1,0:T(8,128)(2,1)} %pad_maximum_fusion) | data formatting | bytes 1769472 | tf_op jit(solution)/shard_map/reshape | solution.py:352
  163.7 1.4 copy.34
  165.2 0.2 pad.8.clone
  165.3 0.8 copy-done.1
  166.1 0.3 copy-done.9
  166.4 21.8 %attention.1.first_ref = bf16[448,512]{1,0:T(8,128)(2,1)S(1)} custom-call(s32[1]{0:T(128)} %bitcast.core_ref, f32[8]{0:T(128)S(1)} %minimum_exponential_fusion.scale_ref, bf16[1152,512]{1,0:T(8,128)(2,1)S(1)} %bitcast.35, f32[3,8,96,128]{3,2,1,0:T(8,128)S(1)} %broadcast_select_fusion.bias_ref, bf16[448,512]{1,0:T(8,128)(2,1)S(1)} %bitcast.36, ...), custom_call_target="tpu_custom_call" | custom-call | flops 6000000000 | bytes 20000000 | tf_op jit(solution)/shard_map/attention/pallas_call | solution.py:382
  188.2 0.8 copy-done.10
  189.0 2.2 %copy-done.2 = bf16[256,32,256]{2,1,0:T(8,128)(2,1)S(1)} copy-done((bf16[256,32,256]{2,1,0:T(8,128)(2,1)S(1)}, bf16[256,32,256]{2,1,0:T(8,128)(2,1)}, u32[]{:S(2)}) %copy-start.2) | copy-done | bytes 4194328
  191.2 1.0 copy-done.11
  192.2 6.5 %feedforward.1 = bf16[6,18,1024]{2,1,0:T(8,128)(2,1)} custom-call(s32[1]{0:T(128)} %bitcast.core_ref, bf16[448,512]{1,0:T(8,128)(2,1)S(1)} %copy-done.11, f32[1,512]{1,0:T(1,128)S(1)} %bitcast.42, f32[1,512]{1,0:T(1,128)S(1)} %bitcast.43, f32[1,1024]{1,0:T(1,128)S(1)} %bitcast.38, f32[1,1024]{1,0:T(1,128)S(1)} %bitcast.39, ...), custom_call_target="tpu_custom_call" | custom-call | flops 3000000000 | bytes 20000000 | tf_op jit(solution)/shard_map/feedforward/pallas_call | solution.py:412
  (56 shorter events, 0.2 us)
Async XLA Ops:
  6.5 0.8 copy-start
  6.5 182.4 %all-gather.3.cloned.1.call-start = ((), (), s32[]{:S(2)}) async-start(), calls=%async_computation.4 | async-start | bytes 4456448 | tf_op jit(solution)/shard_map/all_gather | solution.py:340
  42.6 3.1 %collective-permute-start.4 = (bf16[8,4096]{1,0:T(8,128)(2,1)S(1)}, bf16[8,4096]{1,0:T(8,128)(2,1)S(1)}, u32[]{:S(2)}, u32[]{:S(2)}) collective-permute-start(bf16[8,4096]{1,0:T(8,128)(2,1)S(1)} %constant_dynamic-update-slice_fusion), channel_id=1, source_target_pairs={{0,1},{1,0},{2,3},{3,2},{4,5},{5,4},{6,7},{7,6},{8,9},{9,8},{10,11... | collective-permute-start | bytes 196616 | tf_op jit(solution)/shard_map/ppermute | solution.py:35
  70.7 35.0 %all-to-all-start.2 = ((bf16[16,2,16,16,128]{4,3,2,1,0:T(8,128)(2,1)}), bf16[16,2,16,16,128]{4,3,2,1,0:T(8,128)(2,1)S(1)}, u32[]{:S(2)}, u32[]{:S(2)}) async-start(bf16[16,2,16,16,128]{4,3,2,1,0:T(8,128)(2,1)} %broadcast_in_dim.67), calls=%async_computation.2 | async-start | bytes 4194304 | tf_op jit(solution)/shard_map/all_to_all | solution.py:40
  78.2 44.3 %copy-start.15 = (f32[2,512]{1,0:T(2,128)S(1)}, f32[2,512]{1,0:T(2,128)}, u32[]{:S(2)}) copy-start(f32[2,512]{1,0:T(2,128)} %param.28) | copy-start | bytes 12292
  78.2 46.2 %copy-start.17 = (f32[512,8]{0,1:T(8,128)S(1)}, f32[512,8]{0,1:T(8,128)}, u32[]{:S(2)}) copy-start(f32[512,8]{0,1:T(8,128)} %param.30) | copy-start | bytes 49156
  78.2 46.2 %copy-start.18 = (f32[512]{0:T(512)S(1)}, f32[512]{0:T(512)}, u32[]{:S(2)}) copy-start(f32[512]{0:T(512)} %param.29) | copy-start | bytes 6148
  78.2 46.2 %copy-start.21 = (f32[253]{0:T(256)S(1)}, f32[253]{0:T(256)}, u32[]{:S(2)}) copy-start(f32[253]{0:T(256)} %constant.81) | copy-start | bytes 3040
  78.2 46.2 %copy-start.22 = (f32[253]{0:T(256)S(1)}, f32[253]{0:T(256)}, u32[]{:S(2)}) copy-start(f32[253]{0:T(256)} %constant.83) | copy-start | bytes 3040
  106.9 18.3 %copy-start.14 = (pred[96,128]{1,0:T(32,128)(4,1)S(1)}, pred[96,128]{1,0:T(32,128)(4,1)}, u32[]{:S(2)}) copy-start(pred[96,128]{1,0:T(32,128)(4,1)} %constant.68.clone) | copy-start | bytes 36868
  106.9 24.5 %copy-start.20 = (s32[12288]{0:T(1024)S(1)}, s32[12288]{0:T(1024)}, u32[]{:S(2)}) copy-start(s32[12288]{0:T(1024)} %constant.66.clone) | copy-start | bytes 147460
  106.9 22.4 %all-to-all-start.1 = ((bf16[16,16,16,128]{3,2,1,0:T(8,128)(2,1)}), bf16[16,16,16,128]{3,2,1,0:T(8,128)(2,1)}, u32[]{:S(2)}, u32[]{:S(2)}) async-start(bf16[16,16,16,128]{3,2,1,0:T(8,128)(2,1)} %broadcast_in_dim.66), calls=%async_computation.1 | async-start | bytes 2097152 | tf_op jit(solution)/shard_map/all_to_all | solution.py:40
  116.0 27.8 %collective-permute-start = (bf16[12,6,512]{2,1,0:T(8,128)(2,1)}, bf16[12,6,512]{2,1,0:T(8,128)(2,1)S(1)}, u32[]{:S(2)}, u32[]{:S(2)}) collective-permute-start(bf16[12,6,512]{2,1,0:T(8,128)(2,1)} %get-tuple-element.7), channel_id=1, source_target_pairs={{0,1},{1,2},{2,3},{3,4},{4,5},{5,6},{6,7},{7,8},{8,9},{9,10},{10,1... | collective-permute-start | bytes 221192 | tf_op jit(solution)/shard_map/ppermute | solution.py:35
  117.9 25.9 %collective-permute-start.1 = (bf16[12,6,512]{2,1,0:T(8,128)(2,1)}, bf16[12,6,512]{2,1,0:T(8,128)(2,1)S(1)}, u32[]{:S(2)}, u32[]{:S(2)}) collective-permute-start(bf16[12,6,512]{2,1,0:T(8,128)(2,1)} %get-tuple-element.8), channel_id=1, source_target_pairs={{0,63},{1,0},{2,1},{3,2},{4,3},{5,4},{6,5},{7,6},{8,7},{9,8},{10,9... | collective-permute-start | bytes 221192 | tf_op jit(solution)/shard_map/ppermute | solution.py:35
  122.5 66.5 %collective-permute-start.6 = (bf16[16,2,16,16,128]{4,3,2,1,0:T(8,128)(2,1)S(1)}, bf16[16,2,16,16,128]{4,3,2,1,0:T(8,128)(2,1)}, u32[]{:S(2)}, u32[]{:S(2)}) collective-permute-start(bf16[16,2,16,16,128]{4,3,2,1,0:T(8,128)(2,1)S(1)} %all-to-all-done.2.mine_ref), channel_id=1, source_target_pairs={{0,1},{1,0},{2,3},{3,2},{4,5},{5,4},{6,7},{7,6},{8,9},{9,8},{10,11... | collective-permute-start | bytes 6291464 | tf_op jit(solution)/shard_map/ppermute | solution.py:35
  124.4 10.9 %copy-start.16 = (pred[128]{0:T(512)(128)(4,1)S(1)}, pred[128]{0:T(512)(128)(4,1)}, u32[]{:S(2)}) copy-start(pred[128]{0:T(512)(128)(4,1)} %constant.67.clone) | copy-start | bytes 388
  129.3 6.1 %copy-start.13 = (pred[3,96,128]{2,1,0:T(8,128)(4,1)S(1)}, pred[3,96,128]{2,1,0:T(8,128)(4,1)}, u32[]{:S(2)}) copy-start(pred[3,96,128]{2,1,0:T(8,128)(4,1)} %broadcast_and_fusion) | copy-start | bytes 110596
  129.3 36.0 %collective-permute-start.5 = (bf16[16,16,16,128]{3,2,1,0:T(8,128)(2,1)}, bf16[16,16,16,128]{3,2,1,0:T(8,128)(2,1)}, u32[]{:S(2)}, u32[]{:S(2)}) collective-permute-start(bf16[16,16,16,128]{3,2,1,0:T(8,128)(2,1)} %all-to-all-done.1.mine_ref), channel_id=1, source_target_pairs={{0,1},{1,0},{2,3},{3,2},{4,5},{5,4},{6,7},{7,6},{8,9},{9,8},{10,11... | collective-permute-start | bytes 3145736 | tf_op jit(solution)/shard_map/ppermute | solution.py:35
  139.8 11.2 %copy-start.19 = (f32[8]{0:T(128)S(1)}, f32[8]{0:T(128)}, u32[]{:S(2)}) copy-start(f32[8]{0:T(128)} %param.27) | copy-start | bytes 100
  141.8 2.0 copy-start.12
  143.9 8.8 %collective-permute-start.2 = (bf16[3,48,512]{2,1,0:T(8,128)(2,1)S(1)}, bf16[3,48,512]{2,1,0:T(8,128)(2,1)S(1)}, u32[]{:S(2)}, u32[]{:S(2)}) collective-permute-start(bf16[3,48,512]{2,1,0:T(8,128)(2,1)S(1)} %get-tuple-element.5), channel_id=1, source_target_pairs={{0,64},{64,128},{128,192},{192,256},{256,320},{320,384},{384,448},... | collective-permute-start | bytes 442376 | tf_op jit(solution)/shard_map/ppermute | solution.py:35
  148.9 11.5 %collective-permute-start.3 = (bf16[3,48,512]{2,1,0:T(8,128)(2,1)S(1)}, bf16[3,48,512]{2,1,0:T(8,128)(2,1)S(1)}, u32[]{:S(2)}, u32[]{:S(2)}) collective-permute-start(bf16[3,48,512]{2,1,0:T(8,128)(2,1)S(1)} %get-tuple-element.6), channel_id=1, source_target_pairs={{64,0},{128,64},{192,128},{256,192},{320,256},{384,320},{448,384},... | collective-permute-start | bytes 442376 | tf_op jit(solution)/shard_map/ppermute | solution.py:35
  165.1 1.0 copy-start.1
  165.1 1.0 copy-start.5
  165.1 1.0 copy-start.6
  165.1 1.2 copy-start.9
  166.4 22.6 %copy-start.3 = (f32[1024]{0:T(1024)S(1)}, f32[1024]{0:T(1024)}, u32[]{:S(2)}) copy-start(f32[1024]{0:T(1024)} %param.35) | copy-start | bytes 12292
  166.4 22.6 %copy-start.4 = (f32[1024]{0:T(1024)S(1)}, f32[1024]{0:T(1024)}, u32[]{:S(2)}) copy-start(f32[1024]{0:T(1024)} %param.36) | copy-start | bytes 12292
  166.4 22.6 %copy-start.7 = (f32[512]{0:T(512)S(1)}, f32[512]{0:T(512)}, u32[]{:S(2)}) copy-start(f32[512]{0:T(512)} %param.33) | copy-start | bytes 6148
  166.4 22.6 %copy-start.8 = (f32[512]{0:T(512)S(1)}, f32[512]{0:T(512)}, u32[]{:S(2)}) copy-start(f32[512]{0:T(512)} %param.34) | copy-start | bytes 6148
  188.2 0.8 copy-start.10
  189.0 2.2 %copy-start.2 = (bf16[256,32,256]{2,1,0:T(8,128)(2,1)S(1)}, bf16[256,32,256]{2,1,0:T(8,128)(2,1)}, u32[]{:S(2)}) copy-start(bf16[256,32,256]{2,1,0:T(8,128)(2,1)} %all-gather.3.cloned.1.call-done) | copy-start | bytes 12582916
  191.2 1.0 copy-start.11
Sparse Core Ops, SparseCore 0:
  40.6 39.2 all-gather.2

commit v2 on v1

--- a/solution.py
+++ b/solution.py
@@ -98,9 +98,10 @@
 def attention_kernel(
     core_ref,
     scale_ref,
-    windows_ref,
+    tall_ref,
     bias_ref,
-    patches_ref,
+    arrange_ref,
+    patch_select_ref,
     select_ref,
     gain_ref,
     offset_ref,
@@ -141,7 +142,6 @@
     low_half = lax.broadcasted_iota(jnp.int32, (WIN_PAD, 128), 1) < 64
     zero = jnp.zeros((WIN_PAD, 128), BF16)
     gap = jnp.zeros((KEY_PAD - WIN_PAD, 128), BF16)
-    half = WINS * WIN_PAD
 
     def columns(start, width):
         return weight[:, :, start : start + width].reshape(D, width)
@@ -153,7 +153,8 @@
 
     done = 0
     for band in range(BANDS):
-        tokens = windows_ref[band * half : (band + 1) * half, :]
+        strip = tall_ref[band * WIN_ROWS : (band + 1) * WIN_ROWS].reshape(WIN_ROWS * 48, D)
+        tokens = jnp.dot(arrange_ref[...], strip, preferred_element_type=F32).astype(BF16)
         for target, start in ((queries, 0), (keys, D)):
             total = jnp.dot(tokens, columns(start, D), preferred_element_type=F32)
             for i, part in enumerate(unit_norm(total, ones)):
@@ -193,7 +194,10 @@
     own = jnp.dot(select_ref[...], heads[...], preferred_element_type=F32).astype(BF16)
     projected = jnp.dot(own, columns(3 * D, D), preferred_element_type=F32)
     branch = norm_rows(projected, gain_ref[...], offset_ref[...]).astype(BF16)
-    out_ref[...] = (patches_ref[...].astype(F32) + branch.astype(F32)).astype(BF16)
+    patches = jnp.dot(
+        patch_select_ref[...], tall_ref[...].reshape(18 * 48, D), preferred_element_type=F32
+    )
+    out_ref[...] = (patches + branch.astype(F32)).astype(BF16)
 
 
 def feedforward_kernel(
@@ -222,7 +226,7 @@
             column = pl.multiple_of((m // 2 * 2 + of) * 128, 128)
             ups.append(
                 pltpu.make_async_copy(
-                    ref.at[m, 0],
+                    ref.at[m, :, pl.ds(0, 16), :],
                     up.at[:, pl.ds(y_lo * 16, 16), pl.ds(column, 128)],
                     up_sems.at[m * 2 + part],
                 )
@@ -230,19 +234,22 @@
             start = pl.multiple_of(y_lo * 64 + of * 32 + y_hi * 16, 16)
             downs.append(
                 pltpu.make_async_copy(
-                    ref.at[m, 1],
+                    ref.at[m, :, pl.ds(16, 16), :],
                     down.at[:, pl.ds(start, 16), pl.ds(x * 128, 128)],
                     down_sems.at[m * 2 + part],
                 )
             )
         x, y_lo, of = m // 4, m // 2 % 2, m % 2
-        merges.append(
-            pltpu.make_async_copy(
-                merge_ref.at[m],
-                merge.at[:, pl.ds(y_lo * 64 + of * 32, 32), pl.ds(x * 256, 256)],
-                merge_sems.at[m],
+        for part in range(2):
+            merges.append(
+                pltpu.make_async_copy(
+                    merge_ref.at[m, :, pl.ds(part * 32, 32), :],
+                    merge.at[
+                        :, pl.ds(y_lo * 64 + of * 32, 32), pl.ds(x * 256 + part * 128, 128)
+                    ],
+                    merge_sems.at[m * 2 + part],
+                )
             )
-        )
     for copy in ups + downs + merges:
         copy.start()
     for copy in ups:
@@ -277,6 +284,15 @@
         out_ref[i] = reduced[i * 18 : i * 18 + 18].astype(BF16)
 
 
+def quads_order(place):
+    order = place.reshape(6, 2, 18, 2).transpose(3, 1, 0, 2).reshape(4, 108)
+    return np.pad(order, ((0, 0), (0, QUAD_ROWS - 108)), constant_values=-1).reshape(-1)
+
+
+def one_hot_rows(order, size):
+    return (order[:, None] == np.arange(size)[None]).astype(np.float32)
+
+
 def selection():
     place = np.full((12, 36), -1)
     done = 0
@@ -290,9 +306,18 @@
                 if b < WIN_COLS and 0 <= j < 36:
                     place[i, j] = done + r
             done += count
-    order = place.reshape(6, 2, 18, 2).transpose(3, 1, 0, 2).reshape(4, 108)
-    order = np.pad(order, ((0, 0), (0, QUAD_ROWS - 108)), constant_values=-1).reshape(-1)
-    return (order[:, None] == np.arange(done)[None]).astype(np.float32)
+    return one_hot_rows(quads_order(place), done)
+
+
+def patch_selection():
+    i, j = np.arange(12)[:, None] + SHIFT_ROWS, np.arange(36)[None] + SHIFT_COLS
+    return one_hot_rows(quads_order(i * 48 + j), 18 * 48)
+
+
+def arrangement():
+    r = np.arange(WINS * WIN_PAD)
+    w, a, b = r // WIN_PAD, r % WIN_PAD // PAD_COLS, r % PAD_COLS
+    return one_hot_rows(np.where(b < WIN_COLS, a * 48 + w * WIN_COLS + b, -1), WIN_ROWS * 48)
 
 
 def local(
@@ -325,35 +350,29 @@
         [jnp.where(core == 0, mine, theirs), jnp.where(core == 0, theirs, mine)], axis=0
     )
     at = (lat * 2 + core) * 128
-    units = jnp.stack(
+    units = jnp.concatenate(
         [
             lax.dynamic_slice(rows, (0, at), (16, 128)),
             lax.dynamic_slice(rows, (0, 2048 + at), (16, 128)),
             lax.dynamic_slice(
                 feedforward_out_weight, (lax.axis_index("y_hi") * 16, x * 128), (16, 128)
             ),
+            lax.dynamic_slice(merging_reduction_weight, (0, x * 256), (32, 128)),
+            lax.dynamic_slice(merging_reduction_weight, (0, x * 256 + 128), (32, 128)),
         ]
     )
+    units, patches = lax.optimization_barrier((units, patches))
     along_z = spread(units, "z")
-    merge_part = lax.dynamic_slice(merging_reduction_weight, (0, x * 256), (32, 256))
-    merge_z = spread(merge_part, "z")
-    merge_all = lax.all_gather(merge_z, ("x", "y_lo", "core"), axis=0)
-    attn_mine = spread(along_z[:, 0], PLANE)
-    attn_other = shifted(attn_mine, "core", 1, True)
-    ffn_mine = spread(along_z[:, 1:].transpose(1, 0, 2, 3), PLANE)
-    ffn_other = shifted(ffn_mine, "core", 1, True)
-
     east = shifted(patches[:, :SHIFT_COLS], LON, -1, True)
     west = shifted(patches[:, 36 - SHIFT_COLS :], LON, 1, True)
     wide = jnp.concatenate([west, patches, east], axis=1)
     south = shifted(wide[:SHIFT_ROWS], LAT, -1, False)
     north = shifted(wide[12 - SHIFT_ROWS :], LAT, 1, False)
     tall = jnp.concatenate([north, wide, south], axis=0)
-    windows = tall.reshape(BANDS, WIN_ROWS, WINS, WIN_COLS, D).transpose(0, 2, 1, 3, 4)
-    windows = jnp.pad(windows, ((0, 0), (0, 0), (0, 0), (0, PAD_COLS - WIN_COLS), (0, 0)))
-    windows = windows.reshape(BANDS * WINS * WIN_PAD, D)
-    ordered = patches.reshape(6, 2, 18, 2, D).transpose(3, 1, 0, 2, 4).reshape(4, 108, D)
-    ordered = jnp.pad(ordered, ((0, 0), (0, QUAD_ROWS - 108), (0, 0))).reshape(4 * QUAD_ROWS, D)
+
+    along_z, tall = lax.optimization_barrier((along_z, tall))
+    merge_all = lax.all_gather(along_z[:, 48:], ("x", "y_lo", "core"), axis=0)
+    attn_mine = spread(along_z[:, :16], PLANE)
 
     table = bias_entries(
         bias_network_first_weight, bias_network_first_bias, bias_network_second_weight
@@ -374,15 +393,19 @@
     bias = jnp.where(seam[:, None, None, None] & jnp.asarray(apart), OFF, bias[None])
     head_scale = jnp.exp(jnp.minimum(head_scale_logarithm, jnp.log(100.0)))
 
+    attn_mine, ffn_z, bias = lax.optimization_barrier((attn_mine, along_z[:, 16:48], bias))
+    attn_other = shifted(attn_mine, "core", 1, True)
+    ffn_mine = spread(ffn_z, PLANE)
+
     vmem = pl.BlockSpec(memory_space=pltpu.VMEM)
     smem = pl.BlockSpec(memory_space=pltpu.SMEM)
-    anywhere = pl.BlockSpec(memory_space=pl.ANY)
+    anywhere = pl.BlockSpec(memory_space=pltpu.HBM)
     core_index = core.astype(jnp.int32).reshape(1)
     half = WINS * WIN_PAD
     first = pl.pallas_call(
         attention_kernel,
         out_shape=jax.ShapeDtypeStruct((4 * QUAD_ROWS, D), BF16),
-        in_specs=[smem, smem] + [vmem] * 6 + [anywhere] * 2,
+        in_specs=[smem, smem] + [vmem] * 7 + [anywhere] * 2,
         out_specs=vmem,
         scratch_shapes=[
             pltpu.VMEM((16, 32, 2048), BF16),
@@ -392,23 +415,26 @@
             pltpu.VMEM((768, D), BF16),
             pltpu.SemaphoreType.DMA((32,)),
         ],
-        compiler_params=pltpu.CompilerParams(vmem_limit_bytes=40 * 1024 * 1024),
+        compiler_params=pltpu.CompilerParams(vmem_limit_bytes=24 * 1024 * 1024),
         cost_estimate=pl.CostEstimate(
-            flops=6_000_000_000, bytes_accessed=20_000_000, transcendentals=1_000_000
+            flops=20_000_000_000, bytes_accessed=20_000_000, transcendentals=1_000_000
         ),
         name="attention",
     )(
         core_index,
         head_scale,
-        windows,
+        tall,
         bias,
-        ordered,
+        jnp.asarray(arrangement(), BF16),
+        jnp.asarray(patch_selection(), BF16),
         jnp.asarray(selection(), BF16),
         attention_norm_gain.reshape(1, D),
         attention_norm_offset.reshape(1, D),
         attn_mine,
         attn_other,
     )
+    first, ffn_mine = lax.optimization_barrier((first, ffn_mine))
+    ffn_other = shifted(ffn_mine, "core", 1, True)
     return pl.pallas_call(
         feedforward_kernel,
         out_shape=jax.ShapeDtypeStruct((6, 18, 2 * D), BF16),
@@ -420,9 +446,9 @@
             pltpu.VMEM((16, 128, 2 * D), BF16),
             pltpu.SemaphoreType.DMA((32,)),
             pltpu.SemaphoreType.DMA((32,)),
-            pltpu.SemaphoreType.DMA((16,)),
+            pltpu.SemaphoreType.DMA((32,)),
         ],
-        compiler_params=pltpu.CompilerParams(vmem_limit_bytes=40 * 1024 * 1024),
+        compiler_params=pltpu.CompilerParams(vmem_limit_bytes=24 * 1024 * 1024),
         cost_estimate=pl.CostEstimate(
             flops=3_000_000_000, bytes_accessed=20_000_000, transcendentals=1_000_000
         ),
@@ -436,7 +462,7 @@
         merging_norm_offset.reshape(1, 2 * D),
         ffn_mine,
         ffn_other,
-        merge_all.reshape(16, 16, 32, 256),
+        merge_all,
     )
 
 

time: 207 us -> 168 us (0.81)
  the two profiles are of different devices: /device:TPU:38 before, /device:TPU:1 now
where the time goes in v2:
time: 168 us; the launch traced here: 167 us
  starting transfers between devices  65.1 us (39%)
  waiting for transfers between devices  31.1 us (19%)
  Pallas kernels  30.3 us (18%)
  local copies, waits for them, and re-layouts  20.4 us (12%)
  between operations  13.8 us (8%)
  matrix products  4.62 us (3%)
  other arithmetic  1.71 us (1%)
    all_to_all x3, starting transfers between devices, spread(): lax.all_to_all(jnp.broadcast_to(block[None], (size,) + block.shape), axes...  37.5 us
    ppermute x7, starting transfers between devices, shifted(): return lax.ppermute(block, axes, pairs)  27.6 us
    pallas_call x1, Pallas kernels, local(): pl.pallas_call(attention_kernel, out_shape=jax.ShapeDtypeStruct((4 * QUAD...  22.7 us
    all_to_all x3, waiting for transfers between devices, spread(): lax.all_to_all(jnp.broadcast_to(block[None], (size,) + block.shape), axes...  17.6 us
    unnamed x54, local copies, waits for them, and re-layouts  14.3 us
    ppermute x7, waiting for transfers between devices, shifted(): return lax.ppermute(block, axes, pairs)  13.5 us
    pallas_call x1, Pallas kernels, local(): pl.pallas_call(feedforward_kernel, out_shape=jax.ShapeDtypeStruct((6, 18,...  7.66 us
    dot_general x1, matrix products, local(): bias = jnp.dot(table, one_hot, precision=lax.Precision.HIGHEST)  3.96 us
  transfers between devices with their start and end apart: 11, of which 8 were waited for; matrix products, arithmetic and copies ran while one was open for 6% of the time, Pallas kernels for 14%

profile of v2, /device:TPU:1, one launch (start us, length us, event | category | flops | bytes accessed | tf_op | source)
XLA Modules:
  0.0 167.2 jit_solution(4461177653640672696)
XLA Ops:
  6.5 0.8 constant_dynamic-update-slice_fusion.2
  7.3 0.7 constant_dynamic-update-slice_fusion.1
  8.0 0.8 constant_dynamic-update-slice_fusion
  8.8 8.8 %collective-permute-start = (bf16[8,4096]{1,0:T(8,128)(2,1)S(1)}, bf16[8,4096]{1,0:T(8,128)(2,1)S(1)}, u32[]{:S(2)}, u32[]{:S(2)}) collective-permute-start(bf16[8,4096]{1,0:T(8,128)(2,1)S(1)} %constant_dynamic-update-slice_fusion), channel_id=1, source_target_pairs={{0,1},{1,0},{2,3},{3,2},{4,5},{5,4},{6,7},{7,6},{8,9},{9,8},{10,11... | collective-permute-start | bytes 196616 | tf_op jit(solution)/shard_map/ppermute | solution.py:35
  17.6 0.9 collective-permute-done
  18.5 0.7 constant_dynamic-update-slice_fusion.5
  19.2 0.7 constant_dynamic-update-slice_fusion.4
  19.9 0.7 constant_dynamic-update-slice_fusion.3
  20.6 0.8 broadcast_in_dim.34
  21.4 9.5 %all-to-all-start = ((bf16[16,112,128]{2,1,0:T(8,128)(2,1)}), bf16[16,112,128]{2,1,0:T(8,128)(2,1)S(1)}, u32[]{:S(2)}, u32[]{:S(2)}) async-start(bf16[16,112,128]{2,1,0:T(8,128)(2,1)} %broadcast_in_dim.34), calls=%async_computation | async-start | bytes 917504 | tf_op jit(solution)/shard_map/all_to_all | solution.py:40
  31.0 0.0 all-gather.3.cloned.1.call-start
  31.1 3.7 %collective-permute-start.1 = (bf16[12,6,512]{2,1,0:T(8,128)(2,1)S(1)}, bf16[12,6,512]{2,1,0:T(8,128)(2,1)S(1)}, u32[]{:S(2)}, u32[]{:S(2)}) collective-permute-start(bf16[12,6,512]{2,1,0:T(8,128)(2,1)S(1)} %get-tuple-element.25), channel_id=1, source_target_pairs={{0,1},{1,2},{2,3},{3,4},{4,5},{5,6},{6,7},{7,8},{8,9},{9,10},{10,1... | collective-permute-start | bytes 221192 | tf_op jit(solution)/shard_map/ppermute | solution.py:35
  34.9 2.1 %collective-permute-start.2 = (bf16[12,6,512]{2,1,0:T(8,128)(2,1)S(1)}, bf16[12,6,512]{2,1,0:T(8,128)(2,1)S(1)}, u32[]{:S(2)}, u32[]{:S(2)}) collective-permute-start(bf16[12,6,512]{2,1,0:T(8,128)(2,1)S(1)} %get-tuple-element.26), channel_id=1, source_target_pairs={{0,63},{1,0},{2,1},{3,2},{4,3},{5,4},{6,5},{7,6},{8,7},{9,8},{10,9... | collective-permute-start | bytes 221192 | tf_op jit(solution)/shard_map/ppermute | solution.py:35
  36.9 4.0 %collective-permute-done.2 = bf16[12,6,512]{2,1,0:T(8,128)(2,1)S(1)} collective-permute-done((bf16[12,6,512]{2,1,0:T(8,128)(2,1)S(1)}, bf16[12,6,512]{2,1,0:T(8,128)(2,1)S(1)}, u32[]{:S(2)}, u32[]{:S(2)}) %collective-permute-start.2) | collective-permute-done | bytes 73760 | tf_op jit(solution)/shard_map/ppermute | solution.py:35
  40.9 0.1 pad_maximum_fusion.3
  41.0 3.1 %collective-permute-start.3 = (bf16[3,48,512]{2,1,0:T(8,128)(2,1)S(1)}, bf16[3,48,512]{2,1,0:T(8,128)(2,1)S(1)}, u32[]{:S(2)}, u32[]{:S(2)}) collective-permute-start(bf16[3,48,512]{2,1,0:T(8,128)(2,1)S(1)} %get-tuple-element.23), channel_id=1, source_target_pairs={{0,64},{64,128},{128,192},{192,256},{256,320},{320,384},{384,448},... | collective-permute-start | bytes 442376 | tf_op jit(solution)/shard_map/ppermute | solution.py:35
  44.2 1.3 collective-permute-start.4
  45.5 0.8 collective-permute-done.3
  46.3 4.1 %collective-permute-done.4 = bf16[3,48,512]{2,1,0:T(8,128)(2,1)S(1)} collective-permute-done((bf16[3,48,512]{2,1,0:T(8,128)(2,1)S(1)}, bf16[3,48,512]{2,1,0:T(8,128)(2,1)S(1)}, u32[]{:S(2)}, u32[]{:S(2)}) %collective-permute-start.4) | collective-permute-done | bytes 147488 | tf_op jit(solution)/shard_map/ppermute | solution.py:35
  50.4 1.2 pad_maximum_fusion.tall_ref
  51.5 0.2 all-to-all-done
  51.7 0.7 slice.43
  52.5 0.7 fusion.6
  53.2 1.2 broadcast_in_dim.35
  54.4 22.4 %all-to-all-start.1 = ((bf16[16,16,16,128]{3,2,1,0:T(8,128)(2,1)}), bf16[16,16,16,128]{3,2,1,0:T(8,128)(2,1)}, u32[]{:S(2)}, u32[]{:S(2)}) async-start(bf16[16,16,16,128]{3,2,1,0:T(8,128)(2,1)} %broadcast_in_dim.35), calls=%async_computation.1 | async-start | bytes 2097152 | tf_op jit(solution)/shard_map/all_to_all | solution.py:40
  76.9 0.1 pad_add_fusion
  77.0 4.0 %fusion.2 = f32[8,96,128]{2,0,1:T(8,128)S(1)} fusion(f32[253,8]{0,1:T(8,128)S(1)} %fusion.6, s32[12288]{0:T(1024)S(1)} %copy-done.22), kind=kOutput, calls=%fused_computation.3 | convolution fusion | flops 301559808 | bytes 450464 | tf_op jit(solution)/shard_map/dot_general | solution.py:386
  80.9 0.1 broadcast_and_fusion
  81.0 0.1 copy_select_fusion
  81.1 0.1 broadcast_select_fusion.bias_ref
  81.3 10.3 %all-to-all-done.1.mine_ref = bf16[16,16,16,128]{3,2,1,0:T(8,128)(2,1)} async-done(((bf16[16,16,16,128]{3,2,1,0:T(8,128)(2,1)}), bf16[16,16,16,128]{3,2,1,0:T(8,128)(2,1)}, u32[]{:S(2)}, u32[]{:S(2)}) %all-to-all-start.1) | async-done | bytes 1048608 | tf_op jit(solution)/shard_map/all_to_all | solution.py:40
  91.5 5.9 %collective-permute-start.5 = (bf16[16,16,16,128]{3,2,1,0:T(8,128)(2,1)}, bf16[16,16,16,128]{3,2,1,0:T(8,128)(2,1)}, u32[]{:S(2)}, u32[]{:S(2)}) collective-permute-start(bf16[16,16,16,128]{3,2,1,0:T(8,128)(2,1)} %all-to-all-done.1.mine_ref), channel_id=1, source_target_pairs={{0,1},{1,0},{2,3},{3,2},{4,5},{5,4},{6,7},{7,6},{8,9},{9,8},{10,11... | collective-permute-start | bytes 3145736 | tf_op jit(solution)/shard_map/ppermute | solution.py:35
  97.4 1.8 %broadcast_in_dim.59 = bf16[16,16,32,128]{3,2,1,0:T(8,128)(2,1)} broadcast(bf16[16,32,128]{2,1,0:T(8,128)(2,1)S(1)} %slice.38), dimensions={1,2,3} | broadcast | bytes 2228224 | tf_op jit(solution)/shard_map/broadcast_in_dim | solution.py:40
  99.2 5.6 %all-to-all-start.2 = ((bf16[16,16,32,128]{3,2,1,0:T(8,128)(2,1)}), bf16[16,16,32,128]{3,2,1,0:T(8,128)(2,1)S(1)}, u32[]{:S(2)}, u32[]{:S(2)}) async-start(bf16[16,16,32,128]{3,2,1,0:T(8,128)(2,1)} %broadcast_in_dim.59), calls=%async_computation.2 | async-start | bytes 4194304 | tf_op jit(solution)/shard_map/all_to_all | solution.py:40
  104.9 1.2 copy-done.1
  106.0 1.2 copy-done.11
  107.2 1.1 copy-done.12
  108.3 1.0 copy-done.13
  109.3 22.7 %attention.1.first_ref = bf16[448,512]{1,0:T(8,128)(2,1)S(1)} custom-call(s32[1]{0:T(128)} %bitcast.core_ref, f32[8]{0:T(128)S(1)} %minimum_exponential_fusion.scale_ref, bf16[18,48,512]{2,1,0:T(8,128)(2,1)S(1)} %copy-done.1, f32[3,8,96,128]{3,2,1,0:T(8,128)S(1)} %broadcast_select_fusion.bias_ref, bf16[384,288]{1,0:T(8,128)(2,1)S(1)} %copy-done.13, ...), custom_call_target="tpu_custom_call" | custom-call | flops 20000000000 | bytes 20000000 | tf_op jit(solution)/shard_map/attention/pallas_call | solution.py:405
  132.0 0.8 copy-done.14
  132.7 7.2 %all-to-all-done.2.mine_ref = bf16[16,16,32,128]{3,2,1,0:T(8,128)(2,1)S(1)} async-done(((bf16[16,16,32,128]{3,2,1,0:T(8,128)(2,1)}), bf16[16,16,32,128]{3,2,1,0:T(8,128)(2,1)S(1)}, u32[]{:S(2)}, u32[]{:S(2)}) %all-to-all-start.2) | async-done | bytes 2097184 | tf_op jit(solution)/shard_map/all_to_all | solution.py:40
  139.9 2.7 %collective-permute-start.6 = (bf16[16,16,32,128]{3,2,1,0:T(8,128)(2,1)S(1)}, bf16[16,16,32,128]{3,2,1,0:T(8,128)(2,1)S(1)}, u32[]{:S(2)}, u32[]{:S(2)}) collective-permute-start(bf16[16,16,32,128]{3,2,1,0:T(8,128)(2,1)S(1)} %all-to-all-done.2.mine_ref), channel_id=1, source_target_pairs={{0,1},{1,0},{2,3},{3,2},{4,5},{5,4},{6,7},{7,6},{8,9},{9,8},{10,11... | collective-permute-start | bytes 6291464 | tf_op jit(solution)/shard_map/ppermute | solution.py:35
  142.7 3.8 %collective-permute-done.6.other_ref = bf16[16,16,32,128]{3,2,1,0:T(8,128)(2,1)S(1)} collective-permute-done((bf16[16,16,32,128]{3,2,1,0:T(8,128)(2,1)S(1)}, bf16[16,16,32,128]{3,2,1,0:T(8,128)(2,1)S(1)}, u32[]{:S(2)}, u32[]{:S(2)}) %collective-permute-start.6) | collective-permute-done | bytes 2097184 | tf_op jit(solution)/shard_map/ppermute | solution.py:35
  146.4 1.4 copy-done.3
  147.8 2.2 %copy-done.2 = bf16[256,64,128]{2,1,0:T(8,128)(2,1)S(1)} copy-done((bf16[256,64,128]{2,1,0:T(8,128)(2,1)S(1)}, bf16[256,64,128]{2,1,0:T(8,128)(2,1)}, u32[]{:S(2)}) %copy-start.2) | copy-done | bytes 4194328
  150.0 1.6 copy-done.4
  151.6 1.0 copy-done.15
  152.6 7.7 %feedforward.1 = bf16[6,18,1024]{2,1,0:T(8,128)(2,1)} custom-call(s32[1]{0:T(128)} %bitcast.core_ref, bf16[448,512]{1,0:T(8,128)(2,1)S(1)} %copy-done.15, f32[1,512]{1,0:T(1,128)S(1)} %bitcast.22, f32[1,512]{1,0:T(1,128)S(1)} %bitcast.23, f32[1,1024]{1,0:T(1,128)S(1)} %bitcast.18, f32[1,1024]{1,0:T(1,128)S(1)} %bitcast.19, ...), custom_call_target="tpu_custom_call" | custom-call | flops 3000000000 | bytes 20000000 | tf_op jit(solution)/shard_map/feedforward/pallas_call | solution.py:438
  (53 shorter events, 0.2 us)
Async XLA Ops:
  6.5 46.0 %copy-start = (f32[512,8]{0,1:T(8,128)S(1)}, f32[512,8]{0,1:T(8,128)}, u32[]{:S(2)}) copy-start(f32[512,8]{0,1:T(8,128)} %param.32) | copy-start | bytes 49156
  6.5 24.5 %copy-start.16 = (bf16[12,36,512]{2,1,0:T(8,128)(2,1)S(1)}, bf16[12,36,512]{2,1,0:T(8,128)(2,1)}, u32[]{:S(2)}) copy-start(bf16[12,36,512]{2,1,0:T(8,128)(2,1)} %param.23) | copy-start | bytes 1327108
  8.8 9.7 %collective-permute-start = (bf16[8,4096]{1,0:T(8,128)(2,1)S(1)}, bf16[8,4096]{1,0:T(8,128)(2,1)S(1)}, u32[]{:S(2)}, u32[]{:S(2)}) collective-permute-start(bf16[8,4096]{1,0:T(8,128)(2,1)S(1)} %constant_dynamic-update-slice_fusion), channel_id=1, source_target_pairs={{0,1},{1,0},{2,3},{3,2},{4,5},{5,4},{6,7},{7,6},{8,9},{9,8},{10,11... | collective-permute-start | bytes 196616 | tf_op jit(solution)/shard_map/ppermute | solution.py:35
  21.4 30.2 %all-to-all-start = ((bf16[16,112,128]{2,1,0:T(8,128)(2,1)}), bf16[16,112,128]{2,1,0:T(8,128)(2,1)S(1)}, u32[]{:S(2)}, u32[]{:S(2)}) async-start(bf16[16,112,128]{2,1,0:T(8,128)(2,1)} %broadcast_in_dim.34), calls=%async_computation | async-start | bytes 917504 | tf_op jit(solution)/shard_map/all_to_all | solution.py:40
  31.0 116.8 %all-gather.3.cloned.1.call-start = ((), (), s32[]{:S(2)}) async-start(), calls=%async_computation.3 | async-start | bytes 4456448 | tf_op jit(solution)/shard_map/all_gather | solution.py:374
  31.1 5.8 %collective-permute-start.1 = (bf16[12,6,512]{2,1,0:T(8,128)(2,1)S(1)}, bf16[12,6,512]{2,1,0:T(8,128)(2,1)S(1)}, u32[]{:S(2)}, u32[]{:S(2)}) collective-permute-start(bf16[12,6,512]{2,1,0:T(8,128)(2,1)S(1)} %get-tuple-element.25), channel_id=1, source_target_pairs={{0,1},{1,2},{2,3},{3,4},{4,5},{5,6},{6,7},{7,8},{8,9},{9,10},{10,1... | collective-permute-start | bytes 221192 | tf_op jit(solution)/shard_map/ppermute | solution.py:35
  34.8 17.6 %copy-start.18 = (f32[2,512]{1,0:T(2,128)S(1)}, f32[2,512]{1,0:T(2,128)}, u32[]{:S(2)}) copy-start(f32[2,512]{1,0:T(2,128)} %param.30) | copy-start | bytes 12292
  34.8 17.7 %copy-start.20 = (f32[512]{0:T(512)S(1)}, f32[512]{0:T(512)}, u32[]{:S(2)}) copy-start(f32[512]{0:T(512)} %param.31) | copy-start | bytes 6148
  34.9 17.7 %copy-start.23 = (f32[253]{0:T(256)S(1)}, f32[253]{0:T(256)}, u32[]{:S(2)}) copy-start(f32[253]{0:T(256)} %constant.85) | copy-start | bytes 3040
  34.9 17.6 %copy-start.24 = (f32[253]{0:T(256)S(1)}, f32[253]{0:T(256)}, u32[]{:S(2)}) copy-start(f32[253]{0:T(256)} %constant.83) | copy-start | bytes 3040
  34.9 6.1 %collective-permute-start.2 = (bf16[12,6,512]{2,1,0:T(8,128)(2,1)S(1)}, bf16[12,6,512]{2,1,0:T(8,128)(2,1)S(1)}, u32[]{:S(2)}, u32[]{:S(2)}) collective-permute-start(bf16[12,6,512]{2,1,0:T(8,128)(2,1)S(1)} %get-tuple-element.26), channel_id=1, source_target_pairs={{0,63},{1,0},{2,1},{3,2},{4,3},{5,4},{6,5},{7,6},{8,7},{9,8},{10,9... | collective-permute-start | bytes 221192 | tf_op jit(solution)/shard_map/ppermute | solution.py:35
  41.0 5.2 %collective-permute-start.3 = (bf16[3,48,512]{2,1,0:T(8,128)(2,1)S(1)}, bf16[3,48,512]{2,1,0:T(8,128)(2,1)S(1)}, u32[]{:S(2)}, u32[]{:S(2)}) collective-permute-start(bf16[3,48,512]{2,1,0:T(8,128)(2,1)S(1)} %get-tuple-element.23), channel_id=1, source_target_pairs={{0,64},{64,128},{128,192},{192,256},{256,320},{320,384},{384,448},... | collective-permute-start | bytes 442376 | tf_op jit(solution)/shard_map/ppermute | solution.py:35
  44.2 6.2 %collective-permute-start.4 = (bf16[3,48,512]{2,1,0:T(8,128)(2,1)S(1)}, bf16[3,48,512]{2,1,0:T(8,128)(2,1)S(1)}, u32[]{:S(2)}, u32[]{:S(2)}) collective-permute-start(bf16[3,48,512]{2,1,0:T(8,128)(2,1)S(1)} %get-tuple-element.24), channel_id=1, source_target_pairs={{64,0},{128,64},{192,128},{256,192},{320,256},{384,320},{448,384},... | collective-permute-start | bytes 442376 | tf_op jit(solution)/shard_map/ppermute | solution.py:35
  53.2 23.8 %copy-start.22 = (s32[12288]{0:T(1024)S(1)}, s32[12288]{0:T(1024)}, u32[]{:S(2)}) copy-start(s32[12288]{0:T(1024)} %constant.70.clone) | copy-start | bytes 147460
  54.4 37.1 %all-to-all-start.1 = ((bf16[16,16,16,128]{3,2,1,0:T(8,128)(2,1)}), bf16[16,16,16,128]{3,2,1,0:T(8,128)(2,1)}, u32[]{:S(2)}, u32[]{:S(2)}) async-start(bf16[16,16,16,128]{3,2,1,0:T(8,128)(2,1)} %broadcast_in_dim.35), calls=%async_computation.1 | async-start | bytes 2097152 | tf_op jit(solution)/shard_map/all_to_all | solution.py:40
  76.9 4.1 %copy-start.17 = (pred[96,128]{1,0:T(32,128)(4,1)S(1)}, pred[96,128]{1,0:T(32,128)(4,1)}, u32[]{:S(2)}) copy-start(pred[96,128]{1,0:T(32,128)(4,1)} %constant.72.clone) | copy-start | bytes 36868
  76.9 4.2 %copy-start.19 = (pred[128]{0:T(512)(128)(4,1)S(1)}, pred[128]{0:T(512)(128)(4,1)}, u32[]{:S(2)}) copy-start(pred[128]{0:T(512)(128)(4,1)} %constant.71.clone) | copy-start | bytes 388
  91.5 13.3 %collective-permute-start.5 = (bf16[16,16,16,128]{3,2,1,0:T(8,128)(2,1)}, bf16[16,16,16,128]{3,2,1,0:T(8,128)(2,1)}, u32[]{:S(2)}, u32[]{:S(2)}) collective-permute-start(bf16[16,16,16,128]{3,2,1,0:T(8,128)(2,1)} %all-to-all-done.1.mine_ref), channel_id=1, source_target_pairs={{0,1},{1,0},{2,3},{3,2},{4,5},{5,4},{6,7},{7,6},{8,9},{9,8},{10,11... | collective-permute-start | bytes 3145736 | tf_op jit(solution)/shard_map/ppermute | solution.py:35
  99.2 5.6 %copy-start.21 = (f32[8]{0:T(128)S(1)}, f32[8]{0:T(128)}, u32[]{:S(2)}) copy-start(f32[8]{0:T(128)} %param.29) | copy-start | bytes 100
  99.2 5.6 %copy-start.7 = (f32[512]{0:T(512)S(1)}, f32[512]{0:T(512)}, u32[]{:S(2)}) copy-start(f32[512]{0:T(512)} %param.33) | copy-start | bytes 6148
  99.2 5.6 %copy-start.8 = (f32[512]{0:T(512)S(1)}, f32[512]{0:T(512)}, u32[]{:S(2)}) copy-start(f32[512]{0:T(512)} %param.34) | copy-start | bytes 6148
  99.2 40.7 %all-to-all-start.2 = ((bf16[16,16,32,128]{3,2,1,0:T(8,128)(2,1)}), bf16[16,16,32,128]{3,2,1,0:T(8,128)(2,1)S(1)}, u32[]{:S(2)}, u32[]{:S(2)}) async-start(bf16[16,16,32,128]{3,2,1,0:T(8,128)(2,1)} %broadcast_in_dim.59), calls=%async_computation.2 | async-start | bytes 4194304 | tf_op jit(solution)/shard_map/all_to_all | solution.py:40
  104.8 1.2 copy-start.1
  106.0 1.2 copy-start.11
  107.2 1.1 copy-start.12
  108.3 1.0 copy-start.13
  109.3 38.6 %copy-start.5 = (f32[1024]{0:T(1024)S(1)}, f32[1024]{0:T(1024)}, u32[]{:S(2)}) copy-start(f32[1024]{0:T(1024)} %param.37) | copy-start | bytes 12292
  109.3 38.6 %copy-start.6 = (f32[1024]{0:T(1024)S(1)}, f32[1024]{0:T(1024)}, u32[]{:S(2)}) copy-start(f32[1024]{0:T(1024)} %param.38) | copy-start | bytes 12292
  109.3 38.6 %copy-start.9 = (f32[512]{0:T(512)S(1)}, f32[512]{0:T(512)}, u32[]{:S(2)}) copy-start(f32[512]{0:T(512)} %param.35) | copy-start | bytes 6148
  109.3 38.6 %copy-start.10 = (f32[512]{0:T(512)S(1)}, f32[512]{0:T(512)}, u32[]{:S(2)}) copy-start(f32[512]{0:T(512)} %param.36) | copy-start | bytes 6148
  132.0 0.8 copy-start.14
  139.9 6.5 %collective-permute-start.6 = (bf16[16,16,32,128]{3,2,1,0:T(8,128)(2,1)S(1)}, bf16[16,16,32,128]{3,2,1,0:T(8,128)(2,1)S(1)}, u32[]{:S(2)}, u32[]{:S(2)}) collective-permute-start(bf16[16,16,32,128]{3,2,1,0:T(8,128)(2,1)S(1)} %all-to-all-done.2.mine_ref), channel_id=1, source_target_pairs={{0,1},{1,0},{2,3},{3,2},{4,5},{5,4},{6,7},{7,6},{8,9},{9,8},{10,11... | collective-permute-start | bytes 6291464 | tf_op jit(solution)/shard_map/ppermute | solution.py:35
  146.4 1.4 copy-start.3
  147.8 2.2 %copy-start.2 = (bf16[256,64,128]{2,1,0:T(8,128)(2,1)S(1)}, bf16[256,64,128]{2,1,0:T(8,128)(2,1)}, u32[]{:S(2)}) copy-start(bf16[256,64,128]{2,1,0:T(8,128)(2,1)} %all-gather.3.cloned.1.call-done) | copy-start | bytes 12582916
  150.0 1.6 copy-start.4
  151.6 1.0 copy-start.15
Sparse Core Ops, SparseCore 0:
  52.6 80.4 all-gather.2

commit v3 on v2

--- a/solution.py
+++ b/solution.py
@@ -113,6 +113,8 @@
     keys,
     values,
     heads,
+    patch_select,
+    select,
     sems,
 ):
     core = core_ref[0]
@@ -128,7 +130,11 @@
                     sems.at[m * 2 + part],
                 )
             )
-    for copy in copies:
+    late = [
+        pltpu.make_async_copy(select_ref, select, sems.at[32]),
+        pltpu.make_async_copy(patch_select_ref, patch_select, sems.at[33]),
+    ]
+    for copy in copies + late:
         copy.start()
     for copy in copies:
         copy.wait()
@@ -191,11 +197,13 @@
         lax.fori_loop(0, WINS, window, 0)
         done += WINS * count
 
-    own = jnp.dot(select_ref[...], heads[...], preferred_element_type=F32).astype(BF16)
+    for copy in late:
+        copy.wait()
+    own = jnp.dot(select[...], heads[...], preferred_element_type=F32).astype(BF16)
     projected = jnp.dot(own, columns(3 * D, D), preferred_element_type=F32)
     branch = norm_rows(projected, gain_ref[...], offset_ref[...]).astype(BF16)
     patches = jnp.dot(
-        patch_select_ref[...], tall_ref[...].reshape(18 * 48, D), preferred_element_type=F32
+        patch_select[...], tall_ref[...].reshape(18 * 48, D), preferred_element_type=F32
     )
     out_ref[...] = (patches + branch.astype(F32)).astype(BF16)
 
@@ -209,11 +217,11 @@
     merge_offset_ref,
     mine_ref,
     other_ref,
-    merge_ref,
     out_ref,
     up,
     down,
     merge,
+    tokens_in,
     up_sems,
     down_sems,
     merge_sems,
@@ -239,22 +247,20 @@
                     down_sems.at[m * 2 + part],
                 )
             )
-        x, y_lo, of = m // 4, m // 2 % 2, m % 2
-        for part in range(2):
+            start = pl.multiple_of(y_lo * 64 + of * 32, 32)
             merges.append(
                 pltpu.make_async_copy(
-                    merge_ref.at[m, :, pl.ds(part * 32, 32), :],
-                    merge.at[
-                        :, pl.ds(y_lo * 64 + of * 32, 32), pl.ds(x * 256 + part * 128, 128)
-                    ],
+                    ref.at[m, :, pl.ds(32, 32), :],
+                    merge.at[:, pl.ds(start, 32), pl.ds(m // 2 * 128, 128)],
                     merge_sems.at[m * 2 + part],
                 )
             )
+    ups.append(pltpu.make_async_copy(first_ref, tokens_in, up_sems.at[32]))
     for copy in ups + downs + merges:
         copy.start()
     for copy in ups:
         copy.wait()
-    tokens = first_ref[...]
+    tokens = tokens_in[...]
     total = None
     for n in range(FFN // 512):
         cut = slice(n * 512, n * 512 + 512)
@@ -357,21 +363,20 @@
             lax.dynamic_slice(
                 feedforward_out_weight, (lax.axis_index("y_hi") * 16, x * 128), (16, 128)
             ),
-            lax.dynamic_slice(merging_reduction_weight, (0, x * 256), (32, 128)),
-            lax.dynamic_slice(merging_reduction_weight, (0, x * 256 + 128), (32, 128)),
+            lax.dynamic_slice(merging_reduction_weight, (0, lat * 128), (32, 128)),
         ]
     )
-    units, patches = lax.optimization_barrier((units, patches))
-    along_z = spread(units, "z")
+
     east = shifted(patches[:, :SHIFT_COLS], LON, -1, True)
     west = shifted(patches[:, 36 - SHIFT_COLS :], LON, 1, True)
     wide = jnp.concatenate([west, patches, east], axis=1)
+    units, wide = lax.optimization_barrier((units, wide))
+    along_z = spread(units, "z")
     south = shifted(wide[:SHIFT_ROWS], LAT, -1, False)
     north = shifted(wide[12 - SHIFT_ROWS :], LAT, 1, False)
     tall = jnp.concatenate([north, wide, south], axis=0)
 
     along_z, tall = lax.optimization_barrier((along_z, tall))
-    merge_all = lax.all_gather(along_z[:, 48:], ("x", "y_lo", "core"), axis=0)
     attn_mine = spread(along_z[:, :16], PLANE)
 
     table = bias_entries(
@@ -393,19 +398,25 @@
     bias = jnp.where(seam[:, None, None, None] & jnp.asarray(apart), OFF, bias[None])
     head_scale = jnp.exp(jnp.minimum(head_scale_logarithm, jnp.log(100.0)))
 
-    attn_mine, ffn_z, bias = lax.optimization_barrier((attn_mine, along_z[:, 16:48], bias))
+    attn_mine, along_z, bias = lax.optimization_barrier((attn_mine, along_z, bias))
     attn_other = shifted(attn_mine, "core", 1, True)
-    ffn_mine = spread(ffn_z, PLANE)
+    rest_mine = spread(along_z[:, 16:], PLANE)
 
     vmem = pl.BlockSpec(memory_space=pltpu.VMEM)
     smem = pl.BlockSpec(memory_space=pltpu.SMEM)
-    anywhere = pl.BlockSpec(memory_space=pltpu.HBM)
+    hbm = pl.BlockSpec(memory_space=pltpu.HBM)
+    anywhere = pl.BlockSpec(memory_space=pl.ANY)
+
+    def far(block):
+        return pltpu.with_memory_space_constraint(block, pltpu.HBM)
+
+    params = pltpu.CompilerParams(vmem_limit_bytes=24 * 1024 * 1024)
     core_index = core.astype(jnp.int32).reshape(1)
     half = WINS * WIN_PAD
     first = pl.pallas_call(
         attention_kernel,
         out_shape=jax.ShapeDtypeStruct((4 * QUAD_ROWS, D), BF16),
-        in_specs=[smem, smem] + [vmem] * 7 + [anywhere] * 2,
+        in_specs=[smem, smem] + [vmem] * 3 + [hbm] * 2 + [vmem] * 2 + [anywhere] * 2,
         out_specs=vmem,
         scratch_shapes=[
             pltpu.VMEM((16, 32, 2048), BF16),
@@ -413,9 +424,11 @@
             pltpu.VMEM((half, D), BF16),
             pltpu.VMEM((half, D), BF16),
             pltpu.VMEM((768, D), BF16),
-            pltpu.SemaphoreType.DMA((32,)),
+            pltpu.VMEM((4 * QUAD_ROWS, 864), BF16),
+            pltpu.VMEM((4 * QUAD_ROWS, 768), BF16),
+            pltpu.SemaphoreType.DMA((34,)),
         ],
-        compiler_params=pltpu.CompilerParams(vmem_limit_bytes=24 * 1024 * 1024),
+        compiler_params=params,
         cost_estimate=pl.CostEstimate(
             flops=20_000_000_000, bytes_accessed=20_000_000, transcendentals=1_000_000
         ),
@@ -426,43 +439,43 @@
         tall,
         bias,
         jnp.asarray(arrangement(), BF16),
-        jnp.asarray(patch_selection(), BF16),
-        jnp.asarray(selection(), BF16),
+        far(jnp.asarray(patch_selection(), BF16)),
+        far(jnp.asarray(selection(), BF16)),
         attention_norm_gain.reshape(1, D),
         attention_norm_offset.reshape(1, D),
         attn_mine,
         attn_other,
     )
-    first, ffn_mine = lax.optimization_barrier((first, ffn_mine))
-    ffn_other = shifted(ffn_mine, "core", 1, True)
+    first, rest_mine = lax.optimization_barrier((first, rest_mine))
+    rest_other = shifted(rest_mine, "core", 1, True)
     return pl.pallas_call(
         feedforward_kernel,
         out_shape=jax.ShapeDtypeStruct((6, 18, 2 * D), BF16),
-        in_specs=[smem] + [vmem] * 5 + [anywhere] * 3,
+        in_specs=[smem, hbm] + [vmem] * 4 + [anywhere] * 2,
         out_specs=vmem,
         scratch_shapes=[
             pltpu.VMEM((16, 32, FFN), BF16),
             pltpu.VMEM((16, 128, D), BF16),
             pltpu.VMEM((16, 128, 2 * D), BF16),
-            pltpu.SemaphoreType.DMA((32,)),
+            pltpu.VMEM((4 * QUAD_ROWS, D), BF16),
+            pltpu.SemaphoreType.DMA((33,)),
             pltpu.SemaphoreType.DMA((32,)),
             pltpu.SemaphoreType.DMA((32,)),
         ],
-        compiler_params=pltpu.CompilerParams(vmem_limit_bytes=24 * 1024 * 1024),
+        compiler_params=params,
         cost_estimate=pl.CostEstimate(
-            flops=3_000_000_000, bytes_accessed=20_000_000, transcendentals=1_000_000
+            flops=6_000_000_000, bytes_accessed=20_000_000, transcendentals=1_000_000
         ),
         name="feedforward",
     )(
         core_index,
-        first,
+        far(first),
         feedforward_norm_gain.reshape(1, D),
         feedforward_norm_offset.reshape(1, D),
         merging_norm_gain.reshape(1, 2 * D),
         merging_norm_offset.reshape(1, 2 * D),
-        ffn_mine,
-        ffn_other,
-        merge_all,
+        rest_mine,
+        rest_other,
     )
 
 

time: 168 us -> 158 us (0.940)
  waiting for transfers between devices: 31.1 us -> 60.5 us
  starting transfers between devices: 65.1 us -> 51.6 us
  between operations: 13.8 us -> 0.54 us
  local copies, waits for them, and re-layouts: 20.4 us -> 9.98 us
  Pallas kernels: 30.3 us -> 28.6 us
    all_to_all x3, waiting for transfers between devices: 17.6 us -> 43.8 us  [spread(): lax.all_to_all(jnp.broadcast_to(block[None], (size,) + block.shape), axes...]
    unnamed x54 -> x40, local copies, waits for them, and re-layouts: 14.3 us -> 2.39 us
    all_to_all x3, starting transfers between devices: 37.5 us -> 26 us  [spread(): lax.all_to_all(jnp.broadcast_to(block[None], (size,) + block.shape), axes...]
    ppermute x7, waiting for transfers between devices: 13.5 us -> 16.8 us  [shifted(): return lax.ppermute(block, axes, pairs)]
    ppermute x7, starting transfers between devices: 27.6 us -> 25.6 us  [shifted(): return lax.ppermute(block, axes, pairs)]
  transfers between devices with their start and end apart: 11 -> 10, of which waited for: 8 -> 8; matrix products, arithmetic and copies ran while one was open for 6% -> 4% of each run, Pallas kernels for 14% -> 14%
where the time goes in v3:
time: 158 us; the launch traced here: 157 us
  waiting for transfers between devices  60.5 us (38%)
  starting transfers between devices  51.6 us (33%)
  Pallas kernels  28.6 us (18%)
  local copies, waits for them, and re-layouts  9.98 us (6%)
  matrix products  4.62 us (3%)
    all_to_all x3, waiting for transfers between devices, spread(): lax.all_to_all(jnp.broadcast_to(block[None], (size,) + block.shape), axes...  43.8 us
    all_to_all x3, starting transfers between devices, spread(): lax.all_to_all(jnp.broadcast_to(block[None], (size,) + block.shape), axes...  26 us
    ppermute x7, starting transfers between devices, shifted(): return lax.ppermute(block, axes, pairs)  25.6 us
    pallas_call x1, Pallas kernels, local(): pl.pallas_call(attention_kernel, out_shape=jax.ShapeDtypeStruct((4 * QUAD...  21.7 us
    ppermute x7, waiting for transfers between devices, shifted(): return lax.ppermute(block, axes, pairs)  16.8 us
    pallas_call x1, Pallas kernels, local(): pl.pallas_call(feedforward_kernel, out_shape=jax.ShapeDtypeStruct((6, 18,...  6.86 us
    broadcast_in_dim x3, local copies, waits for them, and re-layouts, spread(): jnp.broadcast_to(block[None], (size,) + block.shape)  5.05 us
    dot_general x1, matrix products, local(): bias = jnp.dot(table, one_hot, precision=lax.Precision.HIGHEST)  3.95 us
  transfers between devices with their start and end apart: 10, of which 8 were waited for; matrix products, arithmetic and copies ran while one was open for 4% of the time, Pallas kernels for 14%

profile of v3, /device:TPU:1, one launch (start us, length us, event | category | flops | bytes accessed | tf_op | source)
XLA Modules:
  0.0 156.6 jit_solution(3182984576956017961)
XLA Ops:
  0.0 0.8 constant_dynamic-update-slice_fusion.2
  0.8 0.7 constant_dynamic-update-slice_fusion.1
  1.5 0.8 constant_dynamic-update-slice_fusion
  2.3 8.8 %collective-permute-start = (bf16[8,4096]{1,0:T(8,128)(2,1)S(1)}, bf16[8,4096]{1,0:T(8,128)(2,1)S(1)}, u32[]{:S(2)}, u32[]{:S(2)}) collective-permute-start(bf16[8,4096]{1,0:T(8,128)(2,1)S(1)} %constant_dynamic-update-slice_fusion), channel_id=1, source_target_pairs={{0,1},{1,0},{2,3},{3,2},{4,5},{5,4},{6,7},{7,6},{8,9},{9,8},{10,11... | collective-permute-start | bytes 196616 | tf_op jit(solution)/shard_map/ppermute | solution.py:35
  11.0 1.0 fusion.22
  12.1 1.9 %collective-permute-start.1 = (bf16[12,6,512]{2,1,0:T(8,128)(2,1)S(1)}, bf16[12,6,512]{2,1,0:T(8,128)(2,1)S(1)}, u32[]{:S(2)}, u32[]{:S(2)}) collective-permute-start(bf16[12,6,512]{2,1,0:T(8,128)(2,1)S(1)} %get-tuple-element.25), channel_id=1, source_target_pairs={{0,1},{1,2},{2,3},{3,4},{4,5},{5,6},{6,7},{7,8},{8,9},{9,10},{10,1... | collective-permute-start | bytes 221192 | tf_op jit(solution)/shard_map/ppermute | solution.py:35
  14.0 2.4 %collective-permute-start.2 = (bf16[12,6,512]{2,1,0:T(8,128)(2,1)S(1)}, bf16[12,6,512]{2,1,0:T(8,128)(2,1)S(1)}, u32[]{:S(2)}, u32[]{:S(2)}) collective-permute-start(bf16[12,6,512]{2,1,0:T(8,128)(2,1)S(1)} %get-tuple-element.26), channel_id=1, source_target_pairs={{0,63},{1,0},{2,1},{3,2},{4,3},{5,4},{6,5},{7,6},{8,7},{9,8},{10,9... | collective-permute-start | bytes 221192 | tf_op jit(solution)/shard_map/ppermute | solution.py:35
  16.4 0.7 dynamic_slice.14
  17.1 0.0 collective-permute-done
  17.2 0.0 copy-start.11
  17.2 0.0 copy-start.13
  17.2 0.0 copy-start.14
  17.2 0.0 copy-start.17
  17.3 0.0 copy-start.18
  17.3 0.0 collective-permute-done.1
  17.3 3.9 %collective-permute-done.2 = bf16[12,6,512]{2,1,0:T(8,128)(2,1)S(1)} collective-permute-done((bf16[12,6,512]{2,1,0:T(8,128)(2,1)S(1)}, bf16[12,6,512]{2,1,0:T(8,128)(2,1)S(1)}, u32[]{:S(2)}, u32[]{:S(2)}) %collective-permute-start.2) | collective-permute-done | bytes 73760 | tf_op jit(solution)/shard_map/ppermute | solution.py:35
  21.1 0.2 pad_maximum_fusion.1
  21.4 0.8 broadcast_in_dim.34
  22.1 9.5 %all-to-all-start = ((bf16[16,80,128]{2,1,0:T(8,128)(2,1)}), bf16[16,80,128]{2,1,0:T(8,128)(2,1)S(1)}, u32[]{:S(2)}, u32[]{:S(2)}) async-start(bf16[16,80,128]{2,1,0:T(8,128)(2,1)} %broadcast_in_dim.34), calls=%async_computation | async-start | bytes 655360 | tf_op jit(solution)/shard_map/all_to_all | solution.py:40
  31.7 3.1 %collective-permute-start.3 = (bf16[3,48,512]{2,1,0:T(8,128)(2,1)S(1)}, bf16[3,48,512]{2,1,0:T(8,128)(2,1)S(1)}, u32[]{:S(2)}, u32[]{:S(2)}) collective-permute-start(bf16[3,48,512]{2,1,0:T(8,128)(2,1)S(1)} %get-tuple-element.23), channel_id=1, source_target_pairs={{0,64},{64,128},{128,192},{192,256},{256,320},{320,384},{384,448},... | collective-permute-start | bytes 442376 | tf_op jit(solution)/shard_map/ppermute | solution.py:35
  34.9 1.3 collective-permute-start.4
  36.2 0.7 fusion.6
  36.9 0.1 collective-permute-done.3
  36.9 3.8 %collective-permute-done.4 = bf16[3,48,512]{2,1,0:T(8,128)(2,1)S(1)} collective-permute-done((bf16[3,48,512]{2,1,0:T(8,128)(2,1)S(1)}, bf16[3,48,512]{2,1,0:T(8,128)(2,1)S(1)}, u32[]{:S(2)}, u32[]{:S(2)}) %collective-permute-start.4) | collective-permute-done | bytes 147488 | tf_op jit(solution)/shard_map/ppermute | solution.py:35
  40.7 0.1 pad_maximum_fusion.tall_ref
  40.9 5.8 %all-to-all-done = bf16[16,80,128]{2,1,0:T(8,128)(2,1)S(1)} async-done(((bf16[16,80,128]{2,1,0:T(8,128)(2,1)}), bf16[16,80,128]{2,1,0:T(8,128)(2,1)S(1)}, u32[]{:S(2)}, u32[]{:S(2)}) %all-to-all-start) | async-done | bytes 327712 | tf_op jit(solution)/shard_map/all_to_all | solution.py:40
  46.7 1.2 broadcast_in_dim.35
  47.9 11.8 %all-to-all-start.1 = ((bf16[16,16,16,128]{3,2,1,0:T(8,128)(2,1)}), bf16[16,16,16,128]{3,2,1,0:T(8,128)(2,1)S(1)}, u32[]{:S(2)}, u32[]{:S(2)}) async-start(bf16[16,16,16,128]{3,2,1,0:T(8,128)(2,1)} %broadcast_in_dim.35), calls=%async_computation.1 | async-start | bytes 2097152 | tf_op jit(solution)/shard_map/all_to_all | solution.py:40
  59.7 0.1 pad_add_fusion
  59.7 0.0 copy-done.16
  59.7 4.0 %fusion.2 = f32[8,96,128]{2,0,1:T(8,128)S(1)} fusion(f32[253,8]{0,1:T(8,128)S(1)} %fusion.6, s32[12288]{0:T(1024)S(1)} %copy-done.16), kind=kOutput, calls=%fused_computation.3 | convolution fusion | flops 301559808 | bytes 450464 | tf_op jit(solution)/shard_map/dot_general | solution.py:391
  63.7 0.1 broadcast_and_fusion
  63.8 0.1 copy_select_fusion
  63.9 0.1 broadcast_select_fusion.bias_ref
  64.1 11.4 %all-to-all-done.1.mine_ref = bf16[16,16,16,128]{3,2,1,0:T(8,128)(2,1)S(1)} async-done(((bf16[16,16,16,128]{3,2,1,0:T(8,128)(2,1)}), bf16[16,16,16,128]{3,2,1,0:T(8,128)(2,1)S(1)}, u32[]{:S(2)}, u32[]{:S(2)}) %all-to-all-start.1) | async-done | bytes 1048608 | tf_op jit(solution)/shard_map/all_to_all | solution.py:40
  75.5 3.1 %broadcast_in_dim.59 = bf16[16,16,64,128]{3,2,1,0:T(8,128)(2,1)} broadcast(bf16[16,64,128]{2,1,0:T(8,128)(2,1)S(1)} %slice.39), dimensions={1,2,3} | broadcast | bytes 4456448 | tf_op jit(solution)/shard_map/broadcast_in_dim | solution.py:40
  78.6 4.7 %all-to-all-start.2 = ((bf16[16,16,64,128]{3,2,1,0:T(8,128)(2,1)}), bf16[16,16,64,128]{3,2,1,0:T(8,128)(2,1)}, u32[]{:S(2)}, u32[]{:S(2)}) async-start(bf16[16,16,64,128]{3,2,1,0:T(8,128)(2,1)} %broadcast_in_dim.59), calls=%async_computation.2 | async-start | bytes 8388608 | tf_op jit(solution)/shard_map/all_to_all | solution.py:40
  83.3 4.9 %collective-permute-start.5 = (bf16[16,16,16,128]{3,2,1,0:T(8,128)(2,1)S(1)}, bf16[16,16,16,128]{3,2,1,0:T(8,128)(2,1)S(1)}, u32[]{:S(2)}, u32[]{:S(2)}) collective-permute-start(bf16[16,16,16,128]{3,2,1,0:T(8,128)(2,1)S(1)} %all-to-all-done.1.mine_ref), channel_id=1, source_target_pairs={{0,1},{1,0},{2,3},{3,2},{4,5},{5,4},{6,7},{7,6},{8,9},{9,8},{10,11... | collective-permute-start | bytes 3145736 | tf_op jit(solution)/shard_map/ppermute | solution.py:35
  88.3 2.1 %collective-permute-done.5.other_ref = bf16[16,16,16,128]{3,2,1,0:T(8,128)(2,1)S(1)} collective-permute-done((bf16[16,16,16,128]{3,2,1,0:T(8,128)(2,1)S(1)}, bf16[16,16,16,128]{3,2,1,0:T(8,128)(2,1)S(1)}, u32[]{:S(2)}, u32[]{:S(2)}) %collective-permute-start.5) | collective-permute-done | bytes 1048608 | tf_op jit(solution)/shard_map/ppermute | solution.py:35
  90.3 0.0 copy-start.2
  90.3 0.0 copy-start.5
  90.4 0.0 copy-start.6
  90.4 21.7 %attention.1.first_ref = bf16[448,512]{1,0:T(8,128)(2,1)S(1)} custom-call(s32[1]{0:T(128)} %bitcast.core_ref, f32[8]{0:T(128)S(1)} %minimum_exponential_fusion.scale_ref, bf16[18,48,512]{2,1,0:T(8,128)(2,1)S(1)} %pad_maximum_fusion.tall_ref, f32[3,8,96,128]{3,2,1,0:T(8,128)S(1)} %broadcast_select_fusion.bias_ref, bf16[384,288]{1,0:T(8,128)(2,1)S(1)} %copy-done.7, ...), custom_call_target="tpu_custom_call" | custom-call | flops 20000000000 | bytes 20000000 | tf_op jit(solution)/shard_map/attention/pallas_call | solution.py:416
  112.1 0.8 copy-done.8
  112.9 26.5 %all-to-all-done.2.mine_ref = bf16[16,16,64,128]{3,2,1,0:T(8,128)(2,1)} async-done(((bf16[16,16,64,128]{3,2,1,0:T(8,128)(2,1)}), bf16[16,16,64,128]{3,2,1,0:T(8,128)(2,1)}, u32[]{:S(2)}, u32[]{:S(2)}) %all-to-all-start.2) | async-done | bytes 4194336 | tf_op jit(solution)/shard_map/all_to_all | solution.py:40
  139.5 3.1 %collective-permute-start.6 = (bf16[16,16,64,128]{3,2,1,0:T(8,128)(2,1)}, bf16[16,16,64,128]{3,2,1,0:T(8,128)(2,1)S(1)}, u32[]{:S(2)}, u32[]{:S(2)}) collective-permute-start(bf16[16,16,64,128]{3,2,1,0:T(8,128)(2,1)} %all-to-all-done.2.mine_ref), channel_id=1, source_target_pairs={{0,1},{1,0},{2,3},{3,2},{4,5},{5,4},{6,7},{7,6},{8,9},{9,8},{10,11... | collective-permute-start | bytes 12582920 | tf_op jit(solution)/shard_map/ppermute | solution.py:35
  142.6 7.0 %collective-permute-done.6.other_ref = bf16[16,16,64,128]{3,2,1,0:T(8,128)(2,1)S(1)} collective-permute-done((bf16[16,16,64,128]{3,2,1,0:T(8,128)(2,1)}, bf16[16,16,64,128]{3,2,1,0:T(8,128)(2,1)S(1)}, u32[]{:S(2)}, u32[]{:S(2)}) %collective-permute-start.6) | collective-permute-done | bytes 4194336 | tf_op jit(solution)/shard_map/ppermute | solution.py:35
  149.6 6.9 %feedforward.1 = bf16[6,18,1024]{2,1,0:T(8,128)(2,1)} custom-call(s32[1]{0:T(128)} %bitcast.core_ref, bf16[448,512]{1,0:T(8,128)(2,1)} %copy-done.8, f32[1,512]{1,0:T(1,128)S(1)} %bitcast.20, f32[1,512]{1,0:T(1,128)S(1)} %bitcast.21, f32[1,1024]{1,0:T(1,128)S(1)} %bitcast.16, f32[1,1024]{1,0:T(1,128)S(1)} %bitcast.17, ...), custom_call_target="tpu_custom_call" | custom-call | flops 6000000000 | bytes 20000000 | tf_op jit(solution)/shard_map/feedforward/pallas_call | solution.py:451
  (37 shorter events, 0.1 us)
Async XLA Ops:
  0.0 17.1 %copy-start = (bf16[32,1024]{1,0:T(8,128)(2,1)S(1)}, bf16[32,1024]{1,0:T(8,128)(2,1)}, u32[]{:S(2)}) copy-start(bf16[32,1024]{1,0:T(8,128)(2,1)} %param.28) | copy-start | bytes 196612
  0.0 21.1 %copy-start.9 = (bf16[12,36,512]{2,1,0:T(8,128)(2,1)S(1)}, bf16[12,36,512]{2,1,0:T(8,128)(2,1)}, u32[]{:S(2)}) copy-start(bf16[12,36,512]{2,1,0:T(8,128)(2,1)} %param.23) | copy-start | bytes 1327108
  2.3 14.9 %collective-permute-start = (bf16[8,4096]{1,0:T(8,128)(2,1)S(1)}, bf16[8,4096]{1,0:T(8,128)(2,1)S(1)}, u32[]{:S(2)}, u32[]{:S(2)}) collective-permute-start(bf16[8,4096]{1,0:T(8,128)(2,1)S(1)} %constant_dynamic-update-slice_fusion), channel_id=1, source_target_pairs={{0,1},{1,0},{2,3},{3,2},{4,5},{5,4},{6,7},{7,6},{8,9},{9,8},{10,11... | collective-permute-start | bytes 196616 | tf_op jit(solution)/shard_map/ppermute | solution.py:35
  12.1 5.2 %collective-permute-start.1 = (bf16[12,6,512]{2,1,0:T(8,128)(2,1)S(1)}, bf16[12,6,512]{2,1,0:T(8,128)(2,1)S(1)}, u32[]{:S(2)}, u32[]{:S(2)}) collective-permute-start(bf16[12,6,512]{2,1,0:T(8,128)(2,1)S(1)} %get-tuple-element.25), channel_id=1, source_target_pairs={{0,1},{1,2},{2,3},{3,4},{4,5},{5,6},{6,7},{7,8},{8,9},{9,10},{10,1... | collective-permute-start | bytes 221192 | tf_op jit(solution)/shard_map/ppermute | solution.py:35
  14.0 7.1 %collective-permute-start.2 = (bf16[12,6,512]{2,1,0:T(8,128)(2,1)S(1)}, bf16[12,6,512]{2,1,0:T(8,128)(2,1)S(1)}, u32[]{:S(2)}, u32[]{:S(2)}) collective-permute-start(bf16[12,6,512]{2,1,0:T(8,128)(2,1)S(1)} %get-tuple-element.26), channel_id=1, source_target_pairs={{0,63},{1,0},{2,1},{3,2},{4,3},{5,4},{6,5},{7,6},{8,7},{9,8},{10,9... | collective-permute-start | bytes 221192 | tf_op jit(solution)/shard_map/ppermute | solution.py:35
  17.2 14.5 %copy-start.11 = (f32[2,512]{1,0:T(2,128)S(1)}, f32[2,512]{1,0:T(2,128)}, u32[]{:S(2)}) copy-start(f32[2,512]{1,0:T(2,128)} %param.30) | copy-start | bytes 12292
  17.2 18.9 %copy-start.13 = (f32[512,8]{0,1:T(8,128)S(1)}, f32[512,8]{0,1:T(8,128)}, u32[]{:S(2)}) copy-start(f32[512,8]{0,1:T(8,128)} %param.32) | copy-start | bytes 49156
  17.2 18.9 %copy-start.14 = (f32[512]{0:T(512)S(1)}, f32[512]{0:T(512)}, u32[]{:S(2)}) copy-start(f32[512]{0:T(512)} %param.31) | copy-start | bytes 6148
  17.2 18.9 %copy-start.17 = (f32[253]{0:T(256)S(1)}, f32[253]{0:T(256)}, u32[]{:S(2)}) copy-start(f32[253]{0:T(256)} %constant.81) | copy-start | bytes 3040
  17.3 18.9 %copy-start.18 = (f32[253]{0:T(256)S(1)}, f32[253]{0:T(256)}, u32[]{:S(2)}) copy-start(f32[253]{0:T(256)} %constant.79) | copy-start | bytes 3040
  22.1 24.5 %all-to-all-start = ((bf16[16,80,128]{2,1,0:T(8,128)(2,1)}), bf16[16,80,128]{2,1,0:T(8,128)(2,1)S(1)}, u32[]{:S(2)}, u32[]{:S(2)}) async-start(bf16[16,80,128]{2,1,0:T(8,128)(2,1)} %broadcast_in_dim.34), calls=%async_computation | async-start | bytes 655360 | tf_op jit(solution)/shard_map/all_to_all | solution.py:40
  31.7 5.2 %collective-permute-start.3 = (bf16[3,48,512]{2,1,0:T(8,128)(2,1)S(1)}, bf16[3,48,512]{2,1,0:T(8,128)(2,1)S(1)}, u32[]{:S(2)}, u32[]{:S(2)}) collective-permute-start(bf16[3,48,512]{2,1,0:T(8,128)(2,1)S(1)} %get-tuple-element.23), channel_id=1, source_target_pairs={{0,64},{64,128},{128,192},{192,256},{256,320},{320,384},{384,448},... | collective-permute-start | bytes 442376 | tf_op jit(solution)/shard_map/ppermute | solution.py:35
  34.9 5.9 %collective-permute-start.4 = (bf16[3,48,512]{2,1,0:T(8,128)(2,1)S(1)}, bf16[3,48,512]{2,1,0:T(8,128)(2,1)S(1)}, u32[]{:S(2)}, u32[]{:S(2)}) collective-permute-start(bf16[3,48,512]{2,1,0:T(8,128)(2,1)S(1)} %get-tuple-element.24), channel_id=1, source_target_pairs={{64,0},{128,64},{192,128},{256,192},{320,256},{384,320},{448,384},... | collective-permute-start | bytes 442376 | tf_op jit(solution)/shard_map/ppermute | solution.py:35
  47.9 11.9 %copy-start.16 = (s32[12288]{0:T(1024)S(1)}, s32[12288]{0:T(1024)}, u32[]{:S(2)}) copy-start(s32[12288]{0:T(1024)} %constant.66.clone) | copy-start | bytes 147460
  47.9 27.6 %all-to-all-start.1 = ((bf16[16,16,16,128]{3,2,1,0:T(8,128)(2,1)}), bf16[16,16,16,128]{3,2,1,0:T(8,128)(2,1)S(1)}, u32[]{:S(2)}, u32[]{:S(2)}) async-start(bf16[16,16,16,128]{3,2,1,0:T(8,128)(2,1)} %broadcast_in_dim.35), calls=%async_computation.1 | async-start | bytes 2097152 | tf_op jit(solution)/shard_map/all_to_all | solution.py:40
  59.7 4.0 %copy-start.10 = (pred[96,128]{1,0:T(32,128)(4,1)S(1)}, pred[96,128]{1,0:T(32,128)(4,1)}, u32[]{:S(2)}) copy-start(pred[96,128]{1,0:T(32,128)(4,1)} %constant.68.clone) | copy-start | bytes 36868
  59.7 4.1 %copy-start.12 = (pred[128]{0:T(512)(128)(4,1)S(1)}, pred[128]{0:T(512)(128)(4,1)}, u32[]{:S(2)}) copy-start(pred[128]{0:T(512)(128)(4,1)} %constant.67.clone) | copy-start | bytes 388
  78.6 9.6 %copy-start.15 = (f32[8]{0:T(128)S(1)}, f32[8]{0:T(128)}, u32[]{:S(2)}) copy-start(f32[8]{0:T(128)} %param.29) | copy-start | bytes 100
  78.6 11.7 %copy-start.3 = (f32[512]{0:T(512)S(1)}, f32[512]{0:T(512)}, u32[]{:S(2)}) copy-start(f32[512]{0:T(512)} %param.33) | copy-start | bytes 6148
  78.6 11.7 %copy-start.4 = (f32[512]{0:T(512)S(1)}, f32[512]{0:T(512)}, u32[]{:S(2)}) copy-start(f32[512]{0:T(512)} %param.34) | copy-start | bytes 6148
  78.6 11.7 %copy-start.7 = (bf16[384,288]{1,0:T(8,128)(2,1)S(1)}, bf16[384,288]{1,0:T(8,128)(2,1)}, u32[]{:S(2)}) copy-start(bf16[384,288]{1,0:T(8,128)(2,1)} %constant.69.clone.arrange_ref) | copy-start | bytes 663556
  78.6 60.8 %all-to-all-start.2 = ((bf16[16,16,64,128]{3,2,1,0:T(8,128)(2,1)}), bf16[16,16,64,128]{3,2,1,0:T(8,128)(2,1)}, u32[]{:S(2)}, u32[]{:S(2)}) async-start(bf16[16,16,64,128]{3,2,1,0:T(8,128)(2,1)} %broadcast_in_dim.59), calls=%async_computation.2 | async-start | bytes 8388608 | tf_op jit(solution)/shard_map/all_to_all | solution.py:40
  83.3 7.0 %collective-permute-start.5 = (bf16[16,16,16,128]{3,2,1,0:T(8,128)(2,1)S(1)}, bf16[16,16,16,128]{3,2,1,0:T(8,128)(2,1)S(1)}, u32[]{:S(2)}, u32[]{:S(2)}) collective-permute-start(bf16[16,16,16,128]{3,2,1,0:T(8,128)(2,1)S(1)} %all-to-all-done.1.mine_ref), channel_id=1, source_target_pairs={{0,1},{1,0},{2,3},{3,2},{4,5},{5,4},{6,7},{7,6},{8,9},{9,8},{10,11... | collective-permute-start | bytes 3145736 | tf_op jit(solution)/shard_map/ppermute | solution.py:35
  90.3 59.3 %copy-start.1 = (f32[1024]{0:T(1024)S(1)}, f32[1024]{0:T(1024)}, u32[]{:S(2)}) copy-start(f32[1024]{0:T(1024)} %param.37) | copy-start | bytes 12292
  90.3 59.3 %copy-start.2 = (f32[1024]{0:T(1024)S(1)}, f32[1024]{0:T(1024)}, u32[]{:S(2)}) copy-start(f32[1024]{0:T(1024)} %param.38) | copy-start | bytes 12292
  90.3 59.2 %copy-start.5 = (f32[512]{0:T(512)S(1)}, f32[512]{0:T(512)}, u32[]{:S(2)}) copy-start(f32[512]{0:T(512)} %param.35) | copy-start | bytes 6148
  90.4 59.2 %copy-start.6 = (f32[512]{0:T(512)S(1)}, f32[512]{0:T(512)}, u32[]{:S(2)}) copy-start(f32[512]{0:T(512)} %param.36) | copy-start | bytes 6148
  112.1 0.8 copy-start.8
  139.5 10.1 %collective-permute-start.6 = (bf16[16,16,64,128]{3,2,1,0:T(8,128)(2,1)}, bf16[16,16,64,128]{3,2,1,0:T(8,128)(2,1)S(1)}, u32[]{:S(2)}, u32[]{:S(2)}) collective-permute-start(bf16[16,16,64,128]{3,2,1,0:T(8,128)(2,1)} %all-to-all-done.2.mine_ref), channel_id=1, source_target_pairs={{0,1},{1,0},{2,3},{3,2},{4,5},{5,4},{6,7},{7,6},{8,9},{9,8},{10,11... | collective-permute-start | bytes 12582920 | tf_op jit(solution)/shard_map/ppermute | solution.py:35

commit v4 on v3

--- a/solution.py
+++ b/solution.py
@@ -22,7 +22,7 @@
 QUAD_ROWS = 112
 LAT = ("y_hi", "x")
 LON = ("z", "y_lo", "core")
-PLANE = ("y_hi", "x", "y_lo")
+ALL = ("y_hi", "x", "z", "y_lo", "core")
 OFF = -1e30
 BF16 = jnp.bfloat16
 F32 = jnp.float32
@@ -38,6 +38,27 @@
 def spread(block, axes):
     size = lax.axis_size(axes)
     return lax.all_to_all(jnp.broadcast_to(block[None], (size,) + block.shape), axes, 0, 0)
+
+
+def rings(x_core):
+    ids = np.arange(512).reshape(2, 4, 16, 2, 2)
+    along_x = ids.transpose(0, 2, 3, 4, 1)[:, :, :, x_core].reshape(-1, 4)
+    along_y = ids.transpose(1, 2, 4, 0, 3)[:, :, 1 - x_core].reshape(-1, 4)
+    return np.concatenate([along_x, along_y]).tolist()
+
+
+def spread_ring(block, x_core):
+    copies = jnp.broadcast_to(block[None], (4,) + block.shape)
+    return lax.all_to_all(copies, ALL, 0, 0, axis_index_groups=rings(x_core))
+
+
+def place(m, of):
+    outer, inner = m // 4, m % 4
+
+    def pick(on_first, on_second):
+        return on_first + of * (on_second - on_first)
+
+    return pick(outer // 2, inner // 2), pick(inner, outer), pick(outer % 2, inner % 2)
 
 
 def bias_entries(first_weight, first_bias, second_weight):
@@ -120,13 +141,14 @@
     core = core_ref[0]
     copies = []
     for m in range(16):
-        lat, y_lo = m // 2, m % 2
         for part, (ref, of) in enumerate(((mine_ref, core), (other_ref, 1 - core))):
-            column = pl.multiple_of((lat * 2 + of) * 128, 128)
+            y_hi, x, y_lo = place(m, of)
+            row = pl.multiple_of(y_lo * 16, 16)
+            column = pl.multiple_of((y_hi * 8 + x * 2 + of) * 128, 128)
             copies.append(
                 pltpu.make_async_copy(
                     ref.at[m],
-                    weight.at[:, pl.ds(y_lo * 16, 16), pl.ds(column, 128)],
+                    weight.at[:, pl.ds(row, 16), pl.ds(column, 128)],
                     sems.at[m * 2 + part],
                 )
             )
@@ -229,29 +251,32 @@
     core = core_ref[0]
     ups, downs, merges = [], [], []
     for m in range(16):
-        y_hi, x, y_lo = m // 8, m // 2 % 4, m % 2
         for part, (ref, of) in enumerate(((mine_ref, core), (other_ref, 1 - core))):
-            column = pl.multiple_of((m // 2 * 2 + of) * 128, 128)
+            y_hi, x, y_lo = place(m, of)
+            row = pl.multiple_of(y_lo * 16, 16)
+            column = pl.multiple_of((y_hi * 8 + x * 2 + of) * 128, 128)
             ups.append(
                 pltpu.make_async_copy(
                     ref.at[m, :, pl.ds(0, 16), :],
-                    up.at[:, pl.ds(y_lo * 16, 16), pl.ds(column, 128)],
+                    up.at[:, pl.ds(row, 16), pl.ds(column, 128)],
                     up_sems.at[m * 2 + part],
                 )
             )
-            start = pl.multiple_of(y_lo * 64 + of * 32 + y_hi * 16, 16)
+            row = pl.multiple_of(y_lo * 64 + of * 32 + y_hi * 16, 16)
+            column = pl.multiple_of(x * 128, 128)
             downs.append(
                 pltpu.make_async_copy(
                     ref.at[m, :, pl.ds(16, 16), :],
-                    down.at[:, pl.ds(start, 16), pl.ds(x * 128, 128)],
+                    down.at[:, pl.ds(row, 16), pl.ds(column, 128)],
                     down_sems.at[m * 2 + part],
                 )
             )
-            start = pl.multiple_of(y_lo * 64 + of * 32, 32)
+            row = pl.multiple_of(y_lo * 64 + of * 32, 32)
+            column = pl.multiple_of((y_hi * 4 + x) * 128, 128)
             merges.append(
                 pltpu.make_async_copy(
                     ref.at[m, :, pl.ds(32, 32), :],
-                    merge.at[:, pl.ds(start, 32), pl.ds(m // 2 * 128, 128)],
+                    merge.at[:, pl.ds(row, 32), pl.ds(column, 128)],
                     merge_sems.at[m * 2 + part],
                 )
             )
@@ -377,7 +402,8 @@
     tall = jnp.concatenate([north, wide, south], axis=0)
 
     along_z, tall = lax.optimization_barrier((along_z, tall))
-    attn_mine = spread(along_z[:, :16], PLANE)
+    in_ring = spread_ring(along_z, 0)
+    attn_mine = spread_ring(in_ring[:, :, :16], 1).reshape(16, 16, 16, 128)
 
     table = bias_entries(
         bias_network_first_weight, bias_network_first_bias, bias_network_second_weight
@@ -398,9 +424,9 @@
     bias = jnp.where(seam[:, None, None, None] & jnp.asarray(apart), OFF, bias[None])
     head_scale = jnp.exp(jnp.minimum(head_scale_logarithm, jnp.log(100.0)))
 
-    attn_mine, along_z, bias = lax.optimization_barrier((attn_mine, along_z, bias))
+    attn_mine, in_ring, bias = lax.optimization_barrier((attn_mine, in_ring, bias))
     attn_other = shifted(attn_mine, "core", 1, True)
-    rest_mine = spread(along_z[:, 16:], PLANE)
+    rest_mine = spread_ring(in_ring[:, :, 16:], 1).reshape(16, 16, 64, 128)
 
     vmem = pl.BlockSpec(memory_space=pltpu.VMEM)
     smem = pl.BlockSpec(memory_space=pltpu.SMEM)

time: 158 us -> 142 us (0.90)
  waiting for transfers between devices: 60.5 us -> 39.5 us
  starting transfers between devices: 51.6 us -> 54.4 us
  local copies, waits for them, and re-layouts: 9.98 us -> 12.7 us
    all_to_all x3 -> x1, waiting for transfers between devices: 43.8 us -> 5.84 us  [spread(): lax.all_to_all(jnp.broadcast_to(block[None], (size,) + block.shape), axes...]
    all_to_all x0 -> x3, starting transfers between devices: none -> 18 us  [spread_ring(): return lax.all_to_all(copies, ALL, 0, 0, axis_index_groups=rings(x_core))]
    all_to_all x3 -> x1, starting transfers between devices: 26 us -> 9.53 us  [spread(): lax.all_to_all(jnp.broadcast_to(block[None], (size,) + block.shape), axes...]
    all_to_all x0 -> x3, waiting for transfers between devices: none -> 16.1 us  [spread_ring(): return lax.all_to_all(copies, ALL, 0, 0, axis_index_groups=rings(x_core))]
    broadcast_in_dim x0 -> x3, local copies, waits for them, and re-layouts: none -> 5.73 us  [spread_ring(): copies = jnp.broadcast_to(block[None], (4,) + block.shape)]
    broadcast_in_dim x3 -> x1, local copies, waits for them, and re-layouts: 5.05 us -> 0.77 us  [spread(): jnp.broadcast_to(block[None], (size,) + block.shape)]
  transfers between devices with their start and end apart: 10 -> 11, of which waited for: 8 -> 8; matrix products, arithmetic and copies ran while one was open for 4% -> 5% of each run, Pallas kernels for 14% -> 15%
where the time goes in v4:
time: 142 us; the launch traced here: 141 us
  starting transfers between devices  54.4 us (38%)
  waiting for transfers between devices  39.5 us (28%)
  Pallas kernels  28.7 us (20%)
  local copies, waits for them, and re-layouts  12.7 us (9%)
  matrix products  4.62 us (3%)
    ppermute x7, starting transfers between devices, shifted(): return lax.ppermute(block, axes, pairs)  26.9 us
    pallas_call x1, Pallas kernels, local(): pl.pallas_call(attention_kernel, out_shape=jax.ShapeDtypeStruct((4 * QUAD...  21.8 us
    all_to_all x3, starting transfers between devices, spread_ring(): return lax.all_to_all(copies, ALL, 0, 0, axis_index_groups=rings(x_core))  18 us
    ppermute x7, waiting for transfers between devices, shifted(): return lax.ppermute(block, axes, pairs)  17.5 us
    all_to_all x3, waiting for transfers between devices, spread_ring(): return lax.all_to_all(copies, ALL, 0, 0, axis_index_groups=rings(x_core))  16.1 us
    all_to_all x1, starting transfers between devices, spread(): lax.all_to_all(jnp.broadcast_to(block[None], (size,) + block.shape), axes...  9.53 us
    pallas_call x1, Pallas kernels, local(): pl.pallas_call(feedforward_kernel, out_shape=jax.ShapeDtypeStruct((6, 18,...  6.91 us
    all_to_all x1, waiting for transfers between devices, spread(): lax.all_to_all(jnp.broadcast_to(block[None], (size,) + block.shape), axes...  5.84 us
  transfers between devices with their start and end apart: 11, of which 8 were waited for; matrix products, arithmetic and copies ran while one was open for 5% of the time, Pallas kernels for 15%

profile of v4, /device:TPU:1, one launch (start us, length us, event | category | flops | bytes accessed | tf_op | source)
XLA Modules:
  0.0 141.1 jit_solution(14892758933141671403)
XLA Ops:
  0.0 0.8 constant_dynamic-update-slice_fusion.2
  0.8 0.7 constant_dynamic-update-slice_fusion.1
  1.5 0.8 constant_dynamic-update-slice_fusion
  2.3 8.8 %collective-permute-start = (bf16[8,4096]{1,0:T(8,128)(2,1)S(1)}, bf16[8,4096]{1,0:T(8,128)(2,1)S(1)}, u32[]{:S(2)}, u32[]{:S(2)}) collective-permute-start(bf16[8,4096]{1,0:T(8,128)(2,1)S(1)} %constant_dynamic-update-slice_fusion), channel_id=1, source_target_pairs={{0,1},{1,0},{2,3},{3,2},{4,5},{5,4},{6,7},{7,6},{8,9},{9,8},{10,11... | collective-permute-start | bytes 196616 | tf_op jit(solution)/shard_map/ppermute | solution.py:35
  11.0 1.0 fusion.22
  12.1 1.9 %collective-permute-start.1 = (bf16[12,6,512]{2,1,0:T(8,128)(2,1)S(1)}, bf16[12,6,512]{2,1,0:T(8,128)(2,1)S(1)}, u32[]{:S(2)}, u32[]{:S(2)}) collective-permute-start(bf16[12,6,512]{2,1,0:T(8,128)(2,1)S(1)} %get-tuple-element.25), channel_id=1, source_target_pairs={{0,1},{1,2},{2,3},{3,4},{4,5},{5,6},{6,7},{7,8},{8,9},{9,10},{10,1... | collective-permute-start | bytes 221192 | tf_op jit(solution)/shard_map/ppermute | solution.py:35
  14.0 2.4 %collective-permute-start.2 = (bf16[12,6,512]{2,1,0:T(8,128)(2,1)S(1)}, bf16[12,6,512]{2,1,0:T(8,128)(2,1)S(1)}, u32[]{:S(2)}, u32[]{:S(2)}) collective-permute-start(bf16[12,6,512]{2,1,0:T(8,128)(2,1)S(1)} %get-tuple-element.26), channel_id=1, source_target_pairs={{0,63},{1,0},{2,1},{3,2},{4,3},{5,4},{6,5},{7,6},{8,7},{9,8},{10,9... | collective-permute-start | bytes 221192 | tf_op jit(solution)/shard_map/ppermute | solution.py:35
  16.4 0.7 dynamic_slice.14
  17.1 0.0 collective-permute-done
  17.2 0.0 collective-permute-done.1
  17.2 3.9 %collective-permute-done.2 = bf16[12,6,512]{2,1,0:T(8,128)(2,1)S(1)} collective-permute-done((bf16[12,6,512]{2,1,0:T(8,128)(2,1)S(1)}, bf16[12,6,512]{2,1,0:T(8,128)(2,1)S(1)}, u32[]{:S(2)}, u32[]{:S(2)}) %collective-permute-start.2) | collective-permute-done | bytes 73760 | tf_op jit(solution)/shard_map/ppermute | solution.py:35
  21.1 0.2 pad_maximum_fusion.1
  21.4 0.8 broadcast_in_dim.36
  22.1 9.5 %all-to-all-start = ((bf16[16,80,128]{2,1,0:T(8,128)(2,1)}), bf16[16,80,128]{2,1,0:T(8,128)(2,1)S(1)}, u32[]{:S(2)}, u32[]{:S(2)}) async-start(bf16[16,80,128]{2,1,0:T(8,128)(2,1)} %broadcast_in_dim.36), calls=%async_computation | async-start | bytes 655360 | tf_op jit(solution)/shard_map/all_to_all | solution.py:40
  31.7 3.1 %collective-permute-start.3 = (bf16[3,48,512]{2,1,0:T(8,128)(2,1)S(1)}, bf16[3,48,512]{2,1,0:T(8,128)(2,1)S(1)}, u32[]{:S(2)}, u32[]{:S(2)}) collective-permute-start(bf16[3,48,512]{2,1,0:T(8,128)(2,1)S(1)} %get-tuple-element.23), channel_id=1, source_target_pairs={{0,64},{64,128},{128,192},{192,256},{256,320},{320,384},{384,448},... | collective-permute-start | bytes 442376 | tf_op jit(solution)/shard_map/ppermute | solution.py:35
  34.8 1.3 collective-permute-start.4
  36.1 0.8 collective-permute-done.3
  36.9 3.8 %collective-permute-done.4 = bf16[3,48,512]{2,1,0:T(8,128)(2,1)S(1)} collective-permute-done((bf16[3,48,512]{2,1,0:T(8,128)(2,1)S(1)}, bf16[3,48,512]{2,1,0:T(8,128)(2,1)S(1)}, u32[]{:S(2)}, u32[]{:S(2)}) %collective-permute-start.4) | collective-permute-done | bytes 147488 | tf_op jit(solution)/shard_map/ppermute | solution.py:35
  40.7 0.1 pad_maximum_fusion.tall_ref
  40.8 5.8 %all-to-all-done = bf16[16,80,128]{2,1,0:T(8,128)(2,1)S(1)} async-done(((bf16[16,80,128]{2,1,0:T(8,128)(2,1)}), bf16[16,80,128]{2,1,0:T(8,128)(2,1)S(1)}, u32[]{:S(2)}, u32[]{:S(2)}) %all-to-all-start) | async-done | bytes 327712 | tf_op jit(solution)/shard_map/all_to_all | solution.py:40
  46.7 1.3 broadcast_in_dim.37
  47.9 0.0 copy-start.19
  48.0 0.0 copy-start.17
  48.0 9.2 %all-to-all-start.1 = ((bf16[4,16,80,128]{3,2,1,0:T(8,128)(2,1)}), bf16[4,16,80,128]{3,2,1,0:T(8,128)(2,1)S(1)}, u32[]{:S(2)}, u32[]{:S(2)}) async-start(bf16[4,16,80,128]{3,2,1,0:T(8,128)(2,1)} %broadcast_in_dim.37), calls=%async_computation.1 | async-start | bytes 2621440 | tf_op jit(solution)/shard_map/all_to_all | solution.py:52
  57.3 0.7 fusion.6
  57.9 4.0 %fusion.2 = f32[8,96,128]{2,0,1:T(8,128)S(1)} fusion(f32[253,8]{0,1:T(8,128)S(1)} %fusion.6, s32[12288]{0:T(1024)S(1)} %copy-done.17), kind=kOutput, calls=%fused_computation.3 | convolution fusion | flops 301559808 | bytes 450464 | tf_op jit(solution)/shard_map/dot_general | solution.py:417
  61.9 6.8 %all-to-all-done.1 = bf16[4,16,80,128]{3,2,1,0:T(8,128)(2,1)S(1)} async-done(((bf16[4,16,80,128]{3,2,1,0:T(8,128)(2,1)}), bf16[4,16,80,128]{3,2,1,0:T(8,128)(2,1)S(1)}, u32[]{:S(2)}, u32[]{:S(2)}) %all-to-all-start.1) | async-done | bytes 1310752 | tf_op jit(solution)/shard_map/all_to_all | solution.py:52
  68.7 1.4 broadcast_in_dim.38
  70.0 0.0 copy-done.9
  70.1 3.7 %all-to-all-start.2 = ((bf16[4,4,16,16,128]{4,3,2,1,0:T(8,128)(2,1)}), bf16[4,4,16,16,128]{4,3,2,1,0:T(8,128)(2,1)S(1)}, u32[]{:S(2)}, u32[]{:S(2)}) async-start(bf16[4,4,16,16,128]{4,3,2,1,0:T(8,128)(2,1)} %broadcast_in_dim.38), calls=%async_computation.2 | async-start | bytes 2097152 | tf_op jit(solution)/shard_map/all_to_all | solution.py:52
  73.8 0.1 pad_add_fusion
  73.9 0.1 broadcast_and_fusion
  74.0 0.1 copy_select_fusion
  74.1 0.1 broadcast_select_fusion.bias_ref
  74.2 9.3 %all-to-all-done.2 = bf16[4,4,16,16,128]{4,3,2,1,0:T(8,128)(2,1)S(1)} async-done(((bf16[4,4,16,16,128]{4,3,2,1,0:T(8,128)(2,1)}), bf16[4,4,16,16,128]{4,3,2,1,0:T(8,128)(2,1)S(1)}, u32[]{:S(2)}, u32[]{:S(2)}) %all-to-all-start.2) | async-done | bytes 1048608 | tf_op jit(solution)/shard_map/all_to_all | solution.py:52
  83.6 1.2 slice-done
  84.8 3.1 %broadcast_in_dim.66 = bf16[4,4,16,64,128]{4,3,2,1,0:T(8,128)(2,1)} broadcast(bf16[4,16,64,128]{3,2,1,0:T(8,128)(2,1)S(1)} %slice-done), dimensions={1,2,3,4} | broadcast | bytes 5242880 | tf_op jit(solution)/shard_map/broadcast_in_dim | solution.py:51
  87.9 5.0 %all-to-all-start.3 = ((bf16[4,4,16,64,128]{4,3,2,1,0:T(8,128)(2,1)}), bf16[4,4,16,64,128]{4,3,2,1,0:T(8,128)(2,1)}, u32[]{:S(2)}, u32[]{:S(2)}) async-start(bf16[4,4,16,64,128]{4,3,2,1,0:T(8,128)(2,1)} %broadcast_in_dim.66), calls=%async_computation.3 | async-start | bytes 8388608 | tf_op jit(solution)/shard_map/all_to_all | solution.py:52
  92.9 6.5 %collective-permute-start.5 = (bf16[16,16,16,128]{3,2,1,0:T(8,128)(2,1)S(1)}, bf16[16,16,16,128]{3,2,1,0:T(8,128)(2,1)S(1)}, u32[]{:S(2)}, u32[]{:S(2)}) collective-permute-start(bf16[16,16,16,128]{3,2,1,0:T(8,128)(2,1)S(1)} %bitcast.18), channel_id=1, source_target_pairs={{0,1},{1,0},{2,3},{3,2},{4,5},{5,4},{6,7},{7,6},{8,9},{9,8},{10,11... | collective-permute-start | bytes 3145736 | tf_op jit(solution)/shard_map/ppermute | solution.py:35
  99.4 2.1 %collective-permute-done.5.other_ref = bf16[16,16,16,128]{3,2,1,0:T(8,128)(2,1)S(1)} collective-permute-done((bf16[16,16,16,128]{3,2,1,0:T(8,128)(2,1)S(1)}, bf16[16,16,16,128]{3,2,1,0:T(8,128)(2,1)S(1)}, u32[]{:S(2)}, u32[]{:S(2)}) %collective-permute-start.5) | collective-permute-done | bytes 1048608 | tf_op jit(solution)/shard_map/ppermute | solution.py:35
  101.5 0.0 copy-start.2
  101.5 0.0 copy-start.5
  101.5 0.0 copy-start.6
  101.6 21.8 %attention.1.first_ref = bf16[448,512]{1,0:T(8,128)(2,1)S(1)} custom-call(s32[1]{0:T(128)} %bitcast.core_ref, f32[8]{0:T(128)S(1)} %minimum_exponential_fusion.scale_ref, bf16[18,48,512]{2,1,0:T(8,128)(2,1)S(1)} %pad_maximum_fusion.tall_ref, f32[3,8,96,128]{3,2,1,0:T(8,128)S(1)} %broadcast_select_fusion.bias_ref, bf16[384,288]{1,0:T(8,128)(2,1)S(1)} %copy-done.7, ...), custom_call_target="tpu_custom_call" | custom-call | flops 20000000000 | bytes 20000000 | tf_op jit(solution)/shard_map/attention/pallas_call | solution.py:442
  123.4 0.8 copy-done.8
  124.2 2.9 %collective-permute-start.6 = (bf16[16,16,64,128]{3,2,1,0:T(8,128)(2,1)}, bf16[16,16,64,128]{3,2,1,0:T(8,128)(2,1)S(1)}, u32[]{:S(2)}, u32[]{:S(2)}) collective-permute-start(bf16[16,16,64,128]{3,2,1,0:T(8,128)(2,1)} %bitcast.9.mine_ref), channel_id=1, source_target_pairs={{0,1},{1,0},{2,3},{3,2},{4,5},{5,4},{6,7},{7,6},{8,9},{9,8},{10,11... | collective-permute-start | bytes 12582920 | tf_op jit(solution)/shard_map/ppermute | solution.py:35
  127.0 7.0 %collective-permute-done.6.other_ref = bf16[16,16,64,128]{3,2,1,0:T(8,128)(2,1)S(1)} collective-permute-done((bf16[16,16,64,128]{3,2,1,0:T(8,128)(2,1)}, bf16[16,16,64,128]{3,2,1,0:T(8,128)(2,1)S(1)}, u32[]{:S(2)}, u32[]{:S(2)}) %collective-permute-start.6) | collective-permute-done | bytes 4194336 | tf_op jit(solution)/shard_map/ppermute | solution.py:35
  134.0 6.9 %feedforward.1 = bf16[6,18,1024]{2,1,0:T(8,128)(2,1)} custom-call(s32[1]{0:T(128)} %bitcast.core_ref, bf16[448,512]{1,0:T(8,128)(2,1)} %copy-done.8, f32[1,512]{1,0:T(1,128)S(1)} %bitcast.24, f32[1,512]{1,0:T(1,128)S(1)} %bitcast.25, f32[1,1024]{1,0:T(1,128)S(1)} %bitcast.20, f32[1,1024]{1,0:T(1,128)S(1)} %bitcast.21, ...), custom_call_target="tpu_custom_call" | custom-call | flops 6000000000 | bytes 20000000 | tf_op jit(solution)/shard_map/feedforward/pallas_call | solution.py:477
  (43 shorter events, 0.2 us)
Async XLA Ops:
  0.0 17.1 %copy-start = (bf16[32,1024]{1,0:T(8,128)(2,1)S(1)}, bf16[32,1024]{1,0:T(8,128)(2,1)}, u32[]{:S(2)}) copy-start(bf16[32,1024]{1,0:T(8,128)(2,1)} %param.28) | copy-start | bytes 196612
  0.0 21.1 %copy-start.10 = (bf16[12,36,512]{2,1,0:T(8,128)(2,1)S(1)}, bf16[12,36,512]{2,1,0:T(8,128)(2,1)}, u32[]{:S(2)}) copy-start(bf16[12,36,512]{2,1,0:T(8,128)(2,1)} %param.23) | copy-start | bytes 1327108
  2.3 14.9 %collective-permute-start = (bf16[8,4096]{1,0:T(8,128)(2,1)S(1)}, bf16[8,4096]{1,0:T(8,128)(2,1)S(1)}, u32[]{:S(2)}, u32[]{:S(2)}) collective-permute-start(bf16[8,4096]{1,0:T(8,128)(2,1)S(1)} %constant_dynamic-update-slice_fusion), channel_id=1, source_target_pairs={{0,1},{1,0},{2,3},{3,2},{4,5},{5,4},{6,7},{7,6},{8,9},{9,8},{10,11... | collective-permute-start | bytes 196616 | tf_op jit(solution)/shard_map/ppermute | solution.py:35
  12.1 5.1 %collective-permute-start.1 = (bf16[12,6,512]{2,1,0:T(8,128)(2,1)S(1)}, bf16[12,6,512]{2,1,0:T(8,128)(2,1)S(1)}, u32[]{:S(2)}, u32[]{:S(2)}) collective-permute-start(bf16[12,6,512]{2,1,0:T(8,128)(2,1)S(1)} %get-tuple-element.25), channel_id=1, source_target_pairs={{0,1},{1,2},{2,3},{3,4},{4,5},{5,6},{6,7},{7,8},{8,9},{9,10},{10,1... | collective-permute-start | bytes 221192 | tf_op jit(solution)/shard_map/ppermute | solution.py:35
  14.0 7.1 %collective-permute-start.2 = (bf16[12,6,512]{2,1,0:T(8,128)(2,1)S(1)}, bf16[12,6,512]{2,1,0:T(8,128)(2,1)S(1)}, u32[]{:S(2)}, u32[]{:S(2)}) collective-permute-start(bf16[12,6,512]{2,1,0:T(8,128)(2,1)S(1)} %get-tuple-element.26), channel_id=1, source_target_pairs={{0,63},{1,0},{2,1},{3,2},{4,3},{5,4},{6,5},{7,6},{8,7},{9,8},{10,9... | collective-permute-start | bytes 221192 | tf_op jit(solution)/shard_map/ppermute | solution.py:35
  22.1 24.5 %all-to-all-start = ((bf16[16,80,128]{2,1,0:T(8,128)(2,1)}), bf16[16,80,128]{2,1,0:T(8,128)(2,1)S(1)}, u32[]{:S(2)}, u32[]{:S(2)}) async-start(bf16[16,80,128]{2,1,0:T(8,128)(2,1)} %broadcast_in_dim.36), calls=%async_computation | async-start | bytes 655360 | tf_op jit(solution)/shard_map/all_to_all | solution.py:40
  31.7 5.2 %collective-permute-start.3 = (bf16[3,48,512]{2,1,0:T(8,128)(2,1)S(1)}, bf16[3,48,512]{2,1,0:T(8,128)(2,1)S(1)}, u32[]{:S(2)}, u32[]{:S(2)}) collective-permute-start(bf16[3,48,512]{2,1,0:T(8,128)(2,1)S(1)} %get-tuple-element.23), channel_id=1, source_target_pairs={{0,64},{64,128},{128,192},{192,256},{256,320},{320,384},{384,448},... | collective-permute-start | bytes 442376 | tf_op jit(solution)/shard_map/ppermute | solution.py:35
  34.8 5.9 %collective-permute-start.4 = (bf16[3,48,512]{2,1,0:T(8,128)(2,1)S(1)}, bf16[3,48,512]{2,1,0:T(8,128)(2,1)S(1)}, u32[]{:S(2)}, u32[]{:S(2)}) collective-permute-start(bf16[3,48,512]{2,1,0:T(8,128)(2,1)S(1)} %get-tuple-element.24), channel_id=1, source_target_pairs={{64,0},{128,64},{192,128},{256,192},{320,256},{384,320},{448,384},... | collective-permute-start | bytes 442376 | tf_op jit(solution)/shard_map/ppermute | solution.py:35
  47.9 9.3 %copy-start.12 = (f32[2,512]{1,0:T(2,128)S(1)}, f32[2,512]{1,0:T(2,128)}, u32[]{:S(2)}) copy-start(f32[2,512]{1,0:T(2,128)} %param.30) | copy-start | bytes 12292
  47.9 9.3 %copy-start.14 = (f32[512,8]{0,1:T(8,128)S(1)}, f32[512,8]{0,1:T(8,128)}, u32[]{:S(2)}) copy-start(f32[512,8]{0,1:T(8,128)} %param.32) | copy-start | bytes 49156
  47.9 9.3 %copy-start.15 = (f32[512]{0:T(512)S(1)}, f32[512]{0:T(512)}, u32[]{:S(2)}) copy-start(f32[512]{0:T(512)} %param.31) | copy-start | bytes 6148
  47.9 9.3 %copy-start.18 = (f32[253]{0:T(256)S(1)}, f32[253]{0:T(256)}, u32[]{:S(2)}) copy-start(f32[253]{0:T(256)} %constant.81) | copy-start | bytes 3040
  47.9 9.3 %copy-start.19 = (f32[253]{0:T(256)S(1)}, f32[253]{0:T(256)}, u32[]{:S(2)}) copy-start(f32[253]{0:T(256)} %constant.79) | copy-start | bytes 3040
  48.0 10.0 %copy-start.17 = (s32[12288]{0:T(1024)S(1)}, s32[12288]{0:T(1024)}, u32[]{:S(2)}) copy-start(s32[12288]{0:T(1024)} %constant.66.clone) | copy-start | bytes 147460
  48.0 20.7 %all-to-all-start.1 = ((bf16[4,16,80,128]{3,2,1,0:T(8,128)(2,1)}), bf16[4,16,80,128]{3,2,1,0:T(8,128)(2,1)S(1)}, u32[]{:S(2)}, u32[]{:S(2)}) async-start(bf16[4,16,80,128]{3,2,1,0:T(8,128)(2,1)} %broadcast_in_dim.37), calls=%async_computation.1 | async-start | bytes 2621440 | tf_op jit(solution)/shard_map/all_to_all | solution.py:52
  68.6 1.4 %copy-start.9 = (bf16[4,16,80,128]{3,2,1,0:T(8,128)(2,1)}, bf16[4,16,80,128]{3,2,1,0:T(8,128)(2,1)S(1)}, u32[]{:S(2)}) copy-start(bf16[4,16,80,128]{3,2,1,0:T(8,128)(2,1)S(1)} %all-to-all-done.1) | copy-start | bytes 3932164
  70.0 3.9 %copy-start.11 = (pred[96,128]{1,0:T(32,128)(4,1)S(1)}, pred[96,128]{1,0:T(32,128)(4,1)}, u32[]{:S(2)}) copy-start(pred[96,128]{1,0:T(32,128)(4,1)} %constant.68.clone) | copy-start | bytes 36868
  70.0 4.0 %copy-start.13 = (pred[128]{0:T(512)(128)(4,1)S(1)}, pred[128]{0:T(512)(128)(4,1)}, u32[]{:S(2)}) copy-start(pred[128]{0:T(512)(128)(4,1)} %constant.67.clone) | copy-start | bytes 388
  70.1 13.5 %all-to-all-start.2 = ((bf16[4,4,16,16,128]{4,3,2,1,0:T(8,128)(2,1)}), bf16[4,4,16,16,128]{4,3,2,1,0:T(8,128)(2,1)S(1)}, u32[]{:S(2)}, u32[]{:S(2)}) async-start(bf16[4,4,16,16,128]{4,3,2,1,0:T(8,128)(2,1)} %broadcast_in_dim.38), calls=%async_computation.2 | async-start | bytes 2097152 | tf_op jit(solution)/shard_map/all_to_all | solution.py:52
  83.6 1.2 slice-start
  87.9 11.5 %copy-start.16 = (f32[8]{0:T(128)S(1)}, f32[8]{0:T(128)}, u32[]{:S(2)}) copy-start(f32[8]{0:T(128)} %param.29) | copy-start | bytes 100
  87.9 13.6 %copy-start.3 = (f32[512]{0:T(512)S(1)}, f32[512]{0:T(512)}, u32[]{:S(2)}) copy-start(f32[512]{0:T(512)} %param.33) | copy-start | bytes 6148
  87.9 13.6 %copy-start.4 = (f32[512]{0:T(512)S(1)}, f32[512]{0:T(512)}, u32[]{:S(2)}) copy-start(f32[512]{0:T(512)} %param.34) | copy-start | bytes 6148
  87.9 13.6 %copy-start.7 = (bf16[384,288]{1,0:T(8,128)(2,1)S(1)}, bf16[384,288]{1,0:T(8,128)(2,1)}, u32[]{:S(2)}) copy-start(bf16[384,288]{1,0:T(8,128)(2,1)} %constant.69.clone.arrange_ref) | copy-start | bytes 663556
  87.9 36.3 %all-to-all-start.3 = ((bf16[4,4,16,64,128]{4,3,2,1,0:T(8,128)(2,1)}), bf16[4,4,16,64,128]{4,3,2,1,0:T(8,128)(2,1)}, u32[]{:S(2)}, u32[]{:S(2)}) async-start(bf16[4,4,16,64,128]{4,3,2,1,0:T(8,128)(2,1)} %broadcast_in_dim.66), calls=%async_computation.3 | async-start | bytes 8388608 | tf_op jit(solution)/shard_map/all_to_all | solution.py:52
  92.9 8.6 %collective-permute-start.5 = (bf16[16,16,16,128]{3,2,1,0:T(8,128)(2,1)S(1)}, bf16[16,16,16,128]{3,2,1,0:T(8,128)(2,1)S(1)}, u32[]{:S(2)}, u32[]{:S(2)}) collective-permute-start(bf16[16,16,16,128]{3,2,1,0:T(8,128)(2,1)S(1)} %bitcast.18), channel_id=1, source_target_pairs={{0,1},{1,0},{2,3},{3,2},{4,5},{5,4},{6,7},{7,6},{8,9},{9,8},{10,11... | collective-permute-start | bytes 3145736 | tf_op jit(solution)/shard_map/ppermute | solution.py:35
  101.5 32.5 %copy-start.1 = (f32[1024]{0:T(1024)S(1)}, f32[1024]{0:T(1024)}, u32[]{:S(2)}) copy-start(f32[1024]{0:T(1024)} %param.37) | copy-start | bytes 12292
  101.5 32.5 %copy-start.2 = (f32[1024]{0:T(1024)S(1)}, f32[1024]{0:T(1024)}, u32[]{:S(2)}) copy-start(f32[1024]{0:T(1024)} %param.38) | copy-start | bytes 12292
  101.5 32.5 %copy-start.5 = (f32[512]{0:T(512)S(1)}, f32[512]{0:T(512)}, u32[]{:S(2)}) copy-start(f32[512]{0:T(512)} %param.35) | copy-start | bytes 6148
  101.5 32.5 %copy-start.6 = (f32[512]{0:T(512)S(1)}, f32[512]{0:T(512)}, u32[]{:S(2)}) copy-start(f32[512]{0:T(512)} %param.36) | copy-start | bytes 6148
  123.4 0.8 copy-start.8
  124.2 9.8 %collective-permute-start.6 = (bf16[16,16,64,128]{3,2,1,0:T(8,128)(2,1)}, bf16[16,16,64,128]{3,2,1,0:T(8,128)(2,1)S(1)}, u32[]{:S(2)}, u32[]{:S(2)}) collective-permute-start(bf16[16,16,64,128]{3,2,1,0:T(8,128)(2,1)} %bitcast.9.mine_ref), channel_id=1, source_target_pairs={{0,1},{1,0},{2,3},{3,2},{4,5},{5,4},{6,7},{7,6},{8,9},{9,8},{10,11... | collective-permute-start | bytes 12582920 | tf_op jit(solution)/shard_map/ppermute | solution.py:35

commit v5 on v4

--- a/solution.py
+++ b/solution.py
@@ -47,8 +47,11 @@
     return np.concatenate([along_x, along_y]).tolist()
 
 
-def spread_ring(block, x_core):
-    copies = jnp.broadcast_to(block[None], (4,) + block.shape)
+def four(block):
+    return jnp.broadcast_to(block[None], (4,) + block.shape)
+
+
+def spread_ring(copies, x_core):
     return lax.all_to_all(copies, ALL, 0, 0, axis_index_groups=rings(x_core))
 
 
@@ -392,18 +395,11 @@
         ]
     )
 
-    east = shifted(patches[:, :SHIFT_COLS], LON, -1, True)
-    west = shifted(patches[:, 36 - SHIFT_COLS :], LON, 1, True)
-    wide = jnp.concatenate([west, patches, east], axis=1)
-    units, wide = lax.optimization_barrier((units, wide))
+    units, patches = lax.optimization_barrier((units, patches))
     along_z = spread(units, "z")
-    south = shifted(wide[:SHIFT_ROWS], LAT, -1, False)
-    north = shifted(wide[12 - SHIFT_ROWS :], LAT, 1, False)
-    tall = jnp.concatenate([north, wide, south], axis=0)
-
-    along_z, tall = lax.optimization_barrier((along_z, tall))
-    in_ring = spread_ring(along_z, 0)
-    attn_mine = spread_ring(in_ring[:, :, :16], 1).reshape(16, 16, 16, 128)
+    south = shifted(patches[:SHIFT_ROWS], LAT, -1, False)
+    north = shifted(patches[12 - SHIFT_ROWS :], LAT, 1, False)
+    strip = jnp.concatenate([north, patches, south], axis=0)
 
     table = bias_entries(
         bias_network_first_weight, bias_network_first_bias, bias_network_second_weight
@@ -424,9 +420,17 @@
     bias = jnp.where(seam[:, None, None, None] & jnp.asarray(apart), OFF, bias[None])
     head_scale = jnp.exp(jnp.minimum(head_scale_logarithm, jnp.log(100.0)))
 
-    attn_mine, in_ring, bias = lax.optimization_barrier((attn_mine, in_ring, bias))
+    along_z, strip, bias = lax.optimization_barrier((along_z, strip, bias))
+    in_ring = spread_ring(four(along_z), 0)
+    east = shifted(strip[:, :SHIFT_COLS], LON, -1, True)
+    west = shifted(strip[:, 36 - SHIFT_COLS :], LON, 1, True)
+    tall = jnp.concatenate([west, strip, east], axis=1)
+    in_ring, tall = lax.optimization_barrier((in_ring, tall))
+    attn_mine = spread_ring(four(in_ring[:, :, :16]), 1).reshape(16, 16, 16, 128)
+    rest_copies = four(in_ring[:, :, 16:])
+    attn_mine, rest_copies = lax.optimization_barrier((attn_mine, rest_copies))
     attn_other = shifted(attn_mine, "core", 1, True)
-    rest_mine = spread_ring(in_ring[:, :, 16:], 1).reshape(16, 16, 64, 128)
+    rest_mine = spread_ring(rest_copies, 1).reshape(16, 16, 64, 128)
 
     vmem = pl.BlockSpec(memory_space=pltpu.VMEM)
     smem = pl.BlockSpec(memory_space=pltpu.SMEM)

time: 142 us -> 135 us (0.951)
  waiting for transfers between devices: 39.5 us -> 29 us
  local copies, waits for them, and re-layouts: 12.7 us -> 14.6 us
    all_to_all x3, waiting for transfers between devices: 16.1 us -> 7.76 us  [spread_ring(): return lax.all_to_all(copies, ALL, 0, 0, axis_index_groups=rings(x_core))]
    all_to_all x3, starting transfers between devices: 18 us -> 13.4 us  [spread_ring(): return lax.all_to_all(copies, ALL, 0, 0, axis_index_groups=rings(x_core))]
    ppermute x7, starting transfers between devices: 26.9 us -> 30.7 us  [shifted(): return lax.ppermute(block, axes, pairs)]
    all_to_all x1, waiting for transfers between devices: 5.84 us -> 2.6 us  [spread(): lax.all_to_all(jnp.broadcast_to(block[None], (size,) + block.shape), axes...]
  transfers between devices with their start and end apart: 11 -> 11, of which waited for: 8 -> 8; matrix products, arithmetic and copies ran while one was open for 5% -> 8% of each run, Pallas kernels for 15% -> 16%
where the time goes in v5:
time: 135 us; the launch traced here: 134 us
  starting transfers between devices  53.7 us (40%)
  waiting for transfers between devices  29 us (21%)
  Pallas kernels  28.7 us (21%)
  local copies, waits for them, and re-layouts  14.6 us (11%)
  matrix products  5.38 us (4%)
  other arithmetic  2.08 us (2%)
    ppermute x7, starting transfers between devices, shifted(): return lax.ppermute(block, axes, pairs)  30.7 us
    pallas_call x1, Pallas kernels, local(): pl.pallas_call(attention_kernel, out_shape=jax.ShapeDtypeStruct((4 * QUAD...  21.8 us
    ppermute x7, waiting for transfers between devices, shifted(): return lax.ppermute(block, axes, pairs)  18.6 us
    all_to_all x3, starting transfers between devices, spread_ring(): return lax.all_to_all(copies, ALL, 0, 0, axis_index_groups=rings(x_core))  13.4 us
    all_to_all x1, starting transfers between devices, spread(): lax.all_to_all(jnp.broadcast_to(block[None], (size,) + block.shape), axes...  9.67 us
    all_to_all x3, waiting for transfers between devices, spread_ring(): return lax.all_to_all(copies, ALL, 0, 0, axis_index_groups=rings(x_core))  7.76 us
    pallas_call x1, Pallas kernels, local(): pl.pallas_call(feedforward_kernel, out_shape=jax.ShapeDtypeStruct((6, 18,...  6.94 us
    broadcast_in_dim x3, local copies, waits for them, and re-layouts, four(): return jnp.broadcast_to(block[None], (4,) + block.shape)  6.92 us
  transfers between devices with their start and end apart: 11, of which 8 were waited for; matrix products, arithmetic and copies ran while one was open for 8% of the time, Pallas kernels for 16%

profile of v5, /device:TPU:1, one launch (start us, length us, event | category | flops | bytes accessed | tf_op | source)
XLA Modules:
  0.0 134.1 jit_solution(12532319371198594917)
XLA Ops:
  0.0 0.8 constant_dynamic-update-slice_fusion.2
  0.8 0.7 constant_dynamic-update-slice_fusion.1
  1.5 0.8 constant_dynamic-update-slice_fusion
  2.2 8.8 %collective-permute-start = (bf16[8,4096]{1,0:T(8,128)(2,1)S(1)}, bf16[8,4096]{1,0:T(8,128)(2,1)S(1)}, u32[]{:S(2)}, u32[]{:S(2)}) collective-permute-start(bf16[8,4096]{1,0:T(8,128)(2,1)S(1)} %constant_dynamic-update-slice_fusion), channel_id=1, source_target_pairs={{0,1},{1,0},{2,3},{3,2},{4,5},{5,4},{6,7},{7,6},{8,9},{9,8},{10,11... | collective-permute-start | bytes 196616 | tf_op jit(solution)/shard_map/ppermute | solution.py:35
  11.0 0.8 fusion.23
  11.8 0.7 dynamic_slice.14
  12.5 1.4 %fusion.6 = f32[253,8]{0,1:T(8,128)S(1)} fusion(f32[512,8]{0,1:T(8,128)} %param.32, f32[512]{0:T(512)} %param.31, f32[512]{0:T(512)S(1)} %bitcast.28, f32[253]{0:T(256)} %constant.81, f32[512]{0:T(512)S(1)} %bitcast.27, f32[253]{0:T(256)} %constant.79), kind=kOutput, calls=%fused_computation.8 | convolution fusion | flops 13091232 | bytes 32648 | tf_op jit(solution)/shard_map/dot_general | solution.py:84
  14.0 0.0 collective-permute-done
  14.0 0.8 broadcast_in_dim.36
  14.8 9.7 %all-to-all-start = ((bf16[16,80,128]{2,1,0:T(8,128)(2,1)}), bf16[16,80,128]{2,1,0:T(8,128)(2,1)S(1)}, u32[]{:S(2)}, u32[]{:S(2)}) async-start(bf16[16,80,128]{2,1,0:T(8,128)(2,1)} %broadcast_in_dim.36), calls=%async_computation | async-start | bytes 655360 | tf_op jit(solution)/shard_map/all_to_all | solution.py:40
  24.5 0.0 copy-start.11
  24.5 4.0 %fusion.2 = f32[8,96,128]{2,0,1:T(8,128)S(1)} fusion(f32[253,8]{0,1:T(8,128)S(1)} %fusion.6, s32[12288]{0:T(1024)S(1)} %copy-done.15), kind=kOutput, calls=%fused_computation.3 | convolution fusion | flops 301559808 | bytes 450464 | tf_op jit(solution)/shard_map/dot_general | solution.py:413
  28.5 0.1 pad_add_fusion
  28.5 0.1 broadcast_and_fusion
  28.7 0.1 copy_select_fusion
  28.8 0.0 copy-done.11
  28.8 3.1 %collective-permute-start.1 = (bf16[3,36,512]{2,1,0:T(8,128)(2,1)S(1)}, bf16[3,36,512]{2,1,0:T(8,128)(2,1)S(1)}, u32[]{:S(2)}, u32[]{:S(2)}) collective-permute-start(bf16[3,36,512]{2,1,0:T(8,128)(2,1)S(1)} %get-tuple-element.29), channel_id=1, source_target_pairs={{0,64},{64,128},{128,192},{192,256},{256,320},{320,384},{384,448},... | collective-permute-start | bytes 331784 | tf_op jit(solution)/shard_map/ppermute | solution.py:35
  31.9 1.3 collective-permute-start.2
  33.2 0.1 broadcast_select_fusion.bias_ref
  33.4 1.0 collective-permute-done.1
  34.3 3.8 %collective-permute-done.2 = bf16[3,36,512]{2,1,0:T(8,128)(2,1)S(1)} collective-permute-done((bf16[3,36,512]{2,1,0:T(8,128)(2,1)S(1)}, bf16[3,36,512]{2,1,0:T(8,128)(2,1)S(1)}, u32[]{:S(2)}, u32[]{:S(2)}) %collective-permute-start.2) | collective-permute-done | bytes 110624 | tf_op jit(solution)/shard_map/ppermute | solution.py:35
  38.1 0.1 pad_maximum_fusion.1
  38.2 2.6 %all-to-all-done = bf16[16,80,128]{2,1,0:T(8,128)(2,1)S(1)} async-done(((bf16[16,80,128]{2,1,0:T(8,128)(2,1)}), bf16[16,80,128]{2,1,0:T(8,128)(2,1)S(1)}, u32[]{:S(2)}, u32[]{:S(2)}) %all-to-all-start) | async-done | bytes 327712 | tf_op jit(solution)/shard_map/all_to_all | solution.py:40
  40.8 1.2 broadcast_in_dim.64
  42.1 4.2 %all-to-all-start.1 = ((bf16[4,16,80,128]{3,2,1,0:T(8,128)(2,1)}), bf16[4,16,80,128]{3,2,1,0:T(8,128)(2,1)S(1)}, u32[]{:S(2)}, u32[]{:S(2)}) async-start(bf16[4,16,80,128]{3,2,1,0:T(8,128)(2,1)} %broadcast_in_dim.64), calls=%async_computation.1 | async-start | bytes 2621440 | tf_op jit(solution)/shard_map/all_to_all | solution.py:55
  46.3 8.7 %collective-permute-start.3 = (bf16[18,6,512]{2,1,0:T(8,128)(2,1)S(1)}, bf16[18,6,512]{2,1,0:T(8,128)(2,1)S(1)}, u32[]{:S(2)}, u32[]{:S(2)}) collective-permute-start(bf16[18,6,512]{2,1,0:T(8,128)(2,1)S(1)} %get-tuple-element.27), channel_id=1, source_target_pairs={{0,1},{1,2},{2,3},{3,4},{4,5},{5,6},{6,7},{7,8},{8,9},{9,10},{10,1... | collective-permute-start | bytes 331784 | tf_op jit(solution)/shard_map/ppermute | solution.py:35
  55.0 1.9 %collective-permute-start.4 = (bf16[18,6,512]{2,1,0:T(8,128)(2,1)S(1)}, bf16[18,6,512]{2,1,0:T(8,128)(2,1)S(1)}, u32[]{:S(2)}, u32[]{:S(2)}) collective-permute-start(bf16[18,6,512]{2,1,0:T(8,128)(2,1)S(1)} %get-tuple-element.28), channel_id=1, source_target_pairs={{0,63},{1,0},{2,1},{3,2},{4,3},{5,4},{6,5},{7,6},{8,7},{9,8},{10,9... | collective-permute-start | bytes 331784 | tf_op jit(solution)/shard_map/ppermute | solution.py:35
  57.0 0.2 collective-permute-done.3
  57.1 4.7 %collective-permute-done.4 = bf16[18,6,512]{2,1,0:T(8,128)(2,1)S(1)} collective-permute-done((bf16[18,6,512]{2,1,0:T(8,128)(2,1)S(1)}, bf16[18,6,512]{2,1,0:T(8,128)(2,1)S(1)}, u32[]{:S(2)}, u32[]{:S(2)}) %collective-permute-start.4) | collective-permute-done | bytes 110624 | tf_op jit(solution)/shard_map/ppermute | solution.py:35
  61.8 1.5 %pad_maximum_fusion.tall_ref = bf16[18,48,512]{2,1,0:T(8,128)(2,1)S(1)} fusion(bf16[18,6,512]{2,1,0:T(8,128)(2,1)S(1)} %collective-permute-done.4, bf16[18,36,512]{2,1,0:T(8,128)(2,1)} %copy-done.10, bf16[18,6,512]{2,1,0:T(8,128)(2,1)S(1)} %collective-permute-done.3), kind=kLoop, calls=%fused_computation.9 | loop fusion | flops 2654208 | bytes 1769472 | tf_op jit(solution)/shard_map/concatenate | solution.py:427
  63.3 0.0 all-to-all-done.1
  63.4 1.4 %broadcast_in_dim.65 = bf16[4,4,16,16,128]{4,3,2,1,0:T(8,128)(2,1)} broadcast(bf16[4,16,16,128]{3,2,1,0:T(8,128)(2,1)S(1)} %slice.38), dimensions={1,2,3,4} | broadcast | bytes 1310720 | tf_op jit(solution)/shard_map/broadcast_in_dim | solution.py:51
  64.7 4.2 %all-to-all-start.2 = ((bf16[4,4,16,16,128]{4,3,2,1,0:T(8,128)(2,1)}), bf16[4,4,16,16,128]{4,3,2,1,0:T(8,128)(2,1)S(1)}, u32[]{:S(2)}, u32[]{:S(2)}) async-start(bf16[4,4,16,16,128]{4,3,2,1,0:T(8,128)(2,1)} %broadcast_in_dim.65), calls=%async_computation.2 | async-start | bytes 2097152 | tf_op jit(solution)/shard_map/all_to_all | solution.py:55
  69.0 2.3 %slice.39 = bf16[4,16,64,128]{3,2,1,0:T(8,128)(2,1)} slice(bf16[4,16,80,128]{3,2,1,0:T(8,128)(2,1)} %copy-done.9), slice={[0:4], [0:16], [16:80], [0:128]} | slice | bytes 2097152 | tf_op jit(solution)/shard_map/slice | solution.py:430
  71.2 7.8 %all-to-all-done.2 = bf16[4,4,16,16,128]{4,3,2,1,0:T(8,128)(2,1)S(1)} async-done(((bf16[4,4,16,16,128]{4,3,2,1,0:T(8,128)(2,1)}), bf16[4,4,16,16,128]{4,3,2,1,0:T(8,128)(2,1)S(1)}, u32[]{:S(2)}, u32[]{:S(2)}) %all-to-all-start.2) | async-done | bytes 1048608 | tf_op jit(solution)/shard_map/all_to_all | solution.py:55
  79.0 4.3 %broadcast_in_dim.66 = bf16[4,4,16,64,128]{4,3,2,1,0:T(8,128)(2,1)} broadcast(bf16[4,16,64,128]{3,2,1,0:T(8,128)(2,1)} %slice.39), dimensions={1,2,3,4} | broadcast | bytes 5242880 | tf_op jit(solution)/shard_map/broadcast_in_dim | solution.py:51
  83.3 5.0 %all-to-all-start.3 = ((bf16[4,4,16,64,128]{4,3,2,1,0:T(8,128)(2,1)}), bf16[4,4,16,64,128]{4,3,2,1,0:T(8,128)(2,1)}, u32[]{:S(2)}, u32[]{:S(2)}) async-start(bf16[4,4,16,64,128]{4,3,2,1,0:T(8,128)(2,1)} %broadcast_in_dim.66), calls=%async_computation.3 | async-start | bytes 8388608 | tf_op jit(solution)/shard_map/all_to_all | solution.py:55
  88.3 4.0 %collective-permute-start.5 = (bf16[16,16,16,128]{3,2,1,0:T(8,128)(2,1)S(1)}, bf16[16,16,16,128]{3,2,1,0:T(8,128)(2,1)S(1)}, u32[]{:S(2)}, u32[]{:S(2)}) collective-permute-start(bf16[16,16,16,128]{3,2,1,0:T(8,128)(2,1)S(1)} %bitcast.18), channel_id=1, source_target_pairs={{0,1},{1,0},{2,3},{3,2},{4,5},{5,4},{6,7},{7,6},{8,9},{9,8},{10,11... | collective-permute-start | bytes 3145736 | tf_op jit(solution)/shard_map/ppermute | solution.py:35
  92.4 2.1 %collective-permute-done.5.other_ref = bf16[16,16,16,128]{3,2,1,0:T(8,128)(2,1)S(1)} collective-permute-done((bf16[16,16,16,128]{3,2,1,0:T(8,128)(2,1)S(1)}, bf16[16,16,16,128]{3,2,1,0:T(8,128)(2,1)S(1)}, u32[]{:S(2)}, u32[]{:S(2)}) %collective-permute-start.5) | collective-permute-done | bytes 1048608 | tf_op jit(solution)/shard_map/ppermute | solution.py:35
  94.5 0.0 copy-start.2
  94.5 0.0 copy-start.5
  94.5 0.0 copy-start.6
  94.5 21.8 %attention.1.first_ref = bf16[448,512]{1,0:T(8,128)(2,1)S(1)} custom-call(s32[1]{0:T(128)} %bitcast.core_ref, f32[8]{0:T(128)S(1)} %minimum_exponential_fusion.scale_ref, bf16[18,48,512]{2,1,0:T(8,128)(2,1)S(1)} %pad_maximum_fusion.tall_ref, f32[3,8,96,128]{3,2,1,0:T(8,128)S(1)} %broadcast_select_fusion.bias_ref, bf16[384,288]{1,0:T(8,128)(2,1)S(1)} %copy-done.7, ...), custom_call_target="tpu_custom_call" | custom-call | flops 20000000000 | bytes 20000000 | tf_op jit(solution)/shard_map/attention/pallas_call | solution.py:446
  116.3 0.8 copy-done.8
  117.1 0.0 all-to-all-done.3
  117.1 2.8 %collective-permute-start.6 = (bf16[16,16,64,128]{3,2,1,0:T(8,128)(2,1)}, bf16[16,16,64,128]{3,2,1,0:T(8,128)(2,1)S(1)}, u32[]{:S(2)}, u32[]{:S(2)}) collective-permute-start(bf16[16,16,64,128]{3,2,1,0:T(8,128)(2,1)} %bitcast.9.mine_ref), channel_id=1, source_target_pairs={{0,1},{1,0},{2,3},{3,2},{4,5},{5,4},{6,7},{7,6},{8,9},{9,8},{10,11... | collective-permute-start | bytes 12582920 | tf_op jit(solution)/shard_map/ppermute | solution.py:35
  120.0 7.0 %collective-permute-done.6.other_ref = bf16[16,16,64,128]{3,2,1,0:T(8,128)(2,1)S(1)} collective-permute-done((bf16[16,16,64,128]{3,2,1,0:T(8,128)(2,1)}, bf16[16,16,64,128]{3,2,1,0:T(8,128)(2,1)S(1)}, u32[]{:S(2)}, u32[]{:S(2)}) %collective-permute-start.6) | collective-permute-done | bytes 4194336 | tf_op jit(solution)/shard_map/ppermute | solution.py:35
  127.0 6.9 %feedforward.1 = bf16[6,18,1024]{2,1,0:T(8,128)(2,1)} custom-call(s32[1]{0:T(128)} %bitcast.core_ref, bf16[448,512]{1,0:T(8,128)(2,1)} %copy-done.8, f32[1,512]{1,0:T(1,128)S(1)} %bitcast.24, f32[1,512]{1,0:T(1,128)S(1)} %bitcast.25, f32[1,1024]{1,0:T(1,128)S(1)} %bitcast.20, f32[1,1024]{1,0:T(1,128)S(1)} %bitcast.21, ...), custom_call_target="tpu_custom_call" | custom-call | flops 6000000000 | bytes 20000000 | tf_op jit(solution)/shard_map/feedforward/pallas_call | solution.py:481
  (34 shorter events, 0.2 us)
Async XLA Ops:
  0.0 13.9 %copy-start = (bf16[32,1024]{1,0:T(8,128)(2,1)S(1)}, bf16[32,1024]{1,0:T(8,128)(2,1)}, u32[]{:S(2)}) copy-start(bf16[32,1024]{1,0:T(8,128)(2,1)} %param.28) | copy-start | bytes 196612
  0.0 24.5 %copy-start.15 = (s32[12288]{0:T(1024)S(1)}, s32[12288]{0:T(1024)}, u32[]{:S(2)}) copy-start(s32[12288]{0:T(1024)} %constant.66.clone) | copy-start | bytes 147460
  2.2 11.7 %collective-permute-start = (bf16[8,4096]{1,0:T(8,128)(2,1)S(1)}, bf16[8,4096]{1,0:T(8,128)(2,1)S(1)}, u32[]{:S(2)}, u32[]{:S(2)}) collective-permute-start(bf16[8,4096]{1,0:T(8,128)(2,1)S(1)} %constant_dynamic-update-slice_fusion), channel_id=1, source_target_pairs={{0,1},{1,0},{2,3},{3,2},{4,5},{5,4},{6,7},{7,6},{8,9},{9,8},{10,11... | collective-permute-start | bytes 196616 | tf_op jit(solution)/shard_map/ppermute | solution.py:35
  14.8 13.7 %copy-start.12 = (pred[96,128]{1,0:T(32,128)(4,1)S(1)}, pred[96,128]{1,0:T(32,128)(4,1)}, u32[]{:S(2)}) copy-start(pred[96,128]{1,0:T(32,128)(4,1)} %constant.68.clone) | copy-start | bytes 36868
  14.8 13.8 %copy-start.13 = (pred[128]{0:T(512)(128)(4,1)S(1)}, pred[128]{0:T(512)(128)(4,1)}, u32[]{:S(2)}) copy-start(pred[128]{0:T(512)(128)(4,1)} %constant.67.clone) | copy-start | bytes 388
  14.8 26.0 %all-to-all-start = ((bf16[16,80,128]{2,1,0:T(8,128)(2,1)}), bf16[16,80,128]{2,1,0:T(8,128)(2,1)S(1)}, u32[]{:S(2)}, u32[]{:S(2)}) async-start(bf16[16,80,128]{2,1,0:T(8,128)(2,1)} %broadcast_in_dim.36), calls=%async_computation | async-start | bytes 655360 | tf_op jit(solution)/shard_map/all_to_all | solution.py:40
  24.5 4.3 %copy-start.11 = (bf16[12,36,512]{2,1,0:T(8,128)(2,1)S(1)}, bf16[12,36,512]{2,1,0:T(8,128)(2,1)}, u32[]{:S(2)}) copy-start(bf16[12,36,512]{2,1,0:T(8,128)(2,1)} %param.23) | copy-start | bytes 1327108
  28.8 5.5 %collective-permute-start.1 = (bf16[3,36,512]{2,1,0:T(8,128)(2,1)S(1)}, bf16[3,36,512]{2,1,0:T(8,128)(2,1)S(1)}, u32[]{:S(2)}, u32[]{:S(2)}) collective-permute-start(bf16[3,36,512]{2,1,0:T(8,128)(2,1)S(1)} %get-tuple-element.29), channel_id=1, source_target_pairs={{0,64},{64,128},{128,192},{192,256},{256,320},{320,384},{384,448},... | collective-permute-start | bytes 331784 | tf_op jit(solution)/shard_map/ppermute | solution.py:35
  31.9 6.2 %collective-permute-start.2 = (bf16[3,36,512]{2,1,0:T(8,128)(2,1)S(1)}, bf16[3,36,512]{2,1,0:T(8,128)(2,1)S(1)}, u32[]{:S(2)}, u32[]{:S(2)}) collective-permute-start(bf16[3,36,512]{2,1,0:T(8,128)(2,1)S(1)} %get-tuple-element.30), channel_id=1, source_target_pairs={{64,0},{128,64},{192,128},{256,192},{320,256},{384,320},{448,384},... | collective-permute-start | bytes 331784 | tf_op jit(solution)/shard_map/ppermute | solution.py:35
  38.2 8.0 %copy-start.10 = (bf16[18,36,512]{2,1,0:T(8,128)(2,1)}, bf16[18,36,512]{2,1,0:T(8,128)(2,1)S(1)}, u32[]{:S(2)}) copy-start(bf16[18,36,512]{2,1,0:T(8,128)(2,1)S(1)} %pad_maximum_fusion.1) | copy-start | bytes 1990660
  42.1 21.3 %all-to-all-start.1 = ((bf16[4,16,80,128]{3,2,1,0:T(8,128)(2,1)}), bf16[4,16,80,128]{3,2,1,0:T(8,128)(2,1)S(1)}, u32[]{:S(2)}, u32[]{:S(2)}) async-start(bf16[4,16,80,128]{3,2,1,0:T(8,128)(2,1)} %broadcast_in_dim.64), calls=%async_computation.1 | async-start | bytes 2621440 | tf_op jit(solution)/shard_map/all_to_all | solution.py:55
  46.3 10.8 %collective-permute-start.3 = (bf16[18,6,512]{2,1,0:T(8,128)(2,1)S(1)}, bf16[18,6,512]{2,1,0:T(8,128)(2,1)S(1)}, u32[]{:S(2)}, u32[]{:S(2)}) collective-permute-start(bf16[18,6,512]{2,1,0:T(8,128)(2,1)S(1)} %get-tuple-element.27), channel_id=1, source_target_pairs={{0,1},{1,2},{2,3},{3,4},{4,5},{5,6},{6,7},{7,8},{8,9},{9,10},{10,1... | collective-permute-start | bytes 331784 | tf_op jit(solution)/shard_map/ppermute | solution.py:35
  55.0 6.8 %collective-permute-start.4 = (bf16[18,6,512]{2,1,0:T(8,128)(2,1)S(1)}, bf16[18,6,512]{2,1,0:T(8,128)(2,1)S(1)}, u32[]{:S(2)}, u32[]{:S(2)}) collective-permute-start(bf16[18,6,512]{2,1,0:T(8,128)(2,1)S(1)} %get-tuple-element.28), channel_id=1, source_target_pairs={{0,63},{1,0},{2,1},{3,2},{4,3},{5,4},{6,5},{7,6},{8,7},{9,8},{10,9... | collective-permute-start | bytes 331784 | tf_op jit(solution)/shard_map/ppermute | solution.py:35
  63.3 1.4 %copy-start.9 = (bf16[4,16,80,128]{3,2,1,0:T(8,128)(2,1)}, bf16[4,16,80,128]{3,2,1,0:T(8,128)(2,1)S(1)}, u32[]{:S(2)}) copy-start(bf16[4,16,80,128]{3,2,1,0:T(8,128)(2,1)S(1)} %all-to-all-done.1) | copy-start | bytes 3932164
  64.7 14.3 %all-to-all-start.2 = ((bf16[4,4,16,16,128]{4,3,2,1,0:T(8,128)(2,1)}), bf16[4,4,16,16,128]{4,3,2,1,0:T(8,128)(2,1)S(1)}, u32[]{:S(2)}, u32[]{:S(2)}) async-start(bf16[4,4,16,16,128]{4,3,2,1,0:T(8,128)(2,1)} %broadcast_in_dim.65), calls=%async_computation.2 | async-start | bytes 2097152 | tf_op jit(solution)/shard_map/all_to_all | solution.py:55
  83.3 9.0 %copy-start.14 = (f32[8]{0:T(128)S(1)}, f32[8]{0:T(128)}, u32[]{:S(2)}) copy-start(f32[8]{0:T(128)} %param.29) | copy-start | bytes 100
  83.3 11.1 %copy-start.3 = (f32[512]{0:T(512)S(1)}, f32[512]{0:T(512)}, u32[]{:S(2)}) copy-start(f32[512]{0:T(512)} %param.33) | copy-start | bytes 6148
  83.3 11.1 %copy-start.4 = (f32[512]{0:T(512)S(1)}, f32[512]{0:T(512)}, u32[]{:S(2)}) copy-start(f32[512]{0:T(512)} %param.34) | copy-start | bytes 6148
  83.3 11.1 %copy-start.7 = (bf16[384,288]{1,0:T(8,128)(2,1)S(1)}, bf16[384,288]{1,0:T(8,128)(2,1)}, u32[]{:S(2)}) copy-start(bf16[384,288]{1,0:T(8,128)(2,1)} %constant.69.clone.arrange_ref) | copy-start | bytes 663556
  83.3 33.8 %all-to-all-start.3 = ((bf16[4,4,16,64,128]{4,3,2,1,0:T(8,128)(2,1)}), bf16[4,4,16,64,128]{4,3,2,1,0:T(8,128)(2,1)}, u32[]{:S(2)}, u32[]{:S(2)}) async-start(bf16[4,4,16,64,128]{4,3,2,1,0:T(8,128)(2,1)} %broadcast_in_dim.66), calls=%async_computation.3 | async-start | bytes 8388608 | tf_op jit(solution)/shard_map/all_to_all | solution.py:55
  88.3 6.1 %collective-permute-start.5 = (bf16[16,16,16,128]{3,2,1,0:T(8,128)(2,1)S(1)}, bf16[16,16,16,128]{3,2,1,0:T(8,128)(2,1)S(1)}, u32[]{:S(2)}, u32[]{:S(2)}) collective-permute-start(bf16[16,16,16,128]{3,2,1,0:T(8,128)(2,1)S(1)} %bitcast.18), channel_id=1, source_target_pairs={{0,1},{1,0},{2,3},{3,2},{4,5},{5,4},{6,7},{7,6},{8,9},{9,8},{10,11... | collective-permute-start | bytes 3145736 | tf_op jit(solution)/shard_map/ppermute | solution.py:35
  94.4 32.5 %copy-start.1 = (f32[1024]{0:T(1024)S(1)}, f32[1024]{0:T(1024)}, u32[]{:S(2)}) copy-start(f32[1024]{0:T(1024)} %param.37) | copy-start | bytes 12292
  94.5 32.5 %copy-start.2 = (f32[1024]{0:T(1024)S(1)}, f32[1024]{0:T(1024)}, u32[]{:S(2)}) copy-start(f32[1024]{0:T(1024)} %param.38) | copy-start | bytes 12292
  94.5 32.5 %copy-start.5 = (f32[512]{0:T(512)S(1)}, f32[512]{0:T(512)}, u32[]{:S(2)}) copy-start(f32[512]{0:T(512)} %param.35) | copy-start | bytes 6148
  94.5 32.5 %copy-start.6 = (f32[512]{0:T(512)S(1)}, f32[512]{0:T(512)}, u32[]{:S(2)}) copy-start(f32[512]{0:T(512)} %param.36) | copy-start | bytes 6148
  116.3 0.8 copy-start.8
  117.1 9.8 %collective-permute-start.6 = (bf16[16,16,64,128]{3,2,1,0:T(8,128)(2,1)}, bf16[16,16,64,128]{3,2,1,0:T(8,128)(2,1)S(1)}, u32[]{:S(2)}, u32[]{:S(2)}) collective-permute-start(bf16[16,16,64,128]{3,2,1,0:T(8,128)(2,1)} %bitcast.9.mine_ref), channel_id=1, source_target_pairs={{0,1},{1,0},{2,3},{3,2},{4,5},{5,4},{6,7},{7,6},{8,9},{9,8},{10,11... | collective-permute-start | bytes 12582920 | tf_op jit(solution)/shard_map/ppermute | solution.py:35

commit v6 on v5

--- a/solution.py
+++ b/solution.py
@@ -53,6 +53,20 @@
 
 def spread_ring(copies, x_core):
     return lax.all_to_all(copies, ALL, 0, 0, axis_index_groups=rings(x_core))
+
+
+def ring_shift(block, x_core, by):
+    pairs = [(ring[i], ring[(i + by) % 4]) for ring in rings(x_core) for i in range(4)]
+    return lax.ppermute(block, ALL, pairs)
+
+
+def place_by(step, inner, of, x, y):
+    outer = ((1 - of) * y + of * x + 4 - step) & 3
+
+    def pick(on_first, on_second):
+        return on_first + of * (on_second - on_first)
+
+    return pick(outer >> 1, inner // 2), pick(inner, outer), pick(outer & 1, inner % 2)
 
 
 def place(m, of):
@@ -195,14 +209,20 @@
 
         def window(w, _, band=band, first=first, count=count, done=done):
             base = pl.multiple_of(w * WIN_PAD, WIN_PAD)
+            all_scores = []
             for pair in range(HEAD_COUNT // 2):
                 cut = slice(pair * 128, pair * 128 + 128)
                 query = queries[pl.ds(base + first, count), cut]
                 key = both(keys[pl.ds(base, WIN_PAD), cut])
+                all_scores.append(
+                    lax.dot_general(
+                        query, key, (((1,), (1,)), ((), ())), preferred_element_type=F32
+                    )
+                )
+            for pair in range(HEAD_COUNT // 2):
+                cut = slice(pair * 128, pair * 128 + 128)
                 value = both(values[pl.ds(base, WIN_PAD), cut])
-                scores = lax.dot_general(
-                    query, key, (((1,), (1,)), ((), ())), preferred_element_type=F32
-                )
+                scores = all_scores[pair]
                 expo = []
                 for h in range(2):
                     head = pair * 2 + h
@@ -219,7 +239,7 @@
                 heads[pl.ds(place, count), cut] = (mixed[:, :128] / mixed[:, 128:]).astype(BF16)
             return 0
 
-        lax.fori_loop(0, WINS, window, 0)
+        lax.fori_loop(0, WINS, window, 0, unroll=True)
         done += WINS * count
 
     for copy in late:
@@ -234,55 +254,47 @@
 
 
 def feedforward_kernel(
-    core_ref,
-    first_ref,
-    gain_ref,
-    offset_ref,
-    merge_gain_ref,
-    merge_offset_ref,
-    mine_ref,
-    other_ref,
-    out_ref,
-    up,
-    down,
-    merge,
-    tokens_in,
-    up_sems,
-    down_sems,
-    merge_sems,
+    where_ref, first_ref, gain_ref, offset_ref, merge_gain_ref, merge_offset_ref, *refs
 ):
-    core = core_ref[0]
+    pieces, (out_ref, up, down, merge, tokens_in, up_sems, down_sems, merge_sems) = refs[:10], refs[10:]
+    core, me_x, me_y = where_ref[0], where_ref[1], where_ref[2]
     ups, downs, merges = [], [], []
-    for m in range(16):
-        for part, (ref, of) in enumerate(((mine_ref, core), (other_ref, 1 - core))):
-            y_hi, x, y_lo = place(m, of)
-            row = pl.multiple_of(y_lo * 16, 16)
-            column = pl.multiple_of((y_hi * 8 + x * 2 + of) * 128, 128)
-            ups.append(
-                pltpu.make_async_copy(
-                    ref.at[m, :, pl.ds(0, 16), :],
-                    up.at[:, pl.ds(row, 16), pl.ds(column, 128)],
-                    up_sems.at[m * 2 + part],
+    for step in range(4):
+        for inner in range(4):
+            for part, of in enumerate((core, 1 - core)):
+                if step == 2:
+                    ref = pieces[6 + inner // 2 * 2 + part].at[inner % 2]
+                else:
+                    ref = pieces[(step + 1) // 2 * 2 + part].at[inner]
+                at = (step * 4 + inner) * 2 + part
+                y_hi, x, y_lo = place_by(step, inner, of, me_x, me_y)
+                row = pl.multiple_of(y_lo * 16, 16)
+                column = pl.multiple_of((y_hi * 8 + x * 2 + of) * 128, 128)
+                ups.append(
+                    pltpu.make_async_copy(
+                        ref.at[:, pl.ds(0, 16), :],
+                        up.at[:, pl.ds(row, 16), pl.ds(column, 128)],
+                        up_sems.at[at],
+                    )
                 )
-            )
-            row = pl.multiple_of(y_lo * 64 + of * 32 + y_hi * 16, 16)
-            column = pl.multiple_of(x * 128, 128)
-            downs.append(
-                pltpu.make_async_copy(
-                    ref.at[m, :, pl.ds(16, 16), :],
-                    down.at[:, pl.ds(row, 16), pl.ds(column, 128)],
-                    down_sems.at[m * 2 + part],
+                row = pl.multiple_of(y_lo * 64 + of * 32 + y_hi * 16, 16)
+                column = pl.multiple_of(x * 128, 128)
+                downs.append(
+                    pltpu.make_async_copy(
+                        ref.at[:, pl.ds(16, 16), :],
+                        down.at[:, pl.ds(row, 16), pl.ds(column, 128)],
+                        down_sems.at[at],
+                    )
                 )
-            )
-            row = pl.multiple_of(y_lo * 64 + of * 32, 32)
-            column = pl.multiple_of((y_hi * 4 + x) * 128, 128)
-            merges.append(
-                pltpu.make_async_copy(
-                    ref.at[m, :, pl.ds(32, 32), :],
-                    merge.at[:, pl.ds(row, 32), pl.ds(column, 128)],
-                    merge_sems.at[m * 2 + part],
+                row = pl.multiple_of(y_lo * 64 + of * 32, 32)
+                column = pl.multiple_of((y_hi * 4 + x) * 128, 128)
+                merges.append(
+                    pltpu.make_async_copy(
+                        ref.at[:, pl.ds(32, 32), :],
+                        merge.at[:, pl.ds(row, 32), pl.ds(column, 128)],
+                        merge_sems.at[at],
+                    )
                 )
-            )
     ups.append(pltpu.make_async_copy(first_ref, tokens_in, up_sems.at[32]))
     for copy in ups + downs + merges:
         copy.start()
@@ -426,11 +438,14 @@
     west = shifted(strip[:, 36 - SHIFT_COLS :], LON, 1, True)
     tall = jnp.concatenate([west, strip, east], axis=1)
     in_ring, tall = lax.optimization_barrier((in_ring, tall))
-    attn_mine = spread_ring(four(in_ring[:, :, :16]), 1).reshape(16, 16, 16, 128)
-    rest_copies = four(in_ring[:, :, 16:])
-    attn_mine, rest_copies = lax.optimization_barrier((attn_mine, rest_copies))
+    attn_copies, rest = lax.optimization_barrier((four(in_ring[:, :, :16]), in_ring[:, :, 16:]))
+    attn_mine = spread_ring(attn_copies, 1).reshape(16, 16, 16, 128)
+    rest_other = shifted(rest, "core", 1, True)
+    one, three = ring_shift(rest, 1, 1), ring_shift(rest, 1, 3)
+    attn_mine, rest_other, one, three = lax.optimization_barrier((attn_mine, rest_other, one, three))
     attn_other = shifted(attn_mine, "core", 1, True)
-    rest_mine = spread_ring(rest_copies, 1).reshape(16, 16, 64, 128)
+    two_low, two_high = ring_shift(one[:2], 1, 1), ring_shift(three[2:], 1, 3)
+    one_other, three_other = shifted(one, "core", 1, True), shifted(three, "core", 1, True)
 
     vmem = pl.BlockSpec(memory_space=pltpu.VMEM)
     smem = pl.BlockSpec(memory_space=pltpu.SMEM)
@@ -476,12 +491,13 @@
         attn_mine,
         attn_other,
     )
-    first, rest_mine = lax.optimization_barrier((first, rest_mine))
-    rest_other = shifted(rest_mine, "core", 1, True)
+    first, two_low, two_high = lax.optimization_barrier((first, two_low, two_high))
+    pieces = [rest, far(rest_other), one, one_other, three, three_other, two_low]
+    pieces += [shifted(two_low, "core", 1, True), two_high, shifted(two_high, "core", 1, True)]
     return pl.pallas_call(
         feedforward_kernel,
         out_shape=jax.ShapeDtypeStruct((6, 18, 2 * D), BF16),
-        in_specs=[smem, hbm] + [vmem] * 4 + [anywhere] * 2,
+        in_specs=[smem, hbm] + [vmem] * 4 + [anywhere] * 10,
         out_specs=vmem,
         scratch_shapes=[
             pltpu.VMEM((16, 32, FFN), BF16),
@@ -498,14 +514,13 @@
         ),
         name="feedforward",
     )(
-        core_index,
+        jnp.stack([core, x, lax.axis_index(("y_hi", "y_lo"))]).astype(jnp.int32),
         far(first),
         feedforward_norm_gain.reshape(1, D),
         feedforward_norm_offset.reshape(1, D),
         merging_norm_gain.reshape(1, 2 * D),
         merging_norm_offset.reshape(1, 2 * D),
-        rest_mine,
-        rest_other,
+        *pieces,
     )
 
 

time: 135 us -> 137 us (1.015)
  blocking collectives: 0 us -> 17.3 us
  waiting for transfers between devices: 29 us -> 14.1 us
  starting transfers between devices: 53.7 us -> 67.1 us
  Pallas kernels: 28.7 us -> 18.9 us
  local copies, waits for them, and re-layouts: 14.6 us -> 11.3 us
    all_to_all x0 -> x1, blocking collectives: none -> 17.3 us  [spread_ring(): return lax.all_to_all(copies, ALL, 0, 0, axis_index_groups=rings(x_core))]
    ppermute x0 -> x4, starting transfers between devices: none -> 12 us  [ring_shift(): return lax.ppermute(block, ALL, pairs)]
    pallas_call x1, Pallas kernels: 21.8 us -> 11.1 us  [local(): pl.pallas_call(attention_kernel, out_shape=jax.ShapeDtypeStruct((4 * QUAD...]
    ppermute x7 -> x11, starting transfers between devices: 30.7 us -> 41.3 us  [shifted(): return lax.ppermute(block, axes, pairs)]
    all_to_all x3 -> x1, starting transfers between devices: 13.4 us -> 4.29 us  [spread_ring(): return lax.all_to_all(copies, ALL, 0, 0, axis_index_groups=rings(x_core))]
    all_to_all x3 -> x1, waiting for transfers between devices: 7.76 us -> 0.01 us  [spread_ring(): return lax.all_to_all(copies, ALL, 0, 0, axis_index_groups=rings(x_core))]
    ppermute x7 -> x11, waiting for transfers between devices: 18.6 us -> 11.5 us  [shifted(): return lax.ppermute(block, axes, pairs)]
    broadcast_in_dim x3 -> x2, local copies, waits for them, and re-layouts: 6.92 us -> 1.45 us  [four(): return jnp.broadcast_to(block[None], (4,) + block.shape)]
  transfers between devices with their start and end apart: 11 -> 17, of which waited for: 8 -> 6; matrix products, arithmetic and copies ran while one was open for 8% -> 7% of each run, Pallas kernels for 16% -> 8%
where the time goes in v6:
time: 137 us; the launch traced here: 136 us
  starting transfers between devices  67.1 us (49%)
  Pallas kernels  18.9 us (14%)
  blocking collectives  17.3 us (13%)
  waiting for transfers between devices  14.1 us (10%)
  local copies, waits for them, and re-layouts  11.3 us (8%)
  matrix products  5.38 us (4%)
    ppermute x11, starting transfers between devices, shifted(): return lax.ppermute(block, axes, pairs)  41.3 us
    all_to_all x1, blocking collectives, spread_ring(): return lax.all_to_all(copies, ALL, 0, 0, axis_index_groups=rings(x_core))  17.3 us
    ppermute x4, starting transfers between devices, ring_shift(): return lax.ppermute(block, ALL, pairs)  12 us
    ppermute x11, waiting for transfers between devices, shifted(): return lax.ppermute(block, axes, pairs)  11.5 us
    pallas_call x1, Pallas kernels, local(): pl.pallas_call(attention_kernel, out_shape=jax.ShapeDtypeStruct((4 * QUAD...  11.1 us
    all_to_all x1, starting transfers between devices, spread(): lax.all_to_all(jnp.broadcast_to(block[None], (size,) + block.shape), axes...  9.54 us
    pallas_call x1, Pallas kernels, local(): pl.pallas_call(feedforward_kernel, out_shape=jax.ShapeDtypeStruct((6, 18,...  7.81 us
    all_to_all x1, starting transfers between devices, spread_ring(): return lax.all_to_all(copies, ALL, 0, 0, axis_index_groups=rings(x_core))  4.29 us
  transfers between devices with their start and end apart: 17, of which 6 were waited for; matrix products, arithmetic and copies ran while one was open for 7% of the time, Pallas kernels for 8%

profile of v6, /device:TPU:1, one launch (start us, length us, event | category | flops | bytes accessed | tf_op | source)
XLA Modules:
  0.0 135.8 jit_solution(14734131279815510001)
XLA Ops:
  0.0 0.8 constant_dynamic-update-slice_fusion.2
  0.8 0.7 constant_dynamic-update-slice_fusion.1
  1.5 0.8 constant_dynamic-update-slice_fusion
  2.2 8.8 %collective-permute-start = (bf16[8,4096]{1,0:T(8,128)(2,1)S(1)}, bf16[8,4096]{1,0:T(8,128)(2,1)S(1)}, u32[]{:S(2)}, u32[]{:S(2)}) collective-permute-start(bf16[8,4096]{1,0:T(8,128)(2,1)S(1)} %constant_dynamic-update-slice_fusion), channel_id=1, source_target_pairs={{0,1},{1,0},{2,3},{3,2},{4,5},{5,4},{6,7},{7,6},{8,9},{9,8},{10,11... | collective-permute-start | bytes 196616 | tf_op jit(solution)/shard_map/ppermute | solution.py:35
  11.0 0.8 fusion.23
  11.8 0.7 dynamic_slice.14
  12.5 1.4 %fusion.6 = f32[253,8]{0,1:T(8,128)S(1)} fusion(f32[512,8]{0,1:T(8,128)} %param.32, f32[512]{0:T(512)} %param.31, f32[512]{0:T(512)S(1)} %bitcast.29, f32[253]{0:T(256)} %constant.83, f32[512]{0:T(512)S(1)} %bitcast.28, f32[253]{0:T(256)} %constant.81), kind=kOutput, calls=%fused_computation.8 | convolution fusion | flops 13091232 | bytes 32648 | tf_op jit(solution)/shard_map/dot_general | solution.py:98
  14.0 0.8 broadcast_in_dim.34
  14.8 9.5 %all-to-all-start = ((bf16[16,80,128]{2,1,0:T(8,128)(2,1)}), bf16[16,80,128]{2,1,0:T(8,128)(2,1)S(1)}, u32[]{:S(2)}, u32[]{:S(2)}) async-start(bf16[16,80,128]{2,1,0:T(8,128)(2,1)} %broadcast_in_dim.34), calls=%async_computation | async-start | bytes 655360 | tf_op jit(solution)/shard_map/all_to_all | solution.py:40
  24.4 4.0 %fusion.2 = f32[8,96,128]{2,0,1:T(8,128)S(1)} fusion(f32[253,8]{0,1:T(8,128)S(1)} %fusion.6, s32[12288]{0:T(1024)S(1)} %copy-done.14), kind=kOutput, calls=%fused_computation.3 | convolution fusion | flops 301559808 | bytes 450464 | tf_op jit(solution)/shard_map/dot_general | solution.py:425
  28.3 0.1 pad_add_fusion
  28.4 0.1 broadcast_and_fusion
  28.5 0.1 copy_select_fusion
  28.7 3.1 %collective-permute-start.1 = (bf16[3,36,512]{2,1,0:T(8,128)(2,1)S(1)}, bf16[3,36,512]{2,1,0:T(8,128)(2,1)S(1)}, u32[]{:S(2)}, u32[]{:S(2)}) collective-permute-start(bf16[3,36,512]{2,1,0:T(8,128)(2,1)S(1)} %get-tuple-element.39), channel_id=1, source_target_pairs={{0,64},{64,128},{128,192},{192,256},{256,320},{320,384},{384,448},... | collective-permute-start | bytes 331784 | tf_op jit(solution)/shard_map/ppermute | solution.py:35
  31.8 1.3 collective-permute-start.2
  33.1 0.1 broadcast_select_fusion.bias_ref
  33.2 1.0 collective-permute-done.1
  34.2 3.8 %collective-permute-done.2 = bf16[3,36,512]{2,1,0:T(8,128)(2,1)S(1)} collective-permute-done((bf16[3,36,512]{2,1,0:T(8,128)(2,1)S(1)}, bf16[3,36,512]{2,1,0:T(8,128)(2,1)S(1)}, u32[]{:S(2)}, u32[]{:S(2)}) %collective-permute-start.2) | collective-permute-done | bytes 110624 | tf_op jit(solution)/shard_map/ppermute | solution.py:35
  38.0 0.1 pad_maximum_fusion.1
  38.1 2.6 %all-to-all-done = bf16[16,80,128]{2,1,0:T(8,128)(2,1)S(1)} async-done(((bf16[16,80,128]{2,1,0:T(8,128)(2,1)}), bf16[16,80,128]{2,1,0:T(8,128)(2,1)S(1)}, u32[]{:S(2)}, u32[]{:S(2)}) %all-to-all-start) | async-done | bytes 327712 | tf_op jit(solution)/shard_map/all_to_all | solution.py:40
  40.7 1.3 broadcast_in_dim.58
  41.9 4.3 %all-to-all-start.1 = ((bf16[4,16,80,128]{3,2,1,0:T(8,128)(2,1)}), bf16[4,16,80,128]{3,2,1,0:T(8,128)(2,1)}, u32[]{:S(2)}, u32[]{:S(2)}) async-start(bf16[4,16,80,128]{3,2,1,0:T(8,128)(2,1)} %broadcast_in_dim.58), calls=%async_computation.1 | async-start | bytes 2621440 | tf_op jit(solution)/shard_map/all_to_all | solution.py:55
  46.3 8.6 %collective-permute-start.3 = (bf16[18,6,512]{2,1,0:T(8,128)(2,1)S(1)}, bf16[18,6,512]{2,1,0:T(8,128)(2,1)S(1)}, u32[]{:S(2)}, u32[]{:S(2)}) collective-permute-start(bf16[18,6,512]{2,1,0:T(8,128)(2,1)S(1)} %get-tuple-element.37), channel_id=1, source_target_pairs={{0,1},{1,2},{2,3},{3,4},{4,5},{5,6},{6,7},{7,8},{8,9},{9,10},{10,1... | collective-permute-start | bytes 331784 | tf_op jit(solution)/shard_map/ppermute | solution.py:35
  54.9 1.9 %collective-permute-start.4 = (bf16[18,6,512]{2,1,0:T(8,128)(2,1)S(1)}, bf16[18,6,512]{2,1,0:T(8,128)(2,1)S(1)}, u32[]{:S(2)}, u32[]{:S(2)}) collective-permute-start(bf16[18,6,512]{2,1,0:T(8,128)(2,1)S(1)} %get-tuple-element.38), channel_id=1, source_target_pairs={{0,63},{1,0},{2,1},{3,2},{4,3},{5,4},{6,5},{7,6},{8,7},{9,8},{10,9... | collective-permute-start | bytes 331784 | tf_op jit(solution)/shard_map/ppermute | solution.py:35
  56.8 0.2 collective-permute-done.3
  57.0 4.8 %collective-permute-done.4 = bf16[18,6,512]{2,1,0:T(8,128)(2,1)S(1)} collective-permute-done((bf16[18,6,512]{2,1,0:T(8,128)(2,1)S(1)}, bf16[18,6,512]{2,1,0:T(8,128)(2,1)S(1)}, u32[]{:S(2)}, u32[]{:S(2)}) %collective-permute-start.4) | collective-permute-done | bytes 110624 | tf_op jit(solution)/shard_map/ppermute | solution.py:35
  61.8 0.4 pad_maximum_fusion.tall_ref
  62.2 1.0 slice.44
  63.2 1.3 slice.45.refs_0_
  64.5 0.2 broadcast_in_dim.59
  64.7 3.8 %collective-permute-start.5 = (bf16[4,16,64,128]{3,2,1,0:T(8,128)(2,1)S(1)}, bf16[4,16,64,128]{3,2,1,0:T(8,128)(2,1)S(1)}, u32[]{:S(2)}, u32[]{:S(2)}) collective-permute-start(bf16[4,16,64,128]{3,2,1,0:T(8,128)(2,1)S(1)} %slice.45.refs_0_), channel_id=1, source_target_pairs={{0,1},{1,0},{2,3},{3,2},{4,5},{5,4},{6,7},{7,6},{8,9},{9,8},{10,11... | collective-permute-start | bytes 3145736 | tf_op jit(solution)/shard_map/ppermute | solution.py:35
  68.6 2.2 %collective-permute-start.6 = (bf16[4,16,64,128]{3,2,1,0:T(8,128)(2,1)S(1)}, bf16[4,16,64,128]{3,2,1,0:T(8,128)(2,1)}, u32[]{:S(2)}, u32[]{:S(2)}) collective-permute-start(bf16[4,16,64,128]{3,2,1,0:T(8,128)(2,1)S(1)} %slice.45.refs_0_), channel_id=1, source_target_pairs={{1,65},{65,129},{129,193},{193,1},{3,67},{67,131},{131,195},{195,3... | collective-permute-start | bytes 3145736 | tf_op jit(solution)/shard_map/ppermute | solution.py:60
  70.8 4.3 %collective-permute-start.7 = (bf16[4,16,64,128]{3,2,1,0:T(8,128)(2,1)S(1)}, bf16[4,16,64,128]{3,2,1,0:T(8,128)(2,1)}, u32[]{:S(2)}, u32[]{:S(2)}) collective-permute-start(bf16[4,16,64,128]{3,2,1,0:T(8,128)(2,1)S(1)} %slice.45.refs_0_), channel_id=1, source_target_pairs={{1,193},{65,1},{129,65},{193,129},{3,195},{67,3},{131,67},{195,131... | collective-permute-start | bytes 3145736 | tf_op jit(solution)/shard_map/ppermute | solution.py:60
  75.1 17.3 %all_to_all.15 = bf16[4,4,16,16,128]{4,3,2,1,0:T(8,128)(2,1)S(1)} all-to-all(bf16[4,4,16,16,128]{4,3,2,1,0:T(8,128)(2,1)S(1)} %broadcast_in_dim.59), channel_id=1, replica_groups={{1,65,129,193},{3,67,131,195},{5,69,133,197},{7,71,135,199},{9,73,137,2..., dimensions={0} | all-to-all | bytes 2097152 | tf_op jit(solution)/shard_map/all_to_all | solution.py:55
  92.5 3.7 %collective-permute-start.8 = (bf16[16,16,16,128]{3,2,1,0:T(8,128)(2,1)S(1)}, bf16[16,16,16,128]{3,2,1,0:T(8,128)(2,1)S(1)}, u32[]{:S(2)}, u32[]{:S(2)}) collective-permute-start(bf16[16,16,16,128]{3,2,1,0:T(8,128)(2,1)S(1)} %bitcast.19), channel_id=1, source_target_pairs={{0,1},{1,0},{2,3},{3,2},{4,5},{5,4},{6,7},{7,6},{8,9},{9,8},{10,11... | collective-permute-start | bytes 3145736 | tf_op jit(solution)/shard_map/ppermute | solution.py:35
  96.1 1.1 slice.46
  97.2 1.9 %collective-permute-start.11 = (bf16[4,16,64,128]{3,2,1,0:T(8,128)(2,1)}, bf16[4,16,64,128]{3,2,1,0:T(8,128)(2,1)}, u32[]{:S(2)}, u32[]{:S(2)}) collective-permute-start(bf16[4,16,64,128]{3,2,1,0:T(8,128)(2,1)} %collective-permute-done.6.refs_2_), channel_id=1, source_target_pairs={{0,1},{1,0},{2,3},{3,2},{4,5},{5,4},{6,7},{7,6},{8,9},{9,8},{10,11... | collective-permute-start | bytes 3145736 | tf_op jit(solution)/shard_map/ppermute | solution.py:35
  99.2 1.1 slice.47
  100.2 2.4 %collective-permute-start.12 = (bf16[4,16,64,128]{3,2,1,0:T(8,128)(2,1)}, bf16[4,16,64,128]{3,2,1,0:T(8,128)(2,1)}, u32[]{:S(2)}, u32[]{:S(2)}) collective-permute-start(bf16[4,16,64,128]{3,2,1,0:T(8,128)(2,1)} %collective-permute-done.7.refs_4_), channel_id=1, source_target_pairs={{0,1},{1,0},{2,3},{3,2},{4,5},{5,4},{6,7},{7,6},{8,9},{9,8},{10,11... | collective-permute-start | bytes 3145736 | tf_op jit(solution)/shard_map/ppermute | solution.py:35
  102.6 3.4 %collective-permute-start.10 = (bf16[2,16,64,128]{3,2,1,0:T(8,128)(2,1)S(1)}, bf16[2,16,64,128]{3,2,1,0:T(8,128)(2,1)}, u32[]{:S(2)}, u32[]{:S(2)}) collective-permute-start(bf16[2,16,64,128]{3,2,1,0:T(8,128)(2,1)S(1)} %slice.47), channel_id=1, source_target_pairs={{1,193},{65,1},{129,65},{193,129},{3,195},{67,3},{131,67},{195,131... | collective-permute-start | bytes 1572872 | tf_op jit(solution)/shard_map/ppermute | solution.py:60
  106.1 2.1 %collective-permute-start.9 = (bf16[2,16,64,128]{3,2,1,0:T(8,128)(2,1)S(1)}, bf16[2,16,64,128]{3,2,1,0:T(8,128)(2,1)}, u32[]{:S(2)}, u32[]{:S(2)}) collective-permute-start(bf16[2,16,64,128]{3,2,1,0:T(8,128)(2,1)S(1)} %slice.46), channel_id=1, source_target_pairs={{1,65},{65,129},{129,193},{193,1},{3,67},{67,131},{131,195},{195,3... | collective-permute-start | bytes 1572872 | tf_op jit(solution)/shard_map/ppermute | solution.py:60
  108.3 11.1 %attention.1.first_ref = bf16[448,512]{1,0:T(8,128)(2,1)S(1)} custom-call(s32[1]{0:T(128)} %bitcast.core_ref, f32[8]{0:T(128)S(1)} %minimum_exponential_fusion.scale_ref, bf16[18,48,512]{2,1,0:T(8,128)(2,1)S(1)} %pad_maximum_fusion.tall_ref, f32[3,8,96,128]{3,2,1,0:T(8,128)S(1)} %broadcast_select_fusion.bias_ref, bf16[384,288]{1,0:T(8,128)(2,1)S(1)} %copy-done.7, ...), custom_call_target="tpu_custom_call" | custom-call | flops 20000000000 | bytes 20000000 | tf_op jit(solution)/shard_map/attention/pallas_call | solution.py:461
  119.4 0.8 copy-done.8
  120.2 3.6 %collective-permute-start.13 = (bf16[2,16,64,128]{3,2,1,0:T(8,128)(2,1)}, bf16[2,16,64,128]{3,2,1,0:T(8,128)(2,1)S(1)}, u32[]{:S(2)}, u32[]{:S(2)}) collective-permute-start(bf16[2,16,64,128]{3,2,1,0:T(8,128)(2,1)} %collective-permute-done.9.refs_6_), channel_id=1, source_target_pairs={{0,1},{1,0},{2,3},{3,2},{4,5},{5,4},{6,7},{7,6},{8,9},{9,8},{10,11... | collective-permute-start | bytes 1572872 | tf_op jit(solution)/shard_map/ppermute | solution.py:35
  123.8 2.1 %collective-permute-start.14 = (bf16[2,16,64,128]{3,2,1,0:T(8,128)(2,1)}, bf16[2,16,64,128]{3,2,1,0:T(8,128)(2,1)S(1)}, u32[]{:S(2)}, u32[]{:S(2)}) collective-permute-start(bf16[2,16,64,128]{3,2,1,0:T(8,128)(2,1)} %collective-permute-done.10.refs_8_), channel_id=1, source_target_pairs={{0,1},{1,0},{2,3},{3,2},{4,5},{5,4},{6,7},{7,6},{8,9},{9,8},{10,11... | collective-permute-start | bytes 1572872 | tf_op jit(solution)/shard_map/ppermute | solution.py:35
  126.0 0.1 pad_add_fusion.1.where_ref
  126.1 1.8 %collective-permute-done.14.refs_9_ = bf16[2,16,64,128]{3,2,1,0:T(8,128)(2,1)S(1)} collective-permute-done((bf16[2,16,64,128]{3,2,1,0:T(8,128)(2,1)}, bf16[2,16,64,128]{3,2,1,0:T(8,128)(2,1)S(1)}, u32[]{:S(2)}, u32[]{:S(2)}) %collective-permute-start.14) | collective-permute-done | bytes 524320 | tf_op jit(solution)/shard_map/ppermute | solution.py:35
  127.8 7.8 %feedforward.1 = bf16[6,18,1024]{2,1,0:T(8,128)(2,1)} custom-call(s32[3]{0:T(128)S(1)} %pad_add_fusion.1.where_ref, bf16[448,512]{1,0:T(8,128)(2,1)} %copy-done.8, f32[1,512]{1,0:T(1,128)S(1)} %bitcast.25, f32[1,512]{1,0:T(1,128)S(1)} %bitcast.26, f32[1,1024]{1,0:T(1,128)S(1)} %bitcast.21, f32[1,1024]{1,0:T(1,128)S(1)} %bitcast.22, ...), custom_call_target="tpu_custom_call" | custom-call | flops 6000000000 | bytes 20000000 | tf_op jit(solution)/shard_map/feedforward/pallas_call | solution.py:497
  (47 shorter events, 0.2 us)
Async XLA Ops:
  0.0 13.9 %copy-start = (bf16[32,1024]{1,0:T(8,128)(2,1)S(1)}, bf16[32,1024]{1,0:T(8,128)(2,1)}, u32[]{:S(2)}) copy-start(bf16[32,1024]{1,0:T(8,128)(2,1)} %param.28) | copy-start | bytes 196612
  0.0 24.3 %copy-start.14 = (s32[12288]{0:T(1024)S(1)}, s32[12288]{0:T(1024)}, u32[]{:S(2)}) copy-start(s32[12288]{0:T(1024)} %constant.68.clone) | copy-start | bytes 147460
  2.2 11.7 %collective-permute-start = (bf16[8,4096]{1,0:T(8,128)(2,1)S(1)}, bf16[8,4096]{1,0:T(8,128)(2,1)S(1)}, u32[]{:S(2)}, u32[]{:S(2)}) collective-permute-start(bf16[8,4096]{1,0:T(8,128)(2,1)S(1)} %constant_dynamic-update-slice_fusion), channel_id=1, source_target_pairs={{0,1},{1,0},{2,3},{3,2},{4,5},{5,4},{6,7},{7,6},{8,9},{9,8},{10,11... | collective-permute-start | bytes 196616 | tf_op jit(solution)/shard_map/ppermute | solution.py:35
  14.8 25.9 %all-to-all-start = ((bf16[16,80,128]{2,1,0:T(8,128)(2,1)}), bf16[16,80,128]{2,1,0:T(8,128)(2,1)S(1)}, u32[]{:S(2)}, u32[]{:S(2)}) async-start(bf16[16,80,128]{2,1,0:T(8,128)(2,1)} %broadcast_in_dim.34), calls=%async_computation | async-start | bytes 655360 | tf_op jit(solution)/shard_map/all_to_all | solution.py:40
  24.4 4.1 %copy-start.10 = (pred[96,128]{1,0:T(32,128)(4,1)S(1)}, pred[96,128]{1,0:T(32,128)(4,1)}, u32[]{:S(2)}) copy-start(pred[96,128]{1,0:T(32,128)(4,1)} %constant.70.clone) | copy-start | bytes 36868
  24.4 4.2 %copy-start.11 = (pred[128]{0:T(512)(128)(4,1)S(1)}, pred[128]{0:T(512)(128)(4,1)}, u32[]{:S(2)}) copy-start(pred[128]{0:T(512)(128)(4,1)} %constant.69.clone) | copy-start | bytes 388
  24.4 4.3 %copy-start.9 = (bf16[12,36,512]{2,1,0:T(8,128)(2,1)S(1)}, bf16[12,36,512]{2,1,0:T(8,128)(2,1)}, u32[]{:S(2)}) copy-start(bf16[12,36,512]{2,1,0:T(8,128)(2,1)} %param.23) | copy-start | bytes 1327108
  28.7 5.5 %collective-permute-start.1 = (bf16[3,36,512]{2,1,0:T(8,128)(2,1)S(1)}, bf16[3,36,512]{2,1,0:T(8,128)(2,1)S(1)}, u32[]{:S(2)}, u32[]{:S(2)}) collective-permute-start(bf16[3,36,512]{2,1,0:T(8,128)(2,1)S(1)} %get-tuple-element.39), channel_id=1, source_target_pairs={{0,64},{64,128},{128,192},{192,256},{256,320},{320,384},{384,448},... | collective-permute-start | bytes 331784 | tf_op jit(solution)/shard_map/ppermute | solution.py:35
  31.8 6.2 %collective-permute-start.2 = (bf16[3,36,512]{2,1,0:T(8,128)(2,1)S(1)}, bf16[3,36,512]{2,1,0:T(8,128)(2,1)S(1)}, u32[]{:S(2)}, u32[]{:S(2)}) collective-permute-start(bf16[3,36,512]{2,1,0:T(8,128)(2,1)S(1)} %get-tuple-element.40), channel_id=1, source_target_pairs={{64,0},{128,64},{192,128},{256,192},{320,256},{384,320},{448,384},... | collective-permute-start | bytes 331784 | tf_op jit(solution)/shard_map/ppermute | solution.py:35
  41.9 20.3 %all-to-all-start.1 = ((bf16[4,16,80,128]{3,2,1,0:T(8,128)(2,1)}), bf16[4,16,80,128]{3,2,1,0:T(8,128)(2,1)}, u32[]{:S(2)}, u32[]{:S(2)}) async-start(bf16[4,16,80,128]{3,2,1,0:T(8,128)(2,1)} %broadcast_in_dim.58), calls=%async_computation.1 | async-start | bytes 2621440 | tf_op jit(solution)/shard_map/all_to_all | solution.py:55
  46.3 10.7 %collective-permute-start.3 = (bf16[18,6,512]{2,1,0:T(8,128)(2,1)S(1)}, bf16[18,6,512]{2,1,0:T(8,128)(2,1)S(1)}, u32[]{:S(2)}, u32[]{:S(2)}) collective-permute-start(bf16[18,6,512]{2,1,0:T(8,128)(2,1)S(1)} %get-tuple-element.37), channel_id=1, source_target_pairs={{0,1},{1,2},{2,3},{3,4},{4,5},{5,6},{6,7},{7,8},{8,9},{9,10},{10,1... | collective-permute-start | bytes 331784 | tf_op jit(solution)/shard_map/ppermute | solution.py:35
  54.9 6.9 %collective-permute-start.4 = (bf16[18,6,512]{2,1,0:T(8,128)(2,1)S(1)}, bf16[18,6,512]{2,1,0:T(8,128)(2,1)S(1)}, u32[]{:S(2)}, u32[]{:S(2)}) collective-permute-start(bf16[18,6,512]{2,1,0:T(8,128)(2,1)S(1)} %get-tuple-element.38), channel_id=1, source_target_pairs={{0,63},{1,0},{2,1},{3,2},{4,3},{5,4},{6,5},{7,6},{8,7},{9,8},{10,9... | collective-permute-start | bytes 331784 | tf_op jit(solution)/shard_map/ppermute | solution.py:35
  64.7 31.4 %copy-start.13 = (f32[8]{0:T(128)S(1)}, f32[8]{0:T(128)}, u32[]{:S(2)}) copy-start(f32[8]{0:T(128)} %param.29) | copy-start | bytes 100
  64.7 27.7 %collective-permute-start.5 = (bf16[4,16,64,128]{3,2,1,0:T(8,128)(2,1)S(1)}, bf16[4,16,64,128]{3,2,1,0:T(8,128)(2,1)S(1)}, u32[]{:S(2)}, u32[]{:S(2)}) collective-permute-start(bf16[4,16,64,128]{3,2,1,0:T(8,128)(2,1)S(1)} %slice.45.refs_0_), channel_id=1, source_target_pairs={{0,1},{1,0},{2,3},{3,2},{4,5},{5,4},{6,7},{7,6},{8,9},{9,8},{10,11... | collective-permute-start | bytes 3145736 | tf_op jit(solution)/shard_map/ppermute | solution.py:35
  68.6 23.9 %collective-permute-start.6 = (bf16[4,16,64,128]{3,2,1,0:T(8,128)(2,1)S(1)}, bf16[4,16,64,128]{3,2,1,0:T(8,128)(2,1)}, u32[]{:S(2)}, u32[]{:S(2)}) collective-permute-start(bf16[4,16,64,128]{3,2,1,0:T(8,128)(2,1)S(1)} %slice.45.refs_0_), channel_id=1, source_target_pairs={{1,65},{65,129},{129,193},{193,1},{3,67},{67,131},{131,195},{195,3... | collective-permute-start | bytes 3145736 | tf_op jit(solution)/shard_map/ppermute | solution.py:60
  70.8 21.7 %collective-permute-start.7 = (bf16[4,16,64,128]{3,2,1,0:T(8,128)(2,1)S(1)}, bf16[4,16,64,128]{3,2,1,0:T(8,128)(2,1)}, u32[]{:S(2)}, u32[]{:S(2)}) collective-permute-start(bf16[4,16,64,128]{3,2,1,0:T(8,128)(2,1)S(1)} %slice.45.refs_0_), channel_id=1, source_target_pairs={{1,193},{65,1},{129,65},{193,129},{3,195},{67,3},{131,67},{195,131... | collective-permute-start | bytes 3145736 | tf_op jit(solution)/shard_map/ppermute | solution.py:60
  92.4 15.8 %copy-start.3 = (f32[512]{0:T(512)S(1)}, f32[512]{0:T(512)}, u32[]{:S(2)}) copy-start(f32[512]{0:T(512)} %param.33) | copy-start | bytes 6148
  92.4 15.8 %copy-start.4 = (f32[512]{0:T(512)S(1)}, f32[512]{0:T(512)}, u32[]{:S(2)}) copy-start(f32[512]{0:T(512)} %param.34) | copy-start | bytes 6148
  92.4 15.8 %copy-start.7 = (bf16[384,288]{1,0:T(8,128)(2,1)S(1)}, bf16[384,288]{1,0:T(8,128)(2,1)}, u32[]{:S(2)}) copy-start(bf16[384,288]{1,0:T(8,128)(2,1)} %constant.71.clone.arrange_ref) | copy-start | bytes 663556
  92.4 15.8 %copy-start.12 = (bf16[4,16,64,128]{3,2,1,0:T(8,128)(2,1)}, bf16[4,16,64,128]{3,2,1,0:T(8,128)(2,1)S(1)}, u32[]{:S(2)}) copy-start(bf16[4,16,64,128]{3,2,1,0:T(8,128)(2,1)S(1)} %collective-permute-done.5.refs_1_) | copy-start | bytes 3145732
  92.5 15.7 %collective-permute-start.8 = (bf16[16,16,16,128]{3,2,1,0:T(8,128)(2,1)S(1)}, bf16[16,16,16,128]{3,2,1,0:T(8,128)(2,1)S(1)}, u32[]{:S(2)}, u32[]{:S(2)}) collective-permute-start(bf16[16,16,16,128]{3,2,1,0:T(8,128)(2,1)S(1)} %bitcast.19), channel_id=1, source_target_pairs={{0,1},{1,0},{2,3},{3,2},{4,5},{5,4},{6,7},{7,6},{8,9},{9,8},{10,11... | collective-permute-start | bytes 3145736 | tf_op jit(solution)/shard_map/ppermute | solution.py:35
  97.2 28.8 %collective-permute-start.11 = (bf16[4,16,64,128]{3,2,1,0:T(8,128)(2,1)}, bf16[4,16,64,128]{3,2,1,0:T(8,128)(2,1)}, u32[]{:S(2)}, u32[]{:S(2)}) collective-permute-start(bf16[4,16,64,128]{3,2,1,0:T(8,128)(2,1)} %collective-permute-done.6.refs_2_), channel_id=1, source_target_pairs={{0,1},{1,0},{2,3},{3,2},{4,5},{5,4},{6,7},{7,6},{8,9},{9,8},{10,11... | collective-permute-start | bytes 3145736 | tf_op jit(solution)/shard_map/ppermute | solution.py:35
  100.2 25.8 %collective-permute-start.12 = (bf16[4,16,64,128]{3,2,1,0:T(8,128)(2,1)}, bf16[4,16,64,128]{3,2,1,0:T(8,128)(2,1)}, u32[]{:S(2)}, u32[]{:S(2)}) collective-permute-start(bf16[4,16,64,128]{3,2,1,0:T(8,128)(2,1)} %collective-permute-done.7.refs_4_), channel_id=1, source_target_pairs={{0,1},{1,0},{2,3},{3,2},{4,5},{5,4},{6,7},{7,6},{8,9},{9,8},{10,11... | collective-permute-start | bytes 3145736 | tf_op jit(solution)/shard_map/ppermute | solution.py:35
  102.6 17.6 %collective-permute-start.10 = (bf16[2,16,64,128]{3,2,1,0:T(8,128)(2,1)S(1)}, bf16[2,16,64,128]{3,2,1,0:T(8,128)(2,1)}, u32[]{:S(2)}, u32[]{:S(2)}) collective-permute-start(bf16[2,16,64,128]{3,2,1,0:T(8,128)(2,1)S(1)} %slice.47), channel_id=1, source_target_pairs={{1,193},{65,1},{129,65},{193,129},{3,195},{67,3},{131,67},{195,131... | collective-permute-start | bytes 1572872 | tf_op jit(solution)/shard_map/ppermute | solution.py:60
  106.1 14.1 %collective-permute-start.9 = (bf16[2,16,64,128]{3,2,1,0:T(8,128)(2,1)S(1)}, bf16[2,16,64,128]{3,2,1,0:T(8,128)(2,1)}, u32[]{:S(2)}, u32[]{:S(2)}) collective-permute-start(bf16[2,16,64,128]{3,2,1,0:T(8,128)(2,1)S(1)} %slice.46), channel_id=1, source_target_pairs={{1,65},{65,129},{129,193},{193,1},{3,67},{67,131},{131,195},{195,3... | collective-permute-start | bytes 1572872 | tf_op jit(solution)/shard_map/ppermute | solution.py:60
  108.2 19.6 %copy-start.1 = (f32[1024]{0:T(1024)S(1)}, f32[1024]{0:T(1024)}, u32[]{:S(2)}) copy-start(f32[1024]{0:T(1024)} %param.37) | copy-start | bytes 12292
  108.2 19.6 %copy-start.2 = (f32[1024]{0:T(1024)S(1)}, f32[1024]{0:T(1024)}, u32[]{:S(2)}) copy-start(f32[1024]{0:T(1024)} %param.38) | copy-start | bytes 12292
  108.3 19.6 %copy-start.5 = (f32[512]{0:T(512)S(1)}, f32[512]{0:T(512)}, u32[]{:S(2)}) copy-start(f32[512]{0:T(512)} %param.35) | copy-start | bytes 6148
  108.3 19.6 %copy-start.6 = (f32[512]{0:T(512)S(1)}, f32[512]{0:T(512)}, u32[]{:S(2)}) copy-start(f32[512]{0:T(512)} %param.36) | copy-start | bytes 6148
  119.4 0.8 copy-start.8
  120.2 5.8 %collective-permute-start.13 = (bf16[2,16,64,128]{3,2,1,0:T(8,128)(2,1)}, bf16[2,16,64,128]{3,2,1,0:T(8,128)(2,1)S(1)}, u32[]{:S(2)}, u32[]{:S(2)}) collective-permute-start(bf16[2,16,64,128]{3,2,1,0:T(8,128)(2,1)} %collective-permute-done.9.refs_6_), channel_id=1, source_target_pairs={{0,1},{1,0},{2,3},{3,2},{4,5},{5,4},{6,7},{7,6},{8,9},{9,8},{10,11... | collective-permute-start | bytes 1572872 | tf_op jit(solution)/shard_map/ppermute | solution.py:35
  123.8 4.0 %collective-permute-start.14 = (bf16[2,16,64,128]{3,2,1,0:T(8,128)(2,1)}, bf16[2,16,64,128]{3,2,1,0:T(8,128)(2,1)S(1)}, u32[]{:S(2)}, u32[]{:S(2)}) collective-permute-start(bf16[2,16,64,128]{3,2,1,0:T(8,128)(2,1)} %collective-permute-done.10.refs_8_), channel_id=1, source_target_pairs={{0,1},{1,0},{2,3},{3,2},{4,5},{5,4},{6,7},{7,6},{8,9},{9,8},{10,11... | collective-permute-start | bytes 1572872 | tf_op jit(solution)/shard_map/ppermute | solution.py:35

commit v7 on v5

--- a/solution.py
+++ b/solution.py
@@ -49,6 +49,31 @@
 
 def four(block):
     return jnp.broadcast_to(block[None], (4,) + block.shape)
+
+
+def fan_kernel(ring_ref, out_ref, sems):
+    copies = [
+        pltpu.make_async_copy(ring_ref.at[:, :, pl.ds(16, 64), :], out_ref.at[i], sems.at[i])
+        for i in range(4)
+    ]
+    for copy in copies:
+        copy.start()
+    for copy in copies:
+        copy.wait()
+
+
+def fan(in_ring):
+    anywhere = pl.BlockSpec(memory_space=pl.ANY)
+    return pl.pallas_call(
+        fan_kernel,
+        out_shape=jax.ShapeDtypeStruct((4, 4, 16, 64, 128), BF16),
+        in_specs=[anywhere],
+        out_specs=anywhere,
+        scratch_shapes=[pltpu.SemaphoreType.DMA((4,))],
+        compiler_params=pltpu.CompilerParams(vmem_limit_bytes=24 * 1024 * 1024),
+        cost_estimate=pl.CostEstimate(flops=0, bytes_accessed=30_000_000, transcendentals=0),
+        name="fan",
+    )(in_ring)
 
 
 def spread_ring(copies, x_core):
@@ -195,14 +220,20 @@
 
         def window(w, _, band=band, first=first, count=count, done=done):
             base = pl.multiple_of(w * WIN_PAD, WIN_PAD)
+            all_scores = []
             for pair in range(HEAD_COUNT // 2):
                 cut = slice(pair * 128, pair * 128 + 128)
                 query = queries[pl.ds(base + first, count), cut]
                 key = both(keys[pl.ds(base, WIN_PAD), cut])
+                all_scores.append(
+                    lax.dot_general(
+                        query, key, (((1,), (1,)), ((), ())), preferred_element_type=F32
+                    )
+                )
+            for pair in range(HEAD_COUNT // 2):
+                cut = slice(pair * 128, pair * 128 + 128)
                 value = both(values[pl.ds(base, WIN_PAD), cut])
-                scores = lax.dot_general(
-                    query, key, (((1,), (1,)), ((), ())), preferred_element_type=F32
-                )
+                scores = all_scores[pair]
                 expo = []
                 for h in range(2):
                     head = pair * 2 + h
@@ -219,7 +250,7 @@
                 heads[pl.ds(place, count), cut] = (mixed[:, :128] / mixed[:, 128:]).astype(BF16)
             return 0
 
-        lax.fori_loop(0, WINS, window, 0)
+        lax.fori_loop(0, WINS, window, 0, unroll=True)
         done += WINS * count
 
     for copy in late:
@@ -427,7 +458,7 @@
     tall = jnp.concatenate([west, strip, east], axis=1)
     in_ring, tall = lax.optimization_barrier((in_ring, tall))
     attn_mine = spread_ring(four(in_ring[:, :, :16]), 1).reshape(16, 16, 16, 128)
-    rest_copies = four(in_ring[:, :, 16:])
+    rest_copies = fan(in_ring)
     attn_mine, rest_copies = lax.optimization_barrier((attn_mine, rest_copies))
     attn_other = shifted(attn_mine, "core", 1, True)
     rest_mine = spread_ring(rest_copies, 1).reshape(16, 16, 64, 128)

time: 135 us -> 131 us (0.970)
  Pallas kernels: 28.7 us -> 19.2 us
  waiting for transfers between devices: 29 us -> 36.7 us
  local copies, waits for them, and re-layouts: 14.6 us -> 9.88 us
  starting transfers between devices: 53.7 us -> 55.8 us
    pallas_call x1, Pallas kernels: 21.8 us -> 11.7 us  [local(): pl.pallas_call(attention_kernel, out_shape=jax.ShapeDtypeStruct((4 * QUAD...]
    all_to_all x3, waiting for transfers between devices: 7.76 us -> 15.5 us  [spread_ring(): return lax.all_to_all(copies, ALL, 0, 0, axis_index_groups=rings(x_core))]
    broadcast_in_dim x3 -> x2, local copies, waits for them, and re-layouts: 6.92 us -> 2.43 us  [four(): return jnp.broadcast_to(block[None], (4,) + block.shape)]
    slice x1 -> x0, local copies, waits for them, and re-layouts: 2.28 us -> none  [local(): rest_copies = four(in_ring[:, :, 16:])]
    ppermute x7, starting transfers between devices: 30.7 us -> 32.7 us  [shifted(): return lax.ppermute(block, axes, pairs)]
    unnamed x34, local copies, waits for them, and re-layouts: 2.36 us -> 4.36 us
  transfers between devices with their start and end apart: 11 -> 11, of which waited for: 8 -> 9; matrix products, arithmetic and copies ran while one was open for 8% -> 7% of each run, Pallas kernels for 16% -> 10%
where the time goes in v7:
time: 131 us; the launch traced here: 130 us
  starting transfers between devices  55.8 us (43%)
  waiting for transfers between devices  36.7 us (28%)
  Pallas kernels  19.2 us (15%)
  local copies, waits for them, and re-layouts  9.88 us (8%)
  matrix products  5.38 us (4%)
  other arithmetic  2.08 us (2%)
    ppermute x7, starting transfers between devices, shifted(): return lax.ppermute(block, axes, pairs)  32.7 us
    ppermute x7, waiting for transfers between devices, shifted(): return lax.ppermute(block, axes, pairs)  18.6 us
    all_to_all x3, waiting for transfers between devices, spread_ring(): return lax.all_to_all(copies, ALL, 0, 0, axis_index_groups=rings(x_core))  15.5 us
    all_to_all x3, starting transfers between devices, spread_ring(): return lax.all_to_all(copies, ALL, 0, 0, axis_index_groups=rings(x_core))  13.4 us
    pallas_call x1, Pallas kernels, local(): pl.pallas_call(attention_kernel, out_shape=jax.ShapeDtypeStruct((4 * QUAD...  11.7 us
    all_to_all x1, starting transfers between devices, spread(): lax.all_to_all(jnp.broadcast_to(block[None], (size,) + block.shape), axes...  9.67 us
    pallas_call x1, Pallas kernels, local(): pl.pallas_call(feedforward_kernel, out_shape=jax.ShapeDtypeStruct((6, 18,...  6.91 us
    unnamed x34, local copies, waits for them, and re-layouts  4.36 us
  transfers between devices with their start and end apart: 11, of which 9 were waited for; matrix products, arithmetic and copies ran while one was open for 7% of the time, Pallas kernels for 10%

profile of v7, /device:TPU:1, one launch (start us, length us, event | category | flops | bytes accessed | tf_op | source)
XLA Modules:
  0.0 129.6 jit_solution(3647181779266272497)
XLA Ops:
  0.0 0.8 constant_dynamic-update-slice_fusion.2
  0.8 0.7 constant_dynamic-update-slice_fusion.1
  1.5 0.8 constant_dynamic-update-slice_fusion
  2.2 8.8 %collective-permute-start = (bf16[8,4096]{1,0:T(8,128)(2,1)S(1)}, bf16[8,4096]{1,0:T(8,128)(2,1)S(1)}, u32[]{:S(2)}, u32[]{:S(2)}) collective-permute-start(bf16[8,4096]{1,0:T(8,128)(2,1)S(1)} %constant_dynamic-update-slice_fusion), channel_id=1, source_target_pairs={{0,1},{1,0},{2,3},{3,2},{4,5},{5,4},{6,7},{7,6},{8,9},{9,8},{10,11... | collective-permute-start | bytes 196616 | tf_op jit(solution)/shard_map/ppermute | solution.py:35
  11.0 0.8 fusion.23
  11.8 0.7 dynamic_slice.14
  12.5 1.4 %fusion.6 = f32[253,8]{0,1:T(8,128)S(1)} fusion(f32[512,8]{0,1:T(8,128)} %param.32, f32[512]{0:T(512)} %param.31, f32[512]{0:T(512)S(1)} %bitcast.26, f32[253]{0:T(256)} %constant.81, f32[512]{0:T(512)S(1)} %bitcast.25, f32[253]{0:T(256)} %constant.79), kind=kOutput, calls=%fused_computation.8 | convolution fusion | flops 13091232 | bytes 32648 | tf_op jit(solution)/shard_map/dot_general | solution.py:109
  14.0 0.0 collective-permute-done
  14.0 0.8 broadcast_in_dim.34
  14.8 9.7 %all-to-all-start = ((bf16[16,80,128]{2,1,0:T(8,128)(2,1)}), bf16[16,80,128]{2,1,0:T(8,128)(2,1)S(1)}, u32[]{:S(2)}, u32[]{:S(2)}) async-start(bf16[16,80,128]{2,1,0:T(8,128)(2,1)} %broadcast_in_dim.34), calls=%async_computation | async-start | bytes 655360 | tf_op jit(solution)/shard_map/all_to_all | solution.py:40
  24.5 0.0 copy-start.11
  24.5 4.0 %fusion.2 = f32[8,96,128]{2,0,1:T(8,128)S(1)} fusion(f32[253,8]{0,1:T(8,128)S(1)} %fusion.6, s32[12288]{0:T(1024)S(1)} %copy-done.15), kind=kOutput, calls=%fused_computation.3 | convolution fusion | flops 301559808 | bytes 450464 | tf_op jit(solution)/shard_map/dot_general | solution.py:444
  28.5 0.1 pad_add_fusion
  28.5 0.1 broadcast_and_fusion
  28.7 0.1 copy_select_fusion
  28.8 0.0 copy-done.11
  28.8 3.1 %collective-permute-start.1 = (bf16[3,36,512]{2,1,0:T(8,128)(2,1)S(1)}, bf16[3,36,512]{2,1,0:T(8,128)(2,1)S(1)}, u32[]{:S(2)}, u32[]{:S(2)}) collective-permute-start(bf16[3,36,512]{2,1,0:T(8,128)(2,1)S(1)} %get-tuple-element.29), channel_id=1, source_target_pairs={{0,64},{64,128},{128,192},{192,256},{256,320},{320,384},{384,448},... | collective-permute-start | bytes 331784 | tf_op jit(solution)/shard_map/ppermute | solution.py:35
  31.9 1.3 collective-permute-start.2
  33.2 0.1 broadcast_select_fusion.bias_ref
  33.4 1.0 collective-permute-done.1
  34.3 3.8 %collective-permute-done.2 = bf16[3,36,512]{2,1,0:T(8,128)(2,1)S(1)} collective-permute-done((bf16[3,36,512]{2,1,0:T(8,128)(2,1)S(1)}, bf16[3,36,512]{2,1,0:T(8,128)(2,1)S(1)}, u32[]{:S(2)}, u32[]{:S(2)}) %collective-permute-start.2) | collective-permute-done | bytes 110624 | tf_op jit(solution)/shard_map/ppermute | solution.py:35
  38.1 0.1 pad_maximum_fusion.1
  38.2 2.6 %all-to-all-done = bf16[16,80,128]{2,1,0:T(8,128)(2,1)S(1)} async-done(((bf16[16,80,128]{2,1,0:T(8,128)(2,1)}), bf16[16,80,128]{2,1,0:T(8,128)(2,1)S(1)}, u32[]{:S(2)}, u32[]{:S(2)}) %all-to-all-start) | async-done | bytes 327712 | tf_op jit(solution)/shard_map/all_to_all | solution.py:40
  40.8 1.2 broadcast_in_dim.58
  42.1 4.2 %all-to-all-start.1 = ((bf16[4,16,80,128]{3,2,1,0:T(8,128)(2,1)}), bf16[4,16,80,128]{3,2,1,0:T(8,128)(2,1)S(1)}, u32[]{:S(2)}, u32[]{:S(2)}) async-start(bf16[4,16,80,128]{3,2,1,0:T(8,128)(2,1)} %broadcast_in_dim.58), calls=%async_computation.1 | async-start | bytes 2621440 | tf_op jit(solution)/shard_map/all_to_all | solution.py:80
  46.3 8.7 %collective-permute-start.3 = (bf16[18,6,512]{2,1,0:T(8,128)(2,1)S(1)}, bf16[18,6,512]{2,1,0:T(8,128)(2,1)S(1)}, u32[]{:S(2)}, u32[]{:S(2)}) collective-permute-start(bf16[18,6,512]{2,1,0:T(8,128)(2,1)S(1)} %get-tuple-element.27), channel_id=1, source_target_pairs={{0,1},{1,2},{2,3},{3,4},{4,5},{5,6},{6,7},{7,8},{8,9},{9,10},{10,1... | collective-permute-start | bytes 331784 | tf_op jit(solution)/shard_map/ppermute | solution.py:35
  55.0 1.9 %collective-permute-start.4 = (bf16[18,6,512]{2,1,0:T(8,128)(2,1)S(1)}, bf16[18,6,512]{2,1,0:T(8,128)(2,1)S(1)}, u32[]{:S(2)}, u32[]{:S(2)}) collective-permute-start(bf16[18,6,512]{2,1,0:T(8,128)(2,1)S(1)} %get-tuple-element.28), channel_id=1, source_target_pairs={{0,63},{1,0},{2,1},{3,2},{4,3},{5,4},{6,5},{7,6},{8,7},{9,8},{10,9... | collective-permute-start | bytes 331784 | tf_op jit(solution)/shard_map/ppermute | solution.py:35
  57.0 0.2 collective-permute-done.3
  57.1 4.7 %collective-permute-done.4 = bf16[18,6,512]{2,1,0:T(8,128)(2,1)S(1)} collective-permute-done((bf16[18,6,512]{2,1,0:T(8,128)(2,1)S(1)}, bf16[18,6,512]{2,1,0:T(8,128)(2,1)S(1)}, u32[]{:S(2)}, u32[]{:S(2)}) %collective-permute-start.4) | collective-permute-done | bytes 110624 | tf_op jit(solution)/shard_map/ppermute | solution.py:35
  61.8 1.5 %pad_maximum_fusion.tall_ref = bf16[18,48,512]{2,1,0:T(8,128)(2,1)S(1)} fusion(bf16[18,6,512]{2,1,0:T(8,128)(2,1)S(1)} %collective-permute-done.4, bf16[18,36,512]{2,1,0:T(8,128)(2,1)} %copy-done.10, bf16[18,6,512]{2,1,0:T(8,128)(2,1)S(1)} %collective-permute-done.3), kind=kLoop, calls=%fused_computation.9 | loop fusion | flops 2654208 | bytes 1769472 | tf_op jit(solution)/shard_map/concatenate | solution.py:458
  63.3 0.0 all-to-all-done.1.ring_ref
  63.4 1.2 broadcast_in_dim.59
  64.6 4.3 %all-to-all-start.2 = ((bf16[4,4,16,16,128]{4,3,2,1,0:T(8,128)(2,1)}), bf16[4,4,16,16,128]{4,3,2,1,0:T(8,128)(2,1)}, u32[]{:S(2)}, u32[]{:S(2)}) async-start(bf16[4,4,16,16,128]{4,3,2,1,0:T(8,128)(2,1)} %broadcast_in_dim.59), calls=%async_computation.2 | async-start | bytes 2097152 | tf_op jit(solution)/shard_map/all_to_all | solution.py:80
  68.8 0.6 fan.1
  69.5 2.0 %copy-done.1 = bf16[4,4,16,64,128]{4,3,2,1,0:T(8,128)(2,1)} copy-done((bf16[4,4,16,64,128]{4,3,2,1,0:T(8,128)(2,1)}, bf16[4,4,16,64,128]{4,3,2,1,0:T(8,128)(2,1)S(1)}, u32[]{:S(2)}) %copy-start.1) | copy-done | bytes 4194328
  71.5 7.5 %all-to-all-done.2 = bf16[4,4,16,16,128]{4,3,2,1,0:T(8,128)(2,1)} async-done(((bf16[4,4,16,16,128]{4,3,2,1,0:T(8,128)(2,1)}), bf16[4,4,16,16,128]{4,3,2,1,0:T(8,128)(2,1)}, u32[]{:S(2)}, u32[]{:S(2)}) %all-to-all-start.2) | async-done | bytes 1048608 | tf_op jit(solution)/shard_map/all_to_all | solution.py:80
  78.9 5.0 %all-to-all-start.3 = ((bf16[4,4,16,64,128]{4,3,2,1,0:T(8,128)(2,1)}), bf16[4,4,16,64,128]{4,3,2,1,0:T(8,128)(2,1)}, u32[]{:S(2)}, u32[]{:S(2)}) async-start(bf16[4,4,16,64,128]{4,3,2,1,0:T(8,128)(2,1)} %copy-done.1), calls=%async_computation.3 | async-start | bytes 8388608 | tf_op jit(solution)/shard_map/all_to_all | solution.py:80
  83.9 4.0 %collective-permute-start.5 = (bf16[16,16,16,128]{3,2,1,0:T(8,128)(2,1)}, bf16[16,16,16,128]{3,2,1,0:T(8,128)(2,1)S(1)}, u32[]{:S(2)}, u32[]{:S(2)}) collective-permute-start(bf16[16,16,16,128]{3,2,1,0:T(8,128)(2,1)} %bitcast.8.mine_ref), channel_id=1, source_target_pairs={{0,1},{1,0},{2,3},{3,2},{4,5},{5,4},{6,7},{7,6},{8,9},{9,8},{10,11... | collective-permute-start | bytes 3145736 | tf_op jit(solution)/shard_map/ppermute | solution.py:35
  88.0 2.3 %collective-permute-done.5.other_ref = bf16[16,16,16,128]{3,2,1,0:T(8,128)(2,1)S(1)} collective-permute-done((bf16[16,16,16,128]{3,2,1,0:T(8,128)(2,1)}, bf16[16,16,16,128]{3,2,1,0:T(8,128)(2,1)S(1)}, u32[]{:S(2)}, u32[]{:S(2)}) %collective-permute-start.5) | collective-permute-done | bytes 1048608 | tf_op jit(solution)/shard_map/ppermute | solution.py:35
  90.3 0.0 copy-start.3
  90.3 0.0 copy-start.6
  90.3 0.0 copy-start.7
  90.3 11.7 %attention.1.first_ref = bf16[448,512]{1,0:T(8,128)(2,1)S(1)} custom-call(s32[1]{0:T(128)} %bitcast.core_ref, f32[8]{0:T(128)S(1)} %minimum_exponential_fusion.scale_ref, bf16[18,48,512]{2,1,0:T(8,128)(2,1)S(1)} %pad_maximum_fusion.tall_ref, f32[3,8,96,128]{3,2,1,0:T(8,128)S(1)} %broadcast_select_fusion.bias_ref, bf16[384,288]{1,0:T(8,128)(2,1)S(1)} %copy-done.8, ...), custom_call_target="tpu_custom_call" | custom-call | flops 20000000000 | bytes 20000000 | tf_op jit(solution)/shard_map/attention/pallas_call | solution.py:477
  102.0 0.8 copy-done.9
  102.8 8.0 %all-to-all-done.3 = bf16[4,4,16,64,128]{4,3,2,1,0:T(8,128)(2,1)} async-done(((bf16[4,4,16,64,128]{4,3,2,1,0:T(8,128)(2,1)}), bf16[4,4,16,64,128]{4,3,2,1,0:T(8,128)(2,1)}, u32[]{:S(2)}, u32[]{:S(2)}) %all-to-all-start.3) | async-done | bytes 4194336 | tf_op jit(solution)/shard_map/all_to_all | solution.py:80
  110.9 4.9 %collective-permute-start.6 = (bf16[16,16,64,128]{3,2,1,0:T(8,128)(2,1)}, bf16[16,16,64,128]{3,2,1,0:T(8,128)(2,1)S(1)}, u32[]{:S(2)}, u32[]{:S(2)}) collective-permute-start(bf16[16,16,64,128]{3,2,1,0:T(8,128)(2,1)} %bitcast.9.mine_ref), channel_id=1, source_target_pairs={{0,1},{1,0},{2,3},{3,2},{4,5},{5,4},{6,7},{7,6},{8,9},{9,8},{10,11... | collective-permute-start | bytes 12582920 | tf_op jit(solution)/shard_map/ppermute | solution.py:35
  115.8 6.8 %collective-permute-done.6.other_ref = bf16[16,16,64,128]{3,2,1,0:T(8,128)(2,1)S(1)} collective-permute-done((bf16[16,16,64,128]{3,2,1,0:T(8,128)(2,1)}, bf16[16,16,64,128]{3,2,1,0:T(8,128)(2,1)S(1)}, u32[]{:S(2)}, u32[]{:S(2)}) %collective-permute-start.6) | collective-permute-done | bytes 4194336 | tf_op jit(solution)/shard_map/ppermute | solution.py:35
  122.6 6.9 %feedforward.1 = bf16[6,18,1024]{2,1,0:T(8,128)(2,1)} custom-call(s32[1]{0:T(128)} %bitcast.core_ref, bf16[448,512]{1,0:T(8,128)(2,1)} %copy-done.9, f32[1,512]{1,0:T(1,128)S(1)} %bitcast.22, f32[1,512]{1,0:T(1,128)S(1)} %bitcast.23, f32[1,1024]{1,0:T(1,128)S(1)} %bitcast.18, f32[1,1024]{1,0:T(1,128)S(1)} %bitcast.19, ...), custom_call_target="tpu_custom_call" | custom-call | flops 6000000000 | bytes 20000000 | tf_op jit(solution)/shard_map/feedforward/pallas_call | solution.py:512
  (33 shorter events, 0.2 us)
Async XLA Ops:
  0.0 13.9 %copy-start = (bf16[32,1024]{1,0:T(8,128)(2,1)S(1)}, bf16[32,1024]{1,0:T(8,128)(2,1)}, u32[]{:S(2)}) copy-start(bf16[32,1024]{1,0:T(8,128)(2,1)} %param.28) | copy-start | bytes 196612
  0.0 24.5 %copy-start.15 = (s32[12288]{0:T(1024)S(1)}, s32[12288]{0:T(1024)}, u32[]{:S(2)}) copy-start(s32[12288]{0:T(1024)} %constant.66.clone) | copy-start | bytes 147460
  2.2 11.7 %collective-permute-start = (bf16[8,4096]{1,0:T(8,128)(2,1)S(1)}, bf16[8,4096]{1,0:T(8,128)(2,1)S(1)}, u32[]{:S(2)}, u32[]{:S(2)}) collective-permute-start(bf16[8,4096]{1,0:T(8,128)(2,1)S(1)} %constant_dynamic-update-slice_fusion), channel_id=1, source_target_pairs={{0,1},{1,0},{2,3},{3,2},{4,5},{5,4},{6,7},{7,6},{8,9},{9,8},{10,11... | collective-permute-start | bytes 196616 | tf_op jit(solution)/shard_map/ppermute | solution.py:35
  14.8 13.7 %copy-start.12 = (pred[96,128]{1,0:T(32,128)(4,1)S(1)}, pred[96,128]{1,0:T(32,128)(4,1)}, u32[]{:S(2)}) copy-start(pred[96,128]{1,0:T(32,128)(4,1)} %constant.68.clone) | copy-start | bytes 36868
  14.8 13.8 %copy-start.13 = (pred[128]{0:T(512)(128)(4,1)S(1)}, pred[128]{0:T(512)(128)(4,1)}, u32[]{:S(2)}) copy-start(pred[128]{0:T(512)(128)(4,1)} %constant.67.clone) | copy-start | bytes 388
  14.8 26.0 %all-to-all-start = ((bf16[16,80,128]{2,1,0:T(8,128)(2,1)}), bf16[16,80,128]{2,1,0:T(8,128)(2,1)S(1)}, u32[]{:S(2)}, u32[]{:S(2)}) async-start(bf16[16,80,128]{2,1,0:T(8,128)(2,1)} %broadcast_in_dim.34), calls=%async_computation | async-start | bytes 655360 | tf_op jit(solution)/shard_map/all_to_all | solution.py:40
  24.5 4.3 %copy-start.11 = (bf16[12,36,512]{2,1,0:T(8,128)(2,1)S(1)}, bf16[12,36,512]{2,1,0:T(8,128)(2,1)}, u32[]{:S(2)}) copy-start(bf16[12,36,512]{2,1,0:T(8,128)(2,1)} %param.23) | copy-start | bytes 1327108
  28.8 5.5 %collective-permute-start.1 = (bf16[3,36,512]{2,1,0:T(8,128)(2,1)S(1)}, bf16[3,36,512]{2,1,0:T(8,128)(2,1)S(1)}, u32[]{:S(2)}, u32[]{:S(2)}) collective-permute-start(bf16[3,36,512]{2,1,0:T(8,128)(2,1)S(1)} %get-tuple-element.29), channel_id=1, source_target_pairs={{0,64},{64,128},{128,192},{192,256},{256,320},{320,384},{384,448},... | collective-permute-start | bytes 331784 | tf_op jit(solution)/shard_map/ppermute | solution.py:35
  31.9 6.2 %collective-permute-start.2 = (bf16[3,36,512]{2,1,0:T(8,128)(2,1)S(1)}, bf16[3,36,512]{2,1,0:T(8,128)(2,1)S(1)}, u32[]{:S(2)}, u32[]{:S(2)}) collective-permute-start(bf16[3,36,512]{2,1,0:T(8,128)(2,1)S(1)} %get-tuple-element.30), channel_id=1, source_target_pairs={{64,0},{128,64},{192,128},{256,192},{320,256},{384,320},{448,384},... | collective-permute-start | bytes 331784 | tf_op jit(solution)/shard_map/ppermute | solution.py:35
  38.2 8.0 %copy-start.10 = (bf16[18,36,512]{2,1,0:T(8,128)(2,1)}, bf16[18,36,512]{2,1,0:T(8,128)(2,1)S(1)}, u32[]{:S(2)}) copy-start(bf16[18,36,512]{2,1,0:T(8,128)(2,1)S(1)} %pad_maximum_fusion.1) | copy-start | bytes 1990660
  42.1 21.3 %all-to-all-start.1 = ((bf16[4,16,80,128]{3,2,1,0:T(8,128)(2,1)}), bf16[4,16,80,128]{3,2,1,0:T(8,128)(2,1)S(1)}, u32[]{:S(2)}, u32[]{:S(2)}) async-start(bf16[4,16,80,128]{3,2,1,0:T(8,128)(2,1)} %broadcast_in_dim.58), calls=%async_computation.1 | async-start | bytes 2621440 | tf_op jit(solution)/shard_map/all_to_all | solution.py:80
  46.3 10.8 %collective-permute-start.3 = (bf16[18,6,512]{2,1,0:T(8,128)(2,1)S(1)}, bf16[18,6,512]{2,1,0:T(8,128)(2,1)S(1)}, u32[]{:S(2)}, u32[]{:S(2)}) collective-permute-start(bf16[18,6,512]{2,1,0:T(8,128)(2,1)S(1)} %get-tuple-element.27), channel_id=1, source_target_pairs={{0,1},{1,2},{2,3},{3,4},{4,5},{5,6},{6,7},{7,8},{8,9},{9,10},{10,1... | collective-permute-start | bytes 331784 | tf_op jit(solution)/shard_map/ppermute | solution.py:35
  55.0 6.8 %collective-permute-start.4 = (bf16[18,6,512]{2,1,0:T(8,128)(2,1)S(1)}, bf16[18,6,512]{2,1,0:T(8,128)(2,1)S(1)}, u32[]{:S(2)}, u32[]{:S(2)}) collective-permute-start(bf16[18,6,512]{2,1,0:T(8,128)(2,1)S(1)} %get-tuple-element.28), channel_id=1, source_target_pairs={{0,63},{1,0},{2,1},{3,2},{4,3},{5,4},{6,5},{7,6},{8,7},{9,8},{10,9... | collective-permute-start | bytes 331784 | tf_op jit(solution)/shard_map/ppermute | solution.py:35
  64.6 14.4 %all-to-all-start.2 = ((bf16[4,4,16,16,128]{4,3,2,1,0:T(8,128)(2,1)}), bf16[4,4,16,16,128]{4,3,2,1,0:T(8,128)(2,1)}, u32[]{:S(2)}, u32[]{:S(2)}) async-start(bf16[4,4,16,16,128]{4,3,2,1,0:T(8,128)(2,1)} %broadcast_in_dim.59), calls=%async_computation.2 | async-start | bytes 2097152 | tf_op jit(solution)/shard_map/all_to_all | solution.py:80
  69.5 2.0 %copy-start.1 = (bf16[4,4,16,64,128]{4,3,2,1,0:T(8,128)(2,1)}, bf16[4,4,16,64,128]{4,3,2,1,0:T(8,128)(2,1)S(1)}, u32[]{:S(2)}) copy-start(bf16[4,4,16,64,128]{4,3,2,1,0:T(8,128)(2,1)S(1)} %fan.1) | copy-start | bytes 12582916
  78.9 9.0 %copy-start.14 = (f32[8]{0:T(128)S(1)}, f32[8]{0:T(128)}, u32[]{:S(2)}) copy-start(f32[8]{0:T(128)} %param.29) | copy-start | bytes 100
  78.9 11.3 %copy-start.4 = (f32[512]{0:T(512)S(1)}, f32[512]{0:T(512)}, u32[]{:S(2)}) copy-start(f32[512]{0:T(512)} %param.33) | copy-start | bytes 6148
  78.9 11.3 %copy-start.5 = (f32[512]{0:T(512)S(1)}, f32[512]{0:T(512)}, u32[]{:S(2)}) copy-start(f32[512]{0:T(512)} %param.34) | copy-start | bytes 6148
  78.9 11.3 %copy-start.8 = (bf16[384,288]{1,0:T(8,128)(2,1)S(1)}, bf16[384,288]{1,0:T(8,128)(2,1)}, u32[]{:S(2)}) copy-start(bf16[384,288]{1,0:T(8,128)(2,1)} %constant.69.clone.arrange_ref) | copy-start | bytes 663556
  78.9 31.9 %all-to-all-start.3 = ((bf16[4,4,16,64,128]{4,3,2,1,0:T(8,128)(2,1)}), bf16[4,4,16,64,128]{4,3,2,1,0:T(8,128)(2,1)}, u32[]{:S(2)}, u32[]{:S(2)}) async-start(bf16[4,4,16,64,128]{4,3,2,1,0:T(8,128)(2,1)} %copy-done.1), calls=%async_computation.3 | async-start | bytes 8388608 | tf_op jit(solution)/shard_map/all_to_all | solution.py:80
  83.9 6.3 %collective-permute-start.5 = (bf16[16,16,16,128]{3,2,1,0:T(8,128)(2,1)}, bf16[16,16,16,128]{3,2,1,0:T(8,128)(2,1)S(1)}, u32[]{:S(2)}, u32[]{:S(2)}) collective-permute-start(bf16[16,16,16,128]{3,2,1,0:T(8,128)(2,1)} %bitcast.8.mine_ref), channel_id=1, source_target_pairs={{0,1},{1,0},{2,3},{3,2},{4,5},{5,4},{6,7},{7,6},{8,9},{9,8},{10,11... | collective-permute-start | bytes 3145736 | tf_op jit(solution)/shard_map/ppermute | solution.py:35
  90.3 32.3 %copy-start.2 = (f32[1024]{0:T(1024)S(1)}, f32[1024]{0:T(1024)}, u32[]{:S(2)}) copy-start(f32[1024]{0:T(1024)} %param.37) | copy-start | bytes 12292
  90.3 32.3 %copy-start.3 = (f32[1024]{0:T(1024)S(1)}, f32[1024]{0:T(1024)}, u32[]{:S(2)}) copy-start(f32[1024]{0:T(1024)} %param.38) | copy-start | bytes 12292
  90.3 32.3 %copy-start.6 = (f32[512]{0:T(512)S(1)}, f32[512]{0:T(512)}, u32[]{:S(2)}) copy-start(f32[512]{0:T(512)} %param.35) | copy-start | bytes 6148
  90.3 32.3 %copy-start.7 = (f32[512]{0:T(512)S(1)}, f32[512]{0:T(512)}, u32[]{:S(2)}) copy-start(f32[512]{0:T(512)} %param.36) | copy-start | bytes 6148
  102.0 0.8 copy-start.9
  110.9 11.7 %collective-permute-start.6 = (bf16[16,16,64,128]{3,2,1,0:T(8,128)(2,1)}, bf16[16,16,64,128]{3,2,1,0:T(8,128)(2,1)S(1)}, u32[]{:S(2)}, u32[]{:S(2)}) collective-permute-start(bf16[16,16,64,128]{3,2,1,0:T(8,128)(2,1)} %bitcast.9.mine_ref), channel_id=1, source_target_pairs={{0,1},{1,0},{2,3},{3,2},{4,5},{5,4},{6,7},{7,6},{8,9},{9,8},{10,11... | collective-permute-start | bytes 12582920 | tf_op jit(solution)/shard_map/ppermute | solution.py:35

commit v8 on v7

--- a/solution.py
+++ b/solution.py
@@ -53,7 +53,7 @@
 
 def fan_kernel(ring_ref, out_ref, sems):
     copies = [
-        pltpu.make_async_copy(ring_ref.at[:, :, pl.ds(16, 64), :], out_ref.at[i], sems.at[i])
+        pltpu.make_async_copy(ring_ref.at[:, :, pl.ds(48, 32), :], out_ref.at[i], sems.at[i])
         for i in range(4)
     ]
     for copy in copies:
@@ -66,7 +66,7 @@
     anywhere = pl.BlockSpec(memory_space=pl.ANY)
     return pl.pallas_call(
         fan_kernel,
-        out_shape=jax.ShapeDtypeStruct((4, 4, 16, 64, 128), BF16),
+        out_shape=jax.ShapeDtypeStruct((4, 4, 16, 32, 128), BF16),
         in_specs=[anywhere],
         out_specs=anywhere,
         scratch_shapes=[pltpu.SemaphoreType.DMA((4,))],
@@ -175,7 +175,7 @@
             column = pl.multiple_of((y_hi * 8 + x * 2 + of) * 128, 128)
             copies.append(
                 pltpu.make_async_copy(
-                    ref.at[m],
+                    ref.at[m, :, pl.ds(0, 16), :],
                     weight.at[:, pl.ds(row, 16), pl.ds(column, 128)],
                     sems.at[m * 2 + part],
                 )
@@ -269,21 +269,17 @@
     first_ref,
     gain_ref,
     offset_ref,
-    merge_gain_ref,
-    merge_offset_ref,
     mine_ref,
     other_ref,
     out_ref,
     up,
     down,
-    merge,
     tokens_in,
     up_sems,
     down_sems,
-    merge_sems,
 ):
     core = core_ref[0]
-    ups, downs, merges = [], [], []
+    ups, downs = [], []
     for m in range(16):
         for part, (ref, of) in enumerate(((mine_ref, core), (other_ref, 1 - core))):
             y_hi, x, y_lo = place(m, of)
@@ -291,7 +287,7 @@
             column = pl.multiple_of((y_hi * 8 + x * 2 + of) * 128, 128)
             ups.append(
                 pltpu.make_async_copy(
-                    ref.at[m, :, pl.ds(0, 16), :],
+                    ref.at[m, :, pl.ds(16, 16), :],
                     up.at[:, pl.ds(row, 16), pl.ds(column, 128)],
                     up_sems.at[m * 2 + part],
                 )
@@ -300,22 +296,13 @@
             column = pl.multiple_of(x * 128, 128)
             downs.append(
                 pltpu.make_async_copy(
-                    ref.at[m, :, pl.ds(16, 16), :],
+                    ref.at[m, :, pl.ds(32, 16), :],
                     down.at[:, pl.ds(row, 16), pl.ds(column, 128)],
                     down_sems.at[m * 2 + part],
                 )
             )
-            row = pl.multiple_of(y_lo * 64 + of * 32, 32)
-            column = pl.multiple_of((y_hi * 4 + x) * 128, 128)
-            merges.append(
-                pltpu.make_async_copy(
-                    ref.at[m, :, pl.ds(32, 32), :],
-                    merge.at[:, pl.ds(row, 32), pl.ds(column, 128)],
-                    merge_sems.at[m * 2 + part],
-                )
-            )
     ups.append(pltpu.make_async_copy(first_ref, tokens_in, up_sems.at[32]))
-    for copy in ups + downs + merges:
+    for copy in ups + downs:
         copy.start()
     for copy in ups:
         copy.wait()
@@ -333,18 +320,39 @@
         )
         total = piece if total is None else total + piece
     branch = norm_rows(total, gain_ref[...], offset_ref[...])
-    second = (tokens.astype(F32) + branch).astype(BF16)
-    for copy in merges:
+    out_ref[...] = (tokens.astype(F32) + branch).astype(BF16)
+
+
+def merge_kernel(
+    core_ref, second_ref, gain_ref, offset_ref, mine_ref, other_ref, out_ref, merge, sems
+):
+    core = core_ref[0]
+    copies = []
+    for m in range(16):
+        for part, (ref, of) in enumerate(((mine_ref, core), (other_ref, 1 - core))):
+            y_hi, x, y_lo = place(m, of)
+            row = pl.multiple_of(y_lo * 64 + of * 32, 32)
+            column = pl.multiple_of((y_hi * 4 + x) * 128, 128)
+            copies.append(
+                pltpu.make_async_copy(
+                    ref.at[m],
+                    merge.at[:, pl.ds(row, 32), pl.ds(column, 128)],
+                    sems.at[m * 2 + part],
+                )
+            )
+    for copy in copies:
+        copy.start()
+    for copy in copies:
         copy.wait()
     total = None
     for n in range(4):
         piece = jnp.dot(
-            second[n * QUAD_ROWS : (n + 1) * QUAD_ROWS],
+            second_ref[n * QUAD_ROWS : (n + 1) * QUAD_ROWS],
             merge[n * 4 : n * 4 + 4].reshape(512, 2 * D),
             preferred_element_type=F32,
         )
         total = piece if total is None else total + piece
-    reduced = norm_rows(total, merge_gain_ref[...], merge_offset_ref[...])
+    reduced = norm_rows(total, gain_ref[...], offset_ref[...])
     for i in range(6):
         out_ref[i] = reduced[i * 18 : i * 18 + 18].astype(BF16)
 
@@ -457,11 +465,11 @@
     west = shifted(strip[:, 36 - SHIFT_COLS :], LON, 1, True)
     tall = jnp.concatenate([west, strip, east], axis=1)
     in_ring, tall = lax.optimization_barrier((in_ring, tall))
-    attn_mine = spread_ring(four(in_ring[:, :, :16]), 1).reshape(16, 16, 16, 128)
+    attn_mine = spread_ring(four(in_ring[:, :, :48]), 1).reshape(16, 16, 48, 128)
     rest_copies = fan(in_ring)
     attn_mine, rest_copies = lax.optimization_barrier((attn_mine, rest_copies))
     attn_other = shifted(attn_mine, "core", 1, True)
-    rest_mine = spread_ring(rest_copies, 1).reshape(16, 16, 64, 128)
+    rest_mine = spread_ring(rest_copies, 1).reshape(16, 16, 32, 128)
 
     vmem = pl.BlockSpec(memory_space=pltpu.VMEM)
     smem = pl.BlockSpec(memory_space=pltpu.SMEM)
@@ -509,18 +517,16 @@
     )
     first, rest_mine = lax.optimization_barrier((first, rest_mine))
     rest_other = shifted(rest_mine, "core", 1, True)
-    return pl.pallas_call(
+    second = pl.pallas_call(
         feedforward_kernel,
-        out_shape=jax.ShapeDtypeStruct((6, 18, 2 * D), BF16),
-        in_specs=[smem, hbm] + [vmem] * 4 + [anywhere] * 2,
+        out_shape=jax.ShapeDtypeStruct((4 * QUAD_ROWS, D), BF16),
+        in_specs=[smem, hbm] + [vmem] * 2 + [anywhere] * 2,
         out_specs=vmem,
         scratch_shapes=[
             pltpu.VMEM((16, 32, FFN), BF16),
             pltpu.VMEM((16, 128, D), BF16),
-            pltpu.VMEM((16, 128, 2 * D), BF16),
             pltpu.VMEM((4 * QUAD_ROWS, D), BF16),
             pltpu.SemaphoreType.DMA((33,)),
-            pltpu.SemaphoreType.DMA((32,)),
             pltpu.SemaphoreType.DMA((32,)),
         ],
         compiler_params=params,
@@ -533,6 +539,23 @@
         far(first),
         feedforward_norm_gain.reshape(1, D),
         feedforward_norm_offset.reshape(1, D),
+        attn_mine,
+        attn_other,
+    )
+    return pl.pallas_call(
+        merge_kernel,
+        out_shape=jax.ShapeDtypeStruct((6, 18, 2 * D), BF16),
+        in_specs=[smem] + [vmem] * 3 + [anywhere] * 2,
+        out_specs=vmem,
+        scratch_shapes=[pltpu.VMEM((16, 128, 2 * D), BF16), pltpu.SemaphoreType.DMA((32,))],
+        compiler_params=params,
+        cost_estimate=pl.CostEstimate(
+            flops=1_000_000_000, bytes_accessed=8_000_000, transcendentals=0
+        ),
+        name="merging",
+    )(
+        core_index,
+        second,
         merging_norm_gain.reshape(1, 2 * D),
         merging_norm_offset.reshape(1, 2 * D),
         rest_mine,

time: 131 us -> 128 us (0.977)
  waiting for transfers between devices: 36.7 us -> 33.4 us
  starting transfers between devices: 55.8 us -> 52.6 us
  local copies, waits for them, and re-layouts: 9.88 us -> 12.5 us
  Pallas kernels: 19.2 us -> 20.8 us
    ppermute x7, waiting for transfers between devices: 18.6 us -> 11.1 us  [shifted(): return lax.ppermute(block, axes, pairs)]
    all_to_all x3, waiting for transfers between devices: 15.5 us -> 19.7 us  [spread_ring(): return lax.all_to_all(copies, ALL, 0, 0, axis_index_groups=rings(x_core))]
    ppermute x7, starting transfers between devices: 32.7 us -> 30.1 us  [shifted(): return lax.ppermute(block, axes, pairs)]
    unnamed x34, local copies, waits for them, and re-layouts: 4.36 us -> 5.86 us
    pallas_call x2 -> x3, Pallas kernels: 7.53 us -> 8.81 us  [the longest x1 5.29 us: local(): pl.pallas_call(feedforward_kernel, out_shape=jax.ShapeDtypeStruct((4 * QU...]
  transfers between devices with their start and end apart: 11 -> 11, of which waited for: 9 -> 7; matrix products, arithmetic and copies ran while one was open for 7% -> 7% of each run, Pallas kernels for 10% -> 14%
where the time goes in v8:
time: 128 us; the launch traced here: 127 us
  starting transfers between devices  52.6 us (41%)
  waiting for transfers between devices  33.4 us (26%)
  Pallas kernels  20.8 us (16%)
  local copies, waits for them, and re-layouts  12.5 us (10%)
  matrix products  5.38 us (4%)
  other arithmetic  1.94 us (2%)
    ppermute x7, starting transfers between devices, shifted(): return lax.ppermute(block, axes, pairs)  30.1 us
    all_to_all x3, waiting for transfers between devices, spread_ring(): return lax.all_to_all(copies, ALL, 0, 0, axis_index_groups=rings(x_core))  19.7 us
    all_to_all x3, starting transfers between devices, spread_ring(): return lax.all_to_all(copies, ALL, 0, 0, axis_index_groups=rings(x_core))  12.9 us
    pallas_call x1, Pallas kernels, local(): pl.pallas_call(attention_kernel, out_shape=jax.ShapeDtypeStruct((4 * QUAD...  12 us
    ppermute x7, waiting for transfers between devices, shifted(): return lax.ppermute(block, axes, pairs)  11.1 us
    all_to_all x1, starting transfers between devices, spread(): lax.all_to_all(jnp.broadcast_to(block[None], (size,) + block.shape), axes...  9.67 us
    unnamed x34, local copies, waits for them, and re-layouts  5.86 us
    pallas_call x1, Pallas kernels, local(): pl.pallas_call(feedforward_kernel, out_shape=jax.ShapeDtypeStruct((4 * QU...  5.29 us
  transfers between devices with their start and end apart: 11, of which 7 were waited for; matrix products, arithmetic and copies ran while one was open for 7% of the time, Pallas kernels for 14%

profile of v8, /device:TPU:1, one launch (start us, length us, event | category | flops | bytes accessed | tf_op | source)
XLA Modules:
  0.0 127.2 jit_solution(5093751041884118989)
XLA Ops:
  0.0 0.8 constant_dynamic-update-slice_fusion.2
  0.8 0.7 constant_dynamic-update-slice_fusion.1
  1.5 0.8 constant_dynamic-update-slice_fusion
  2.2 8.8 %collective-permute-start = (bf16[8,4096]{1,0:T(8,128)(2,1)S(1)}, bf16[8,4096]{1,0:T(8,128)(2,1)S(1)}, u32[]{:S(2)}, u32[]{:S(2)}) collective-permute-start(bf16[8,4096]{1,0:T(8,128)(2,1)S(1)} %constant_dynamic-update-slice_fusion), channel_id=1, source_target_pairs={{0,1},{1,0},{2,3},{3,2},{4,5},{5,4},{6,7},{7,6},{8,9},{9,8},{10,11... | collective-permute-start | bytes 196616 | tf_op jit(solution)/shard_map/ppermute | solution.py:35
  11.0 0.8 fusion.23
  11.8 0.7 dynamic_slice.14
  12.5 1.4 %fusion.6 = f32[253,8]{0,1:T(8,128)S(1)} fusion(f32[512,8]{0,1:T(8,128)} %param.32, f32[512]{0:T(512)} %param.31, f32[512]{0:T(512)S(1)} %bitcast.28, f32[253]{0:T(256)} %constant.81, f32[512]{0:T(512)S(1)} %bitcast.27, f32[253]{0:T(256)} %constant.79), kind=kOutput, calls=%fused_computation.8 | convolution fusion | flops 13091232 | bytes 32648 | tf_op jit(solution)/shard_map/dot_general | solution.py:109
  14.0 0.8 broadcast_in_dim.34
  14.8 9.7 %all-to-all-start = ((bf16[16,80,128]{2,1,0:T(8,128)(2,1)}), bf16[16,80,128]{2,1,0:T(8,128)(2,1)S(1)}, u32[]{:S(2)}, u32[]{:S(2)}) async-start(bf16[16,80,128]{2,1,0:T(8,128)(2,1)} %broadcast_in_dim.34), calls=%async_computation | async-start | bytes 655360 | tf_op jit(solution)/shard_map/all_to_all | solution.py:40
  24.5 0.0 copy-start.11
  24.5 4.0 %fusion.2 = f32[8,96,128]{2,0,1:T(8,128)S(1)} fusion(f32[253,8]{0,1:T(8,128)S(1)} %fusion.6, s32[12288]{0:T(1024)S(1)} %copy-done.15), kind=kOutput, calls=%fused_computation.3 | convolution fusion | flops 301559808 | bytes 450464 | tf_op jit(solution)/shard_map/dot_general | solution.py:452
  28.5 0.1 pad_add_fusion
  28.5 0.1 broadcast_and_fusion
  28.7 0.1 copy_select_fusion
  28.8 3.1 %collective-permute-start.1 = (bf16[3,36,512]{2,1,0:T(8,128)(2,1)S(1)}, bf16[3,36,512]{2,1,0:T(8,128)(2,1)S(1)}, u32[]{:S(2)}, u32[]{:S(2)}) collective-permute-start(bf16[3,36,512]{2,1,0:T(8,128)(2,1)S(1)} %get-tuple-element.29), channel_id=1, source_target_pairs={{0,64},{64,128},{128,192},{192,256},{256,320},{320,384},{384,448},... | collective-permute-start | bytes 331784 | tf_op jit(solution)/shard_map/ppermute | solution.py:35
  31.9 1.3 %collective-permute-start.2 = (bf16[3,36,512]{2,1,0:T(8,128)(2,1)S(1)}, bf16[3,36,512]{2,1,0:T(8,128)(2,1)S(1)}, u32[]{:S(2)}, u32[]{:S(2)}) collective-permute-start(bf16[3,36,512]{2,1,0:T(8,128)(2,1)S(1)} %get-tuple-element.30), channel_id=1, source_target_pairs={{64,0},{128,64},{192,128},{256,192},{320,256},{384,320},{448,384},... | collective-permute-start | bytes 331784 | tf_op jit(solution)/shard_map/ppermute | solution.py:35
  33.2 0.1 broadcast_select_fusion.bias_ref
  33.4 1.0 collective-permute-done.1
  34.3 3.8 %collective-permute-done.2 = bf16[3,36,512]{2,1,0:T(8,128)(2,1)S(1)} collective-permute-done((bf16[3,36,512]{2,1,0:T(8,128)(2,1)S(1)}, bf16[3,36,512]{2,1,0:T(8,128)(2,1)S(1)}, u32[]{:S(2)}, u32[]{:S(2)}) %collective-permute-start.2) | collective-permute-done | bytes 110624 | tf_op jit(solution)/shard_map/ppermute | solution.py:35
  38.1 0.1 pad_maximum_fusion.1
  38.2 2.6 %all-to-all-done = bf16[16,80,128]{2,1,0:T(8,128)(2,1)S(1)} async-done(((bf16[16,80,128]{2,1,0:T(8,128)(2,1)}), bf16[16,80,128]{2,1,0:T(8,128)(2,1)S(1)}, u32[]{:S(2)}, u32[]{:S(2)}) %all-to-all-start) | async-done | bytes 327712 | tf_op jit(solution)/shard_map/all_to_all | solution.py:40
  40.8 1.2 broadcast_in_dim.58
  42.1 4.2 %all-to-all-start.1 = ((bf16[4,16,80,128]{3,2,1,0:T(8,128)(2,1)}), bf16[4,16,80,128]{3,2,1,0:T(8,128)(2,1)S(1)}, u32[]{:S(2)}, u32[]{:S(2)}) async-start(bf16[4,16,80,128]{3,2,1,0:T(8,128)(2,1)} %broadcast_in_dim.58), calls=%async_computation.1 | async-start | bytes 2621440 | tf_op jit(solution)/shard_map/all_to_all | solution.py:80
  46.3 8.7 %collective-permute-start.3 = (bf16[18,6,512]{2,1,0:T(8,128)(2,1)S(1)}, bf16[18,6,512]{2,1,0:T(8,128)(2,1)S(1)}, u32[]{:S(2)}, u32[]{:S(2)}) collective-permute-start(bf16[18,6,512]{2,1,0:T(8,128)(2,1)S(1)} %get-tuple-element.27), channel_id=1, source_target_pairs={{0,1},{1,2},{2,3},{3,4},{4,5},{5,6},{6,7},{7,8},{8,9},{9,10},{10,1... | collective-permute-start | bytes 331784 | tf_op jit(solution)/shard_map/ppermute | solution.py:35
  55.0 1.9 %collective-permute-start.4 = (bf16[18,6,512]{2,1,0:T(8,128)(2,1)S(1)}, bf16[18,6,512]{2,1,0:T(8,128)(2,1)S(1)}, u32[]{:S(2)}, u32[]{:S(2)}) collective-permute-start(bf16[18,6,512]{2,1,0:T(8,128)(2,1)S(1)} %get-tuple-element.28), channel_id=1, source_target_pairs={{0,63},{1,0},{2,1},{3,2},{4,3},{5,4},{6,5},{7,6},{8,7},{9,8},{10,9... | collective-permute-start | bytes 331784 | tf_op jit(solution)/shard_map/ppermute | solution.py:35
  57.0 0.2 collective-permute-done.3
  57.1 4.7 %collective-permute-done.4 = bf16[18,6,512]{2,1,0:T(8,128)(2,1)S(1)} collective-permute-done((bf16[18,6,512]{2,1,0:T(8,128)(2,1)S(1)}, bf16[18,6,512]{2,1,0:T(8,128)(2,1)S(1)}, u32[]{:S(2)}, u32[]{:S(2)}) %collective-permute-start.4) | collective-permute-done | bytes 110624 | tf_op jit(solution)/shard_map/ppermute | solution.py:35
  61.8 1.4 %pad_maximum_fusion.tall_ref = bf16[18,48,512]{2,1,0:T(8,128)(2,1)} fusion(bf16[18,6,512]{2,1,0:T(8,128)(2,1)S(1)} %collective-permute-done.4, bf16[18,36,512]{2,1,0:T(8,128)(2,1)S(1)} %pad_maximum_fusion.1, bf16[18,6,512]{2,1,0:T(8,128)(2,1)S(1)} %collective-permute-done.3), kind=kLoop, calls=%fused_computation.9 | loop fusion | flops 2654208 | bytes 1769472 | tf_op jit(solution)/shard_map/concatenate | solution.py:466
  63.2 0.1 slice.35
  63.2 2.3 %broadcast_in_dim.59 = bf16[4,4,16,48,128]{4,3,2,1,0:T(8,128)(2,1)} broadcast(bf16[4,16,48,128]{3,2,1,0:T(8,128)(2,1)S(1)} %slice.35), dimensions={1,2,3,4} | broadcast | bytes 3932160 | tf_op jit(solution)/shard_map/broadcast_in_dim | solution.py:51
  65.5 4.7 %all-to-all-start.2 = ((bf16[4,4,16,48,128]{4,3,2,1,0:T(8,128)(2,1)}), bf16[4,4,16,48,128]{4,3,2,1,0:T(8,128)(2,1)}, u32[]{:S(2)}, u32[]{:S(2)}) async-start(bf16[4,4,16,48,128]{4,3,2,1,0:T(8,128)(2,1)} %broadcast_in_dim.59), calls=%async_computation.2 | async-start | bytes 6291456 | tf_op jit(solution)/shard_map/all_to_all | solution.py:80
  70.2 0.0 copy-start.14
  70.2 0.2 fan.1
  70.4 1.4 %copy-done.1 = bf16[4,4,16,32,128]{4,3,2,1,0:T(8,128)(2,1)} copy-done((bf16[4,4,16,32,128]{4,3,2,1,0:T(8,128)(2,1)}, bf16[4,4,16,32,128]{4,3,2,1,0:T(8,128)(2,1)S(1)}, u32[]{:S(2)}) %copy-start.1) | copy-done | bytes 2097176
  71.8 19.7 %all-to-all-done.2 = bf16[4,4,16,48,128]{4,3,2,1,0:T(8,128)(2,1)} async-done(((bf16[4,4,16,48,128]{4,3,2,1,0:T(8,128)(2,1)}), bf16[4,4,16,48,128]{4,3,2,1,0:T(8,128)(2,1)}, u32[]{:S(2)}, u32[]{:S(2)}) %all-to-all-start.2) | async-done | bytes 3145760 | tf_op jit(solution)/shard_map/all_to_all | solution.py:80
  91.5 3.7 %collective-permute-start.5 = (bf16[16,16,48,128]{3,2,1,0:T(8,128)(2,1)}, bf16[16,16,48,128]{3,2,1,0:T(8,128)(2,1)}, u32[]{:S(2)}, u32[]{:S(2)}) collective-permute-start(bf16[16,16,48,128]{3,2,1,0:T(8,128)(2,1)} %bitcast.8.mine_ref), channel_id=1, source_target_pairs={{0,1},{1,0},{2,3},{3,2},{4,5},{5,4},{6,7},{7,6},{8,9},{9,8},{10,11... | collective-permute-start | bytes 9437192 | tf_op jit(solution)/shard_map/ppermute | solution.py:35
  95.3 0.0 copy-start.5
  95.3 4.0 %all-to-all-start.3 = ((bf16[4,4,16,32,128]{4,3,2,1,0:T(8,128)(2,1)}), bf16[4,4,16,32,128]{4,3,2,1,0:T(8,128)(2,1)S(1)}, u32[]{:S(2)}, u32[]{:S(2)}) async-start(bf16[4,4,16,32,128]{4,3,2,1,0:T(8,128)(2,1)} %copy-done.1), calls=%async_computation.3 | async-start | bytes 4194304 | tf_op jit(solution)/shard_map/all_to_all | solution.py:80
  99.4 1.5 %collective-permute-done.5.other_ref = bf16[16,16,48,128]{3,2,1,0:T(8,128)(2,1)} collective-permute-done((bf16[16,16,48,128]{3,2,1,0:T(8,128)(2,1)}, bf16[16,16,48,128]{3,2,1,0:T(8,128)(2,1)}, u32[]{:S(2)}, u32[]{:S(2)}) %collective-permute-start.5) | collective-permute-done | bytes 3145760 | tf_op jit(solution)/shard_map/ppermute | solution.py:35
  100.9 1.2 copy-done.2
  102.1 1.0 copy-done.9
  103.0 12.0 %attention.1.first_ref = bf16[448,512]{1,0:T(8,128)(2,1)S(1)} custom-call(s32[1]{0:T(128)} %bitcast.core_ref, f32[8]{0:T(128)S(1)} %minimum_exponential_fusion.scale_ref, bf16[18,48,512]{2,1,0:T(8,128)(2,1)S(1)} %copy-done.2, f32[3,8,96,128]{3,2,1,0:T(8,128)S(1)} %broadcast_select_fusion.bias_ref, bf16[384,288]{1,0:T(8,128)(2,1)S(1)} %copy-done.9, ...), custom_call_target="tpu_custom_call" | custom-call | flops 20000000000 | bytes 20000000 | tf_op jit(solution)/shard_map/attention/pallas_call | solution.py:485
  115.1 0.8 copy-done.10
  115.9 2.5 %collective-permute-start.6 = (bf16[16,16,32,128]{3,2,1,0:T(8,128)(2,1)S(1)}, bf16[16,16,32,128]{3,2,1,0:T(8,128)(2,1)S(1)}, u32[]{:S(2)}, u32[]{:S(2)}) collective-permute-start(bf16[16,16,32,128]{3,2,1,0:T(8,128)(2,1)S(1)} %bitcast.18), channel_id=1, source_target_pairs={{0,1},{1,0},{2,3},{3,2},{4,5},{5,4},{6,7},{7,6},{8,9},{9,8},{10,11... | collective-permute-start | bytes 6291464 | tf_op jit(solution)/shard_map/ppermute | solution.py:35
  118.4 0.0 copy-start.3
  118.4 0.0 copy-start.4
  118.4 5.3 %feedforward.1.second_ref = bf16[448,512]{1,0:T(8,128)(2,1)S(1)} custom-call(s32[1]{0:T(128)} %bitcast.core_ref, bf16[448,512]{1,0:T(8,128)(2,1)} %copy-done.10, f32[1,512]{1,0:T(1,128)S(1)} %bitcast.24, f32[1,512]{1,0:T(1,128)S(1)} %bitcast.25, bf16[16,16,48,128]{3,2,1,0:T(8,128)(2,1)} %bitcast.8.mine_ref, ...), custom_call_target="tpu_custom_call" | custom-call | flops 6000000000 | bytes 20000000 | tf_op jit(solution)/shard_map/feedforward/pallas_call | solution.py:520
  123.7 3.3 %merging.1 = bf16[6,18,1024]{2,1,0:T(8,128)(2,1)} custom-call(s32[1]{0:T(128)} %bitcast.core_ref, bf16[448,512]{1,0:T(8,128)(2,1)S(1)} %feedforward.1.second_ref, f32[1,1024]{1,0:T(1,128)S(1)} %bitcast.20, f32[1,1024]{1,0:T(1,128)S(1)} %bitcast.21, bf16[16,16,32,128]{3,2,1,0:T(8,128)(2,1)S(1)} %bitcast.19, ...), custom_call_target="tpu_custom_call" | custom-call | flops 1000000000 | bytes 8000000 | tf_op jit(solution)/shard_map/merging/pallas_call | solution.py:545
  (34 shorter events, 0.2 us)
Async XLA Ops:
  0.0 13.9 %copy-start = (bf16[32,1024]{1,0:T(8,128)(2,1)S(1)}, bf16[32,1024]{1,0:T(8,128)(2,1)}, u32[]{:S(2)}) copy-start(bf16[32,1024]{1,0:T(8,128)(2,1)} %param.28) | copy-start | bytes 196612
  0.0 24.5 %copy-start.15 = (s32[12288]{0:T(1024)S(1)}, s32[12288]{0:T(1024)}, u32[]{:S(2)}) copy-start(s32[12288]{0:T(1024)} %constant.66.clone) | copy-start | bytes 147460
  2.2 11.7 %collective-permute-start = (bf16[8,4096]{1,0:T(8,128)(2,1)S(1)}, bf16[8,4096]{1,0:T(8,128)(2,1)S(1)}, u32[]{:S(2)}, u32[]{:S(2)}) collective-permute-start(bf16[8,4096]{1,0:T(8,128)(2,1)S(1)} %constant_dynamic-update-slice_fusion), channel_id=1, source_target_pairs={{0,1},{1,0},{2,3},{3,2},{4,5},{5,4},{6,7},{7,6},{8,9},{9,8},{10,11... | collective-permute-start | bytes 196616 | tf_op jit(solution)/shard_map/ppermute | solution.py:35
  14.8 13.7 %copy-start.12 = (pred[96,128]{1,0:T(32,128)(4,1)S(1)}, pred[96,128]{1,0:T(32,128)(4,1)}, u32[]{:S(2)}) copy-start(pred[96,128]{1,0:T(32,128)(4,1)} %constant.68.clone) | copy-start | bytes 36868
  14.8 13.8 %copy-start.13 = (pred[128]{0:T(512)(128)(4,1)S(1)}, pred[128]{0:T(512)(128)(4,1)}, u32[]{:S(2)}) copy-start(pred[128]{0:T(512)(128)(4,1)} %constant.67.clone) | copy-start | bytes 388
  14.8 26.0 %all-to-all-start = ((bf16[16,80,128]{2,1,0:T(8,128)(2,1)}), bf16[16,80,128]{2,1,0:T(8,128)(2,1)S(1)}, u32[]{:S(2)}, u32[]{:S(2)}) async-start(bf16[16,80,128]{2,1,0:T(8,128)(2,1)} %broadcast_in_dim.34), calls=%async_computation | async-start | bytes 655360 | tf_op jit(solution)/shard_map/all_to_all | solution.py:40
  24.5 4.3 %copy-start.11 = (bf16[12,36,512]{2,1,0:T(8,128)(2,1)S(1)}, bf16[12,36,512]{2,1,0:T(8,128)(2,1)}, u32[]{:S(2)}) copy-start(bf16[12,36,512]{2,1,0:T(8,128)(2,1)} %param.23) | copy-start | bytes 1327108
  28.8 5.5 %collective-permute-start.1 = (bf16[3,36,512]{2,1,0:T(8,128)(2,1)S(1)}, bf16[3,36,512]{2,1,0:T(8,128)(2,1)S(1)}, u32[]{:S(2)}, u32[]{:S(2)}) collective-permute-start(bf16[3,36,512]{2,1,0:T(8,128)(2,1)S(1)} %get-tuple-element.29), channel_id=1, source_target_pairs={{0,64},{64,128},{128,192},{192,256},{256,320},{320,384},{384,448},... | collective-permute-start | bytes 331784 | tf_op jit(solution)/shard_map/ppermute | solution.py:35
  31.9 6.2 %collective-permute-start.2 = (bf16[3,36,512]{2,1,0:T(8,128)(2,1)S(1)}, bf16[3,36,512]{2,1,0:T(8,128)(2,1)S(1)}, u32[]{:S(2)}, u32[]{:S(2)}) collective-permute-start(bf16[3,36,512]{2,1,0:T(8,128)(2,1)S(1)} %get-tuple-element.30), channel_id=1, source_target_pairs={{64,0},{128,64},{192,128},{256,192},{320,256},{384,320},{448,384},... | collective-permute-start | bytes 331784 | tf_op jit(solution)/shard_map/ppermute | solution.py:35
  42.1 21.1 %all-to-all-start.1 = ((bf16[4,16,80,128]{3,2,1,0:T(8,128)(2,1)}), bf16[4,16,80,128]{3,2,1,0:T(8,128)(2,1)S(1)}, u32[]{:S(2)}, u32[]{:S(2)}) async-start(bf16[4,16,80,128]{3,2,1,0:T(8,128)(2,1)} %broadcast_in_dim.58), calls=%async_computation.1 | async-start | bytes 2621440 | tf_op jit(solution)/shard_map/all_to_all | solution.py:80
  46.3 10.8 %collective-permute-start.3 = (bf16[18,6,512]{2,1,0:T(8,128)(2,1)S(1)}, bf16[18,6,512]{2,1,0:T(8,128)(2,1)S(1)}, u32[]{:S(2)}, u32[]{:S(2)}) collective-permute-start(bf16[18,6,512]{2,1,0:T(8,128)(2,1)S(1)} %get-tuple-element.27), channel_id=1, source_target_pairs={{0,1},{1,2},{2,3},{3,4},{4,5},{5,6},{6,7},{7,8},{8,9},{9,10},{10,1... | collective-permute-start | bytes 331784 | tf_op jit(solution)/shard_map/ppermute | solution.py:35
  55.0 6.8 %collective-permute-start.4 = (bf16[18,6,512]{2,1,0:T(8,128)(2,1)S(1)}, bf16[18,6,512]{2,1,0:T(8,128)(2,1)S(1)}, u32[]{:S(2)}, u32[]{:S(2)}) collective-permute-start(bf16[18,6,512]{2,1,0:T(8,128)(2,1)S(1)} %get-tuple-element.28), channel_id=1, source_target_pairs={{0,63},{1,0},{2,1},{3,2},{4,3},{5,4},{6,5},{7,6},{8,7},{9,8},{10,9... | collective-permute-start | bytes 331784 | tf_op jit(solution)/shard_map/ppermute | solution.py:35
  65.5 26.0 %all-to-all-start.2 = ((bf16[4,4,16,48,128]{4,3,2,1,0:T(8,128)(2,1)}), bf16[4,4,16,48,128]{4,3,2,1,0:T(8,128)(2,1)}, u32[]{:S(2)}, u32[]{:S(2)}) async-start(bf16[4,4,16,48,128]{4,3,2,1,0:T(8,128)(2,1)} %broadcast_in_dim.59), calls=%async_computation.2 | async-start | bytes 6291456 | tf_op jit(solution)/shard_map/all_to_all | solution.py:80
  70.2 25.1 %copy-start.14 = (f32[8]{0:T(128)S(1)}, f32[8]{0:T(128)}, u32[]{:S(2)}) copy-start(f32[8]{0:T(128)} %param.29) | copy-start | bytes 100
  70.4 1.4 %copy-start.1 = (bf16[4,4,16,32,128]{4,3,2,1,0:T(8,128)(2,1)}, bf16[4,4,16,32,128]{4,3,2,1,0:T(8,128)(2,1)S(1)}, u32[]{:S(2)}) copy-start(bf16[4,4,16,32,128]{4,3,2,1,0:T(8,128)(2,1)S(1)} %fan.1) | copy-start | bytes 6291460
  91.5 9.4 %collective-permute-start.5 = (bf16[16,16,48,128]{3,2,1,0:T(8,128)(2,1)}, bf16[16,16,48,128]{3,2,1,0:T(8,128)(2,1)}, u32[]{:S(2)}, u32[]{:S(2)}) collective-permute-start(bf16[16,16,48,128]{3,2,1,0:T(8,128)(2,1)} %bitcast.8.mine_ref), channel_id=1, source_target_pairs={{0,1},{1,0},{2,3},{3,2},{4,5},{5,4},{6,7},{7,6},{8,9},{9,8},{10,11... | collective-permute-start | bytes 9437192 | tf_op jit(solution)/shard_map/ppermute | solution.py:35
  95.3 5.6 %copy-start.5 = (f32[512]{0:T(512)S(1)}, f32[512]{0:T(512)}, u32[]{:S(2)}) copy-start(f32[512]{0:T(512)} %param.33) | copy-start | bytes 6148
  95.3 5.6 %copy-start.6 = (f32[512]{0:T(512)S(1)}, f32[512]{0:T(512)}, u32[]{:S(2)}) copy-start(f32[512]{0:T(512)} %param.34) | copy-start | bytes 6148
  95.3 20.6 %all-to-all-start.3 = ((bf16[4,4,16,32,128]{4,3,2,1,0:T(8,128)(2,1)}), bf16[4,4,16,32,128]{4,3,2,1,0:T(8,128)(2,1)S(1)}, u32[]{:S(2)}, u32[]{:S(2)}) async-start(bf16[4,4,16,32,128]{4,3,2,1,0:T(8,128)(2,1)} %copy-done.1), calls=%async_computation.3 | async-start | bytes 4194304 | tf_op jit(solution)/shard_map/all_to_all | solution.py:80
  100.9 1.2 copy-start.2
  102.1 1.0 copy-start.9
  103.0 15.4 %copy-start.7 = (f32[512]{0:T(512)S(1)}, f32[512]{0:T(512)}, u32[]{:S(2)}) copy-start(f32[512]{0:T(512)} %param.35) | copy-start | bytes 6148
  103.0 15.4 %copy-start.8 = (f32[512]{0:T(512)S(1)}, f32[512]{0:T(512)}, u32[]{:S(2)}) copy-start(f32[512]{0:T(512)} %param.36) | copy-start | bytes 6148
  115.0 0.8 copy-start.10
  115.9 7.8 %collective-permute-start.6 = (bf16[16,16,32,128]{3,2,1,0:T(8,128)(2,1)S(1)}, bf16[16,16,32,128]{3,2,1,0:T(8,128)(2,1)S(1)}, u32[]{:S(2)}, u32[]{:S(2)}) collective-permute-start(bf16[16,16,32,128]{3,2,1,0:T(8,128)(2,1)S(1)} %bitcast.18), channel_id=1, source_target_pairs={{0,1},{1,0},{2,3},{3,2},{4,5},{5,4},{6,7},{7,6},{8,9},{9,8},{10,11... | collective-permute-start | bytes 6291464 | tf_op jit(solution)/shard_map/ppermute | solution.py:35
  118.4 5.3 %copy-start.3 = (f32[1024]{0:T(1024)S(1)}, f32[1024]{0:T(1024)}, u32[]{:S(2)}) copy-start(f32[1024]{0:T(1024)} %param.37) | copy-start | bytes 12292
  118.4 5.3 %copy-start.4 = (f32[1024]{0:T(1024)S(1)}, f32[1024]{0:T(1024)}, u32[]{:S(2)}) copy-start(f32[1024]{0:T(1024)} %param.38) | copy-start | bytes 12292

commit v9 on v8

--- a/solution.py
+++ b/solution.py
@@ -147,9 +147,9 @@
 def attention_kernel(
     core_ref,
     scale_ref,
-    tall_ref,
+    tall_in,
     bias_ref,
-    arrange_ref,
+    arrange_in,
     patch_select_ref,
     select_ref,
     gain_ref,
@@ -164,6 +164,8 @@
     heads,
     patch_select,
     select,
+    tall_ref,
+    arrange_ref,
     sems,
 ):
     core = core_ref[0]
@@ -180,6 +182,8 @@
                     sems.at[m * 2 + part],
                 )
             )
+    copies.append(pltpu.make_async_copy(tall_in, tall_ref, sems.at[34]))
+    copies.append(pltpu.make_async_copy(arrange_in, arrange_ref, sems.at[35]))
     late = [
         pltpu.make_async_copy(select_ref, select, sems.at[32]),
         pltpu.make_async_copy(patch_select_ref, patch_select, sems.at[33]),
@@ -485,7 +489,7 @@
     first = pl.pallas_call(
         attention_kernel,
         out_shape=jax.ShapeDtypeStruct((4 * QUAD_ROWS, D), BF16),
-        in_specs=[smem, smem] + [vmem] * 3 + [hbm] * 2 + [vmem] * 2 + [anywhere] * 2,
+        in_specs=[smem, smem, hbm, vmem] + [hbm] * 3 + [vmem] * 2 + [anywhere] * 2,
         out_specs=vmem,
         scratch_shapes=[
             pltpu.VMEM((16, 32, 2048), BF16),
@@ -495,7 +499,9 @@
             pltpu.VMEM((768, D), BF16),
             pltpu.VMEM((4 * QUAD_ROWS, 864), BF16),
             pltpu.VMEM((4 * QUAD_ROWS, 768), BF16),
-            pltpu.SemaphoreType.DMA((34,)),
+            pltpu.VMEM((18, 48, D), BF16),
+            pltpu.VMEM((WINS * WIN_PAD, WIN_ROWS * 48), BF16),
+            pltpu.SemaphoreType.DMA((36,)),
         ],
         compiler_params=params,
         cost_estimate=pl.CostEstimate(
@@ -505,9 +511,9 @@
     )(
         core_index,
         head_scale,
-        tall,
+        far(tall),
         bias,
-        jnp.asarray(arrangement(), BF16),
+        far(jnp.asarray(arrangement(), BF16)),
         far(jnp.asarray(patch_selection(), BF16)),
         far(jnp.asarray(selection(), BF16)),
         attention_norm_gain.reshape(1, D),

time: 128 us -> 127 us (level)
  local copies, waits for them, and re-layouts: 12.5 us -> 10.4 us
    unnamed x34 -> x30, local copies, waits for them, and re-layouts: 5.86 us -> 3.74 us
  transfers between devices with their start and end apart: 11 -> 11, of which waited for: 7 -> 8; matrix products, arithmetic and copies ran while one was open for 7% -> 7% of each run, Pallas kernels for 14% -> 14%
where the time goes in v9:
time: 127 us; the launch traced here: 126 us
  starting transfers between devices  52.7 us (41%)
  waiting for transfers between devices  34.3 us (27%)
  Pallas kernels  21.2 us (17%)
  local copies, waits for them, and re-layouts  10.4 us (8%)
  matrix products  5.38 us (4%)
  other arithmetic  1.92 us (2%)
    ppermute x7, starting transfers between devices, shifted(): return lax.ppermute(block, axes, pairs)  30.1 us
    all_to_all x3, waiting for transfers between devices, spread_ring(): return lax.all_to_all(copies, ALL, 0, 0, axis_index_groups=rings(x_core))  20.5 us
    all_to_all x3, starting transfers between devices, spread_ring(): return lax.all_to_all(copies, ALL, 0, 0, axis_index_groups=rings(x_core))  12.9 us
    pallas_call x1, Pallas kernels, local(): pl.pallas_call(attention_kernel, out_shape=jax.ShapeDtypeStruct((4 * QUAD...  12.4 us
    ppermute x7, waiting for transfers between devices, shifted(): return lax.ppermute(block, axes, pairs)  11.1 us
    all_to_all x1, starting transfers between devices, spread(): lax.all_to_all(jnp.broadcast_to(block[None], (size,) + block.shape), axes...  9.67 us
    pallas_call x1, Pallas kernels, local(): pl.pallas_call(feedforward_kernel, out_shape=jax.ShapeDtypeStruct((4 * QU...  5.28 us
    dot_general x1, matrix products, local(): bias = jnp.dot(table, one_hot, precision=lax.Precision.HIGHEST)  3.95 us
  transfers between devices with their start and end apart: 11, of which 8 were waited for; matrix products, arithmetic and copies ran while one was open for 7% of the time, Pallas kernels for 14%

profile of v9, /device:TPU:1, one launch (start us, length us, event | category | flops | bytes accessed | tf_op | source)
XLA Modules:
  0.0 126.4 jit_solution(10309717200817227644)
XLA Ops:
  0.0 0.8 constant_dynamic-update-slice_fusion.2
  0.8 0.7 constant_dynamic-update-slice_fusion.1
  1.5 0.8 constant_dynamic-update-slice_fusion
  2.2 8.8 %collective-permute-start = (bf16[8,4096]{1,0:T(8,128)(2,1)S(1)}, bf16[8,4096]{1,0:T(8,128)(2,1)S(1)}, u32[]{:S(2)}, u32[]{:S(2)}) collective-permute-start(bf16[8,4096]{1,0:T(8,128)(2,1)S(1)} %constant_dynamic-update-slice_fusion), channel_id=1, source_target_pairs={{0,1},{1,0},{2,3},{3,2},{4,5},{5,4},{6,7},{7,6},{8,9},{9,8},{10,11... | collective-permute-start | bytes 196616 | tf_op jit(solution)/shard_map/ppermute | solution.py:35
  11.0 0.8 fusion.23
  11.8 0.7 dynamic_slice.14
  12.5 1.4 %fusion.6 = f32[253,8]{0,1:T(8,128)S(1)} fusion(f32[512,8]{0,1:T(8,128)} %param.32, f32[512]{0:T(512)} %param.31, f32[512]{0:T(512)S(1)} %bitcast.28, f32[253]{0:T(256)} %constant.81, f32[512]{0:T(512)S(1)} %bitcast.27, f32[253]{0:T(256)} %constant.79), kind=kOutput, calls=%fused_computation.8 | convolution fusion | flops 13091232 | bytes 32648 | tf_op jit(solution)/shard_map/dot_general | solution.py:109
  14.0 0.8 broadcast_in_dim.34
  14.8 9.7 %all-to-all-start = ((bf16[16,80,128]{2,1,0:T(8,128)(2,1)}), bf16[16,80,128]{2,1,0:T(8,128)(2,1)S(1)}, u32[]{:S(2)}, u32[]{:S(2)}) async-start(bf16[16,80,128]{2,1,0:T(8,128)(2,1)} %broadcast_in_dim.34), calls=%async_computation | async-start | bytes 655360 | tf_op jit(solution)/shard_map/all_to_all | solution.py:40
  24.5 0.0 copy-start.9
  24.5 4.0 %fusion.2 = f32[8,96,128]{2,0,1:T(8,128)S(1)} fusion(f32[253,8]{0,1:T(8,128)S(1)} %fusion.6, s32[12288]{0:T(1024)S(1)} %copy-done.13), kind=kOutput, calls=%fused_computation.3 | convolution fusion | flops 301559808 | bytes 450464 | tf_op jit(solution)/shard_map/dot_general | solution.py:456
  28.5 0.1 pad_add_fusion
  28.5 0.1 broadcast_and_fusion
  28.7 0.1 copy_select_fusion
  28.8 3.1 %collective-permute-start.1 = (bf16[3,36,512]{2,1,0:T(8,128)(2,1)S(1)}, bf16[3,36,512]{2,1,0:T(8,128)(2,1)S(1)}, u32[]{:S(2)}, u32[]{:S(2)}) collective-permute-start(bf16[3,36,512]{2,1,0:T(8,128)(2,1)S(1)} %get-tuple-element.29), channel_id=1, source_target_pairs={{0,64},{64,128},{128,192},{192,256},{256,320},{320,384},{384,448},... | collective-permute-start | bytes 331784 | tf_op jit(solution)/shard_map/ppermute | solution.py:35
  31.9 1.3 %collective-permute-start.2 = (bf16[3,36,512]{2,1,0:T(8,128)(2,1)S(1)}, bf16[3,36,512]{2,1,0:T(8,128)(2,1)S(1)}, u32[]{:S(2)}, u32[]{:S(2)}) collective-permute-start(bf16[3,36,512]{2,1,0:T(8,128)(2,1)S(1)} %get-tuple-element.30), channel_id=1, source_target_pairs={{64,0},{128,64},{192,128},{256,192},{320,256},{384,320},{448,384},... | collective-permute-start | bytes 331784 | tf_op jit(solution)/shard_map/ppermute | solution.py:35
  33.2 0.1 broadcast_select_fusion.bias_ref
  33.4 1.0 collective-permute-done.1
  34.3 3.8 %collective-permute-done.2 = bf16[3,36,512]{2,1,0:T(8,128)(2,1)S(1)} collective-permute-done((bf16[3,36,512]{2,1,0:T(8,128)(2,1)S(1)}, bf16[3,36,512]{2,1,0:T(8,128)(2,1)S(1)}, u32[]{:S(2)}, u32[]{:S(2)}) %collective-permute-start.2) | collective-permute-done | bytes 110624 | tf_op jit(solution)/shard_map/ppermute | solution.py:35
  38.1 0.1 pad_maximum_fusion.1
  38.2 2.6 %all-to-all-done = bf16[16,80,128]{2,1,0:T(8,128)(2,1)S(1)} async-done(((bf16[16,80,128]{2,1,0:T(8,128)(2,1)}), bf16[16,80,128]{2,1,0:T(8,128)(2,1)S(1)}, u32[]{:S(2)}, u32[]{:S(2)}) %all-to-all-start) | async-done | bytes 327712 | tf_op jit(solution)/shard_map/all_to_all | solution.py:40
  40.8 1.2 broadcast_in_dim.58
  42.1 4.2 %all-to-all-start.1 = ((bf16[4,16,80,128]{3,2,1,0:T(8,128)(2,1)}), bf16[4,16,80,128]{3,2,1,0:T(8,128)(2,1)S(1)}, u32[]{:S(2)}, u32[]{:S(2)}) async-start(bf16[4,16,80,128]{3,2,1,0:T(8,128)(2,1)} %broadcast_in_dim.58), calls=%async_computation.1 | async-start | bytes 2621440 | tf_op jit(solution)/shard_map/all_to_all | solution.py:80
  46.3 8.7 %collective-permute-start.3 = (bf16[18,6,512]{2,1,0:T(8,128)(2,1)S(1)}, bf16[18,6,512]{2,1,0:T(8,128)(2,1)S(1)}, u32[]{:S(2)}, u32[]{:S(2)}) collective-permute-start(bf16[18,6,512]{2,1,0:T(8,128)(2,1)S(1)} %get-tuple-element.27), channel_id=1, source_target_pairs={{0,1},{1,2},{2,3},{3,4},{4,5},{5,6},{6,7},{7,8},{8,9},{9,10},{10,1... | collective-permute-start | bytes 331784 | tf_op jit(solution)/shard_map/ppermute | solution.py:35
  55.0 1.9 %collective-permute-start.4 = (bf16[18,6,512]{2,1,0:T(8,128)(2,1)S(1)}, bf16[18,6,512]{2,1,0:T(8,128)(2,1)S(1)}, u32[]{:S(2)}, u32[]{:S(2)}) collective-permute-start(bf16[18,6,512]{2,1,0:T(8,128)(2,1)S(1)} %get-tuple-element.28), channel_id=1, source_target_pairs={{0,63},{1,0},{2,1},{3,2},{4,3},{5,4},{6,5},{7,6},{8,7},{9,8},{10,9... | collective-permute-start | bytes 331784 | tf_op jit(solution)/shard_map/ppermute | solution.py:35
  57.0 0.2 collective-permute-done.3
  57.1 4.7 %collective-permute-done.4 = bf16[18,6,512]{2,1,0:T(8,128)(2,1)S(1)} collective-permute-done((bf16[18,6,512]{2,1,0:T(8,128)(2,1)S(1)}, bf16[18,6,512]{2,1,0:T(8,128)(2,1)S(1)}, u32[]{:S(2)}, u32[]{:S(2)}) %collective-permute-start.4) | collective-permute-done | bytes 110624 | tf_op jit(solution)/shard_map/ppermute | solution.py:35
  61.8 1.4 %pad_maximum_fusion.tall_in = bf16[18,48,512]{2,1,0:T(8,128)(2,1)} fusion(bf16[18,6,512]{2,1,0:T(8,128)(2,1)S(1)} %collective-permute-done.4, bf16[18,36,512]{2,1,0:T(8,128)(2,1)S(1)} %pad_maximum_fusion.1, bf16[18,6,512]{2,1,0:T(8,128)(2,1)S(1)} %collective-permute-done.3), kind=kLoop, calls=%fused_computation.9 | loop fusion | flops 2654208 | bytes 1769472 | tf_op jit(solution)/shard_map/concatenate | solution.py:470
  63.2 0.1 slice.35
  63.2 2.3 %broadcast_in_dim.59 = bf16[4,4,16,48,128]{4,3,2,1,0:T(8,128)(2,1)} broadcast(bf16[4,16,48,128]{3,2,1,0:T(8,128)(2,1)S(1)} %slice.35), dimensions={1,2,3,4} | broadcast | bytes 3932160 | tf_op jit(solution)/shard_map/broadcast_in_dim | solution.py:51
  65.5 4.7 %all-to-all-start.2 = ((bf16[4,4,16,48,128]{4,3,2,1,0:T(8,128)(2,1)}), bf16[4,4,16,48,128]{4,3,2,1,0:T(8,128)(2,1)}, u32[]{:S(2)}, u32[]{:S(2)}) async-start(bf16[4,4,16,48,128]{4,3,2,1,0:T(8,128)(2,1)} %broadcast_in_dim.59), calls=%async_computation.2 | async-start | bytes 6291456 | tf_op jit(solution)/shard_map/all_to_all | solution.py:80
  70.2 0.0 copy-start.12
  70.2 0.2 fan.1
  70.4 1.4 %copy-done.1 = bf16[4,4,16,32,128]{4,3,2,1,0:T(8,128)(2,1)} copy-done((bf16[4,4,16,32,128]{4,3,2,1,0:T(8,128)(2,1)}, bf16[4,4,16,32,128]{4,3,2,1,0:T(8,128)(2,1)S(1)}, u32[]{:S(2)}) %copy-start.1) | copy-done | bytes 2097176
  71.8 19.7 %all-to-all-done.2 = bf16[4,4,16,48,128]{4,3,2,1,0:T(8,128)(2,1)} async-done(((bf16[4,4,16,48,128]{4,3,2,1,0:T(8,128)(2,1)}), bf16[4,4,16,48,128]{4,3,2,1,0:T(8,128)(2,1)}, u32[]{:S(2)}, u32[]{:S(2)}) %all-to-all-start.2) | async-done | bytes 3145760 | tf_op jit(solution)/shard_map/all_to_all | solution.py:80
  91.5 3.8 %collective-permute-start.5 = (bf16[16,16,48,128]{3,2,1,0:T(8,128)(2,1)}, bf16[16,16,48,128]{3,2,1,0:T(8,128)(2,1)}, u32[]{:S(2)}, u32[]{:S(2)}) collective-permute-start(bf16[16,16,48,128]{3,2,1,0:T(8,128)(2,1)} %bitcast.8.mine_ref), channel_id=1, source_target_pairs={{0,1},{1,0},{2,3},{3,2},{4,5},{5,4},{6,7},{7,6},{8,9},{9,8},{10,11... | collective-permute-start | bytes 9437192 | tf_op jit(solution)/shard_map/ppermute | solution.py:35
  95.3 0.0 copy-start.4
  95.3 0.0 copy-start.5
  95.3 4.0 %all-to-all-start.3 = ((bf16[4,4,16,32,128]{4,3,2,1,0:T(8,128)(2,1)}), bf16[4,4,16,32,128]{4,3,2,1,0:T(8,128)(2,1)S(1)}, u32[]{:S(2)}, u32[]{:S(2)}) async-start(bf16[4,4,16,32,128]{4,3,2,1,0:T(8,128)(2,1)} %copy-done.1), calls=%async_computation.3 | async-start | bytes 4194304 | tf_op jit(solution)/shard_map/all_to_all | solution.py:80
  99.4 1.6 %collective-permute-done.5.other_ref = bf16[16,16,48,128]{3,2,1,0:T(8,128)(2,1)} collective-permute-done((bf16[16,16,48,128]{3,2,1,0:T(8,128)(2,1)}, bf16[16,16,48,128]{3,2,1,0:T(8,128)(2,1)}, u32[]{:S(2)}, u32[]{:S(2)}) %collective-permute-start.5) | collective-permute-done | bytes 3145760 | tf_op jit(solution)/shard_map/ppermute | solution.py:35
  100.9 12.4 %attention.1.first_ref = bf16[448,512]{1,0:T(8,128)(2,1)S(1)} custom-call(s32[1]{0:T(128)} %bitcast.core_ref, f32[8]{0:T(128)S(1)} %minimum_exponential_fusion.scale_ref, bf16[18,48,512]{2,1,0:T(8,128)(2,1)} %pad_maximum_fusion.tall_in, f32[3,8,96,128]{3,2,1,0:T(8,128)S(1)} %broadcast_select_fusion.bias_ref, bf16[384,288]{1,0:T(8,128)(2,1)} %constant.69.clone.arrange_in, ...), custom_call_target="tpu_custom_call" | custom-call | flops 20000000000 | bytes 20000000 | tf_op jit(solution)/shard_map/attention/pallas_call | solution.py:489
  113.4 0.8 copy-done.8
  114.2 0.8 all-to-all-done.3
  115.0 2.6 %collective-permute-start.6 = (bf16[16,16,32,128]{3,2,1,0:T(8,128)(2,1)S(1)}, bf16[16,16,32,128]{3,2,1,0:T(8,128)(2,1)S(1)}, u32[]{:S(2)}, u32[]{:S(2)}) collective-permute-start(bf16[16,16,32,128]{3,2,1,0:T(8,128)(2,1)S(1)} %bitcast.18), channel_id=1, source_target_pairs={{0,1},{1,0},{2,3},{3,2},{4,5},{5,4},{6,7},{7,6},{8,9},{9,8},{10,11... | collective-permute-start | bytes 6291464 | tf_op jit(solution)/shard_map/ppermute | solution.py:35
  117.6 0.0 copy-start.2
  117.6 0.0 copy-start.3
  117.6 5.3 %feedforward.1.second_ref = bf16[448,512]{1,0:T(8,128)(2,1)S(1)} custom-call(s32[1]{0:T(128)} %bitcast.core_ref, bf16[448,512]{1,0:T(8,128)(2,1)} %copy-done.8, f32[1,512]{1,0:T(1,128)S(1)} %bitcast.24, f32[1,512]{1,0:T(1,128)S(1)} %bitcast.25, bf16[16,16,48,128]{3,2,1,0:T(8,128)(2,1)} %bitcast.8.mine_ref, ...), custom_call_target="tpu_custom_call" | custom-call | flops 6000000000 | bytes 20000000 | tf_op jit(solution)/shard_map/feedforward/pallas_call | solution.py:526
  123.0 3.3 %merging.1 = bf16[6,18,1024]{2,1,0:T(8,128)(2,1)} custom-call(s32[1]{0:T(128)} %bitcast.core_ref, bf16[448,512]{1,0:T(8,128)(2,1)S(1)} %feedforward.1.second_ref, f32[1,1024]{1,0:T(1,128)S(1)} %bitcast.20, f32[1,1024]{1,0:T(1,128)S(1)} %bitcast.21, bf16[16,16,32,128]{3,2,1,0:T(8,128)(2,1)S(1)} %bitcast.19, ...), custom_call_target="tpu_custom_call" | custom-call | flops 1000000000 | bytes 8000000 | tf_op jit(solution)/shard_map/merging/pallas_call | solution.py:551
  (30 shorter events, 0.2 us)
Async XLA Ops:
  0.0 13.9 %copy-start = (bf16[32,1024]{1,0:T(8,128)(2,1)S(1)}, bf16[32,1024]{1,0:T(8,128)(2,1)}, u32[]{:S(2)}) copy-start(bf16[32,1024]{1,0:T(8,128)(2,1)} %param.28) | copy-start | bytes 196612
  0.0 24.5 %copy-start.13 = (s32[12288]{0:T(1024)S(1)}, s32[12288]{0:T(1024)}, u32[]{:S(2)}) copy-start(s32[12288]{0:T(1024)} %constant.66.clone) | copy-start | bytes 147460
  2.2 11.7 %collective-permute-start = (bf16[8,4096]{1,0:T(8,128)(2,1)S(1)}, bf16[8,4096]{1,0:T(8,128)(2,1)S(1)}, u32[]{:S(2)}, u32[]{:S(2)}) collective-permute-start(bf16[8,4096]{1,0:T(8,128)(2,1)S(1)} %constant_dynamic-update-slice_fusion), channel_id=1, source_target_pairs={{0,1},{1,0},{2,3},{3,2},{4,5},{5,4},{6,7},{7,6},{8,9},{9,8},{10,11... | collective-permute-start | bytes 196616 | tf_op jit(solution)/shard_map/ppermute | solution.py:35
  14.8 13.7 %copy-start.10 = (pred[96,128]{1,0:T(32,128)(4,1)S(1)}, pred[96,128]{1,0:T(32,128)(4,1)}, u32[]{:S(2)}) copy-start(pred[96,128]{1,0:T(32,128)(4,1)} %constant.68.clone) | copy-start | bytes 36868
  14.8 13.8 %copy-start.11 = (pred[128]{0:T(512)(128)(4,1)S(1)}, pred[128]{0:T(512)(128)(4,1)}, u32[]{:S(2)}) copy-start(pred[128]{0:T(512)(128)(4,1)} %constant.67.clone) | copy-start | bytes 388
  14.8 26.0 %all-to-all-start = ((bf16[16,80,128]{2,1,0:T(8,128)(2,1)}), bf16[16,80,128]{2,1,0:T(8,128)(2,1)S(1)}, u32[]{:S(2)}, u32[]{:S(2)}) async-start(bf16[16,80,128]{2,1,0:T(8,128)(2,1)} %broadcast_in_dim.34), calls=%async_computation | async-start | bytes 655360 | tf_op jit(solution)/shard_map/all_to_all | solution.py:40
  24.5 4.3 %copy-start.9 = (bf16[12,36,512]{2,1,0:T(8,128)(2,1)S(1)}, bf16[12,36,512]{2,1,0:T(8,128)(2,1)}, u32[]{:S(2)}) copy-start(bf16[12,36,512]{2,1,0:T(8,128)(2,1)} %param.23) | copy-start | bytes 1327108
  28.8 5.5 %collective-permute-start.1 = (bf16[3,36,512]{2,1,0:T(8,128)(2,1)S(1)}, bf16[3,36,512]{2,1,0:T(8,128)(2,1)S(1)}, u32[]{:S(2)}, u32[]{:S(2)}) collective-permute-start(bf16[3,36,512]{2,1,0:T(8,128)(2,1)S(1)} %get-tuple-element.29), channel_id=1, source_target_pairs={{0,64},{64,128},{128,192},{192,256},{256,320},{320,384},{384,448},... | collective-permute-start | bytes 331784 | tf_op jit(solution)/shard_map/ppermute | solution.py:35
  31.9 6.2 %collective-permute-start.2 = (bf16[3,36,512]{2,1,0:T(8,128)(2,1)S(1)}, bf16[3,36,512]{2,1,0:T(8,128)(2,1)S(1)}, u32[]{:S(2)}, u32[]{:S(2)}) collective-permute-start(bf16[3,36,512]{2,1,0:T(8,128)(2,1)S(1)} %get-tuple-element.30), channel_id=1, source_target_pairs={{64,0},{128,64},{192,128},{256,192},{320,256},{384,320},{448,384},... | collective-permute-start | bytes 331784 | tf_op jit(solution)/shard_map/ppermute | solution.py:35
  42.1 21.1 %all-to-all-start.1 = ((bf16[4,16,80,128]{3,2,1,0:T(8,128)(2,1)}), bf16[4,16,80,128]{3,2,1,0:T(8,128)(2,1)S(1)}, u32[]{:S(2)}, u32[]{:S(2)}) async-start(bf16[4,16,80,128]{3,2,1,0:T(8,128)(2,1)} %broadcast_in_dim.58), calls=%async_computation.1 | async-start | bytes 2621440 | tf_op jit(solution)/shard_map/all_to_all | solution.py:80
  46.3 10.8 %collective-permute-start.3 = (bf16[18,6,512]{2,1,0:T(8,128)(2,1)S(1)}, bf16[18,6,512]{2,1,0:T(8,128)(2,1)S(1)}, u32[]{:S(2)}, u32[]{:S(2)}) collective-permute-start(bf16[18,6,512]{2,1,0:T(8,128)(2,1)S(1)} %get-tuple-element.27), channel_id=1, source_target_pairs={{0,1},{1,2},{2,3},{3,4},{4,5},{5,6},{6,7},{7,8},{8,9},{9,10},{10,1... | collective-permute-start | bytes 331784 | tf_op jit(solution)/shard_map/ppermute | solution.py:35
  55.0 6.8 %collective-permute-start.4 = (bf16[18,6,512]{2,1,0:T(8,128)(2,1)S(1)}, bf16[18,6,512]{2,1,0:T(8,128)(2,1)S(1)}, u32[]{:S(2)}, u32[]{:S(2)}) collective-permute-start(bf16[18,6,512]{2,1,0:T(8,128)(2,1)S(1)} %get-tuple-element.28), channel_id=1, source_target_pairs={{0,63},{1,0},{2,1},{3,2},{4,3},{5,4},{6,5},{7,6},{8,7},{9,8},{10,9... | collective-permute-start | bytes 331784 | tf_op jit(solution)/shard_map/ppermute | solution.py:35
  65.5 26.0 %all-to-all-start.2 = ((bf16[4,4,16,48,128]{4,3,2,1,0:T(8,128)(2,1)}), bf16[4,4,16,48,128]{4,3,2,1,0:T(8,128)(2,1)}, u32[]{:S(2)}, u32[]{:S(2)}) async-start(bf16[4,4,16,48,128]{4,3,2,1,0:T(8,128)(2,1)} %broadcast_in_dim.59), calls=%async_computation.2 | async-start | bytes 6291456 | tf_op jit(solution)/shard_map/all_to_all | solution.py:80
  70.2 25.1 %copy-start.12 = (f32[8]{0:T(128)S(1)}, f32[8]{0:T(128)}, u32[]{:S(2)}) copy-start(f32[8]{0:T(128)} %param.29) | copy-start | bytes 100
  70.4 1.4 %copy-start.1 = (bf16[4,4,16,32,128]{4,3,2,1,0:T(8,128)(2,1)}, bf16[4,4,16,32,128]{4,3,2,1,0:T(8,128)(2,1)S(1)}, u32[]{:S(2)}) copy-start(bf16[4,4,16,32,128]{4,3,2,1,0:T(8,128)(2,1)S(1)} %fan.1) | copy-start | bytes 6291460
  91.5 9.4 %collective-permute-start.5 = (bf16[16,16,48,128]{3,2,1,0:T(8,128)(2,1)}, bf16[16,16,48,128]{3,2,1,0:T(8,128)(2,1)}, u32[]{:S(2)}, u32[]{:S(2)}) collective-permute-start(bf16[16,16,48,128]{3,2,1,0:T(8,128)(2,1)} %bitcast.8.mine_ref), channel_id=1, source_target_pairs={{0,1},{1,0},{2,3},{3,2},{4,5},{5,4},{6,7},{7,6},{8,9},{9,8},{10,11... | collective-permute-start | bytes 9437192 | tf_op jit(solution)/shard_map/ppermute | solution.py:35
  95.3 5.6 %copy-start.4 = (f32[512]{0:T(512)S(1)}, f32[512]{0:T(512)}, u32[]{:S(2)}) copy-start(f32[512]{0:T(512)} %param.33) | copy-start | bytes 6148
  95.3 5.6 %copy-start.5 = (f32[512]{0:T(512)S(1)}, f32[512]{0:T(512)}, u32[]{:S(2)}) copy-start(f32[512]{0:T(512)} %param.34) | copy-start | bytes 6148
  95.3 19.7 %all-to-all-start.3 = ((bf16[4,4,16,32,128]{4,3,2,1,0:T(8,128)(2,1)}), bf16[4,4,16,32,128]{4,3,2,1,0:T(8,128)(2,1)S(1)}, u32[]{:S(2)}, u32[]{:S(2)}) async-start(bf16[4,4,16,32,128]{4,3,2,1,0:T(8,128)(2,1)} %copy-done.1), calls=%async_computation.3 | async-start | bytes 4194304 | tf_op jit(solution)/shard_map/all_to_all | solution.py:80
  100.9 16.7 %copy-start.6 = (f32[512]{0:T(512)S(1)}, f32[512]{0:T(512)}, u32[]{:S(2)}) copy-start(f32[512]{0:T(512)} %param.35) | copy-start | bytes 6148
  100.9 16.7 %copy-start.7 = (f32[512]{0:T(512)S(1)}, f32[512]{0:T(512)}, u32[]{:S(2)}) copy-start(f32[512]{0:T(512)} %param.36) | copy-start | bytes 6148
  113.4 0.8 copy-start.8
  115.0 7.9 %collective-permute-start.6 = (bf16[16,16,32,128]{3,2,1,0:T(8,128)(2,1)S(1)}, bf16[16,16,32,128]{3,2,1,0:T(8,128)(2,1)S(1)}, u32[]{:S(2)}, u32[]{:S(2)}) collective-permute-start(bf16[16,16,32,128]{3,2,1,0:T(8,128)(2,1)S(1)} %bitcast.18), channel_id=1, source_target_pairs={{0,1},{1,0},{2,3},{3,2},{4,5},{5,4},{6,7},{7,6},{8,9},{9,8},{10,11... | collective-permute-start | bytes 6291464 | tf_op jit(solution)/shard_map/ppermute | solution.py:35
  117.6 5.3 %copy-start.2 = (f32[1024]{0:T(1024)S(1)}, f32[1024]{0:T(1024)}, u32[]{:S(2)}) copy-start(f32[1024]{0:T(1024)} %param.37) | copy-start | bytes 12292
  117.6 5.3 %copy-start.3 = (f32[1024]{0:T(1024)S(1)}, f32[1024]{0:T(1024)}, u32[]{:S(2)}) copy-start(f32[1024]{0:T(1024)} %param.38) | copy-start | bytes 12292
